TPU v7x, 256 devices: a whole 4x4x8 slice. The times are simulated.
256 devices in a mesh: dp: 32 (over x, z), seq: 8 (over y, core).
Axes of the slice: x: 4, y: 4, z: 8, core: 2. Of those that a mesh axis runs over, the one named last changes fastest.
Arguments:
- pixels: bfloat16 [32768, 1176], P(('dp', 'seq')), may hold values from -6 to 6
- patch_weight: bfloat16 [1176, 1280], replicated, may hold values from -0.1875 to 0.1875
- ln_gain: float32 [1280], replicated, may hold values from 0.1 to 1.9
- ln_bias: float32 [1280], replicated, may hold values from -1.5 to 1.5
- qkv_weight: bfloat16 [1280, 3840], P('dp'), may hold values from -4 to 4
- qkv_bias: float32 [3840], replicated, may hold values from -2.5 to 2.5
- out_weight: bfloat16 [1280, 1280], P('dp'), may hold values from -0.15625 to 0.15625
- out_bias: float32 [1280], replicated, may hold values from -1.5 to 1.5
- offsets: int32 [32, 3], P('dp'), may hold values from 0 to 854, as said below
- widths: int32 [32, 3], P('dp'), may hold values from 16 to 64
Outputs:
- encoded: bfloat16 [32768, 1280], P(('dp', 'seq'))
Inputs may be any that keep to these rules, and one draw needn't show every extreme that they name: In every group the first offset is 0 and offsets rise; every image holds 170 or more tokens and the last image ends at position 1024; in some group the last image holds exactly 170 tokens.
All inputs are finite; a program needn't handle non-finite values.
Results may differ from a plain program's by a relative error of at most 0.012.
Values may be sent and summed in bfloat16 or wider, within the bound.
No kernel may reach another device: no remote copies, remote signals or barrier semaphores. Data moves between devices by JAX's collectives and lax.ppermute only.
A program may use at most 64 MiB of HBM per device.

v0:
```python
import jax
import jax.numpy as jnp
from jax import lax
from jax.sharding import PartitionSpec as P

HEADS = 16
HDIM = 80


def image_lookup(positions, starts):
    return jnp.sum((positions[:, None] >= starts[None, :]).astype(jnp.int32), axis=1) - 1


def rotation_tables(positions, starts, image_widths, head_size):
    image_index = image_lookup(positions, starts)
    onehot = (image_index[:, None] == jnp.arange(starts.shape[0], dtype=jnp.int32)[None, :]).astype(
        jnp.int32
    )
    first_position = jnp.sum(onehot * starts[None, :], axis=1)
    across = jnp.sum(onehot * image_widths[None, :], axis=1)
    within = positions - first_position
    row_index = within // across
    column_index = within - row_index * across
    quarter = head_size // 4
    inverse = 1.0 / 10000.0 ** (jnp.arange(quarter, dtype=jnp.float32) * 2.0 / (head_size // 2))
    angles = jnp.concatenate(
        [
            row_index.astype(jnp.float32)[:, None] * inverse[None, :],
            column_index.astype(jnp.float32)[:, None] * inverse[None, :],
        ],
        axis=1,
    )
    angles = jnp.concatenate([angles, angles], axis=1)
    return (jnp.cos(angles), jnp.sin(angles), image_index)


def rotate_heads(values, cosine, sine_table, head_size):
    half_size = head_size // 2
    turned = jnp.concatenate([-values[..., half_size:], values[..., :half_size]], axis=-1)
    return values * cosine[:, None, :] + turned * sine_table[:, None, :]


def layer_norm(embedded, ln_gain, ln_bias):
    values = embedded.astype(jnp.float32)
    center = values - jnp.mean(values, axis=-1, keepdims=True)
    variance = jnp.mean(center * center, axis=-1, keepdims=True)
    return (center * lax.rsqrt(variance + 1e-06) * ln_gain + ln_bias).astype(jnp.bfloat16)


def block_length(count):
    length = min(count, 512)
    while count % length:
        length -= 1
    return length


def attend_block(state, queries3, key_block, value_block, query_image, key_image, score_scale):
    running_max, running_total, accum = state
    count = key_block.shape[0]
    scores = (
        jnp.einsum(
            "qhd,khd->hqk",
            queries3,
            key_block.reshape(count, HEADS, HDIM),
            preferred_element_type=jnp.float32,
        )
        * score_scale
    )
    allowed = (query_image[:, None] == key_image[None, :])[None]
    scores = jnp.where(allowed, scores, -1e30)
    new_max = jnp.maximum(running_max, jnp.max(scores, axis=-1))
    weights = jnp.where(allowed, jnp.exp(scores - new_max[..., None]), 0.0)
    factor = jnp.exp(running_max - new_max)
    running_total = running_total * factor + jnp.sum(weights, axis=-1)
    part_sum = jnp.einsum(
        "hqk,khd->qhd",
        weights.astype(jnp.bfloat16),
        value_block.reshape(count, HEADS, HDIM),
        preferred_element_type=jnp.float32,
    )
    accum = accum * factor.T[:, :, None] + part_sum
    return (new_max, running_total, accum)


def per_device(
    pixels,
    patch_weight,
    ln_gain,
    ln_bias,
    qkv_weight,
    qkv_bias,
    out_weight,
    out_bias,
    offsets,
    widths,
):
    local_pixels = lax.all_to_all(pixels, "dp", split_axis=0, concat_axis=0, tiled=True)
    tok_rows = local_pixels.shape[0]
    dmodel = patch_weight.shape[1]
    score_scale = HDIM ** (-0.5)
    embedded = jnp.dot(local_pixels, patch_weight, preferred_element_type=jnp.float32).astype(
        jnp.bfloat16
    )
    normed = layer_norm(embedded, ln_gain, ln_bias)
    columns = normed
    projected = (
        jnp.dot(
            columns,
            lax.all_gather(qkv_weight, "dp", axis=0, tiled=True),
            preferred_element_type=jnp.float32,
        )
        + qkv_bias
    )
    starts = offsets[0]
    image_widths = widths[0]
    positions = lax.axis_index("seq") * tok_rows + jnp.arange(tok_rows, dtype=jnp.int32)
    cosine, sine_table, query_image = rotation_tables(positions, starts, image_widths, HDIM)
    queries = (
        rotate_heads(projected[:, :dmodel].reshape(tok_rows, HEADS, HDIM), cosine, sine_table, HDIM)
        .reshape(tok_rows, dmodel)
        .astype(jnp.bfloat16)
    )
    key_rows = (
        rotate_heads(
            projected[:, dmodel : 2 * dmodel].reshape(tok_rows, HEADS, HDIM),
            cosine,
            sine_table,
            HDIM,
        )
        .reshape(tok_rows, dmodel)
        .astype(jnp.bfloat16)
    )
    values = projected[:, 2 * dmodel :].astype(jnp.bfloat16)
    queries3 = queries.reshape(tok_rows, HEADS, HDIM)
    initial = (
        jnp.full((HEADS, tok_rows), -1e30, jnp.float32),
        jnp.zeros((HEADS, tok_rows), jnp.float32),
        jnp.zeros((tok_rows, HEADS, HDIM), jnp.float32),
    )
    piece_keys = lax.all_gather(key_rows, "seq", axis=0, tiled=True)
    piece_values = lax.all_gather(values, "seq", axis=0, tiled=True)
    count = piece_keys.shape[0]
    length = block_length(count)

    def one_block(block_index, inner):
        first_row = block_index * length
        key_block = lax.dynamic_slice_in_dim(piece_keys, first_row, length, 0)
        value_block = lax.dynamic_slice_in_dim(piece_values, first_row, length, 0)
        key_image = image_lookup(first_row + jnp.arange(length, dtype=jnp.int32), starts)
        return attend_block(
            inner, queries3, key_block, value_block, query_image, key_image, score_scale
        )

    final_state = lax.fori_loop(0, count // length, one_block, initial)
    attended = (
        (final_state[2] / final_state[1].T[:, :, None])
        .reshape(tok_rows, dmodel)
        .astype(jnp.bfloat16)
    )
    columns = attended
    mixed = jnp.dot(
        columns,
        lax.all_gather(out_weight, "dp", axis=0, tiled=True),
        preferred_element_type=jnp.float32,
    )
    return (embedded.astype(jnp.float32) + mixed + out_bias).astype(jnp.bfloat16)


def solution(mesh):
    in_specs = (
        P(("dp", "seq"), None),
        P(),
        P(),
        P(),
        P("dp", None),
        P(),
        P("dp", None),
        P(),
        P("dp", None),
        P("dp", None),
    )
    out_specs = P(("dp", "seq"), None)
    return jax.shard_map(
        per_device, mesh=mesh, in_specs=in_specs, out_specs=out_specs, check_vma=False
    )
```

profile of v0, /device:TPU:1, one launch (start us, length us, event | category | flops | bytes accessed | tf_op | source)
XLA Modules:
  0.0 287.5 jit_solution(15201041775588603741)
XLA Ops:
  6.5 0.0 copy-start
  6.5 0.0 all-gather.5.cloned.1.call-start
  6.5 0.7 all-gather.5.cloned.1.call-update
  7.3 1.3 copy.27
  8.6 0.8 all_to_all.8
  9.4 12.0 %all-to-all-start = ((bf16[32,4,1176]{2,1,0:T(4,128)(2,1)}), bf16[32,4,1176]{2,1,0:T(4,128)(2,1)}, u32[]{:S(2)}, u32[]{:S(2)}) async-start(bf16[32,4,1176]{2,1,0:T(4,128)(2,1)} %all_to_all.8), calls=%async_computation | async-start | bytes 655360 | tf_op jit(solution)/shard_map/all_to_all | solution.py:97
  21.4 0.0 all-gather.7.cloned.1.call-start
  21.4 0.7 convert_reduce_fusion.1
  22.2 0.8 select_reduce_fusion.1
  22.9 0.1 fusion.26
  23.1 0.1 broadcast_multiply_fusion.1
  23.2 0.2 fusion.25
  23.3 0.9 mul.198
  24.2 2.2 copy.28
  26.4 5.1 %all-to-all-done = bf16[32,4,1176]{2,1,0:T(4,128)(2,1)} async-done(((bf16[32,4,1176]{2,1,0:T(4,128)(2,1)}), bf16[32,4,1176]{2,1,0:T(4,128)(2,1)}, u32[]{:S(2)}, u32[]{:S(2)}) %all-to-all-start) | async-done | bytes 301088 | tf_op jit(solution)/shard_map/all_to_all | solution.py:97
  31.6 1.1 all_to_all.10
  32.7 0.0 copy-done
  32.7 0.7 fusion.28
  33.4 0.0 copy-start.2
  33.4 0.8 copy-done.2
  34.3 0.2 multiply_reduce_fusion
  34.5 84.3 %all-gather.5.cloned.1.call-done = bf16[1280,3840]{1,0:T(8,128)(2,1)} async-done(((bf16[40,3840]{1,0:T(8,128)(2,1)}), bf16[1280,3840]{1,0:T(8,128)(2,1)}) %all-gather.5.cloned.1.call-update) | async-done | bytes 9830416 | tf_op jit(solution)/shard_map/all_gather | solution.py:109
  118.8 0.0 copy-done.4
  118.8 0.0 copy-done.7
  118.8 5.5 %convolution_add_fusion = f32[128,3840]{1,0:T(8,128)S(1)} fusion(bf16[1280,3840]{1,0:T(8,128)(2,1)} %all-gather.5.cloned.1.call-done, f32[3840]{0:T(1024)S(1)} %copy-done.7, f32[128,1280]{1,0:T(8,128)} %copy-done.2, f32[1280]{0:T(1024)S(1)} %copy-done.4, f32[1280]{0:T(1024)S(1)} %copy-done.5, f32[128]{0:T(128)S(1)} %add_rsqrt_fusion, ...), kind=kOutput, calls=%fused_computation.24 | convolution fusion | flops 1259601920 | bytes 12478464 | tf_op jit(solution)/shard_map/dot_general | solution.py:107
  124.3 1.3 copy-done.3
  125.6 1.1 fusion.27
  126.8 2.1 copy.29
  128.9 2.2 copy.32
  131.1 1.4 slice_negate_fusion
  132.4 1.2 maximum_multiply_fusion.1
  133.6 2.2 copy.30
  135.8 2.2 copy.33
  137.9 2.9 %add_convert_fusion = (bf16[128,1280]{1,0:T(8,128)(2,1)}, bf16[128,1280]{1,0:T(8,128)(2,1)}) fusion(f32[128,1280]{1,0:T(8,128)} %copy.33, f32[128,1280]{1,0:T(8,128)} %copy.28, f32[128,3840]{1,0:T(8,128)} %copy-done.3, f32[128,1280]{1,0:T(8,128)} %copy.30), kind=kLoop, calls=%fused_computation.34 | loop fusion | flops 983040 | bytes 3932160 | tf_op jit(solution)/shard_map/convert_element_type | solution.py:121
  140.8 0.0 all-gather.7.cloned.1.call-update
  140.8 0.0 all-gather.9.cloned.1.call-start
  140.9 1.8 slice.41
  142.7 0.0 all-gather.9.cloned.1.call-update
  142.7 0.0 all-gather.11.cloned.1.call-start
  142.8 0.5 all-gather.11.cloned.1.call-update
  143.3 1.2 copy.34
  144.5 23.1 %all-gather.7.cloned.1.call-done = bf16[1024,1280]{1,0:T(8,128)(2,1)} async-done(((bf16[128,1280]{1,0:T(8,128)(2,1)}), bf16[1024,1280]{1,0:T(8,128)(2,1)}) %all-gather.7.cloned.1.call-update) | async-done | bytes 2621456 | tf_op jit(solution)/shard_map/all_gather | solution.py:140
  167.6 31.1 %all-gather.9.cloned.1.call-done = bf16[1024,1280]{1,0:T(8,128)(2,1)} async-done(((bf16[128,1280]{1,0:T(8,128)(2,1)}), bf16[1024,1280]{1,0:T(8,128)(2,1)}) %all-gather.9.cloned.1.call-update) | async-done | bytes 2621456 | tf_op jit(solution)/shard_map/all_gather | solution.py:141
  198.7 37.8 %while.20 = (s32[]{:T(128)}, f32[16,128]{1,0:T(8,128)S(1)}, f32[16,128]{1,0:T(8,128)S(1)}, f32[128,16,80]{0,2,1:T(8,128)}, s32[128]{0:T(128)S(1)}, /*index=5*/s3...) while((s32[]{:T(128)}, f32[16,128]{1,0:T(8,128)S(1)}, ...), condition=%wide.region_9.10_spmd.clone, body=%wide.region_5.9_spmd.clone.sunk | while | flops 349750272 | bytes 44511972 | solution.py:154
  198.7 3.5 %constant_dynamic-slice_fusion.3 = (bf16[512,1280]{1,0:T(8,128)(2,1)}, bf16[512,1280]{1,0:T(8,128)(2,1)}) fusion(bf16[1024,1280]{1,0:T(8,128)(2,1)} %get-tuple-element.432, s32[]{:T(128)S(6)} %select_n.85, bf16[1024,1280]{1,0:T(8,128)(2,1)} %get-tuple-element.430), kind=kLoop, calls=%fused_computation.19.clone.1 | loop fusion | bytes 5242884 | tf_op jit(solution)/shard_map/while/body/eval_jaxpr/dynamic_slice | solution.py:148
  202.2 2.4 copy.42
  204.6 0.1 convert_reduce_fusion.3
  204.7 0.1 broadcast_compare_fusion.2
  204.9 4.3 %fusion.50 = (f32[16,128]{1,0:T(8,128)S(1)}, f32[16,512,128]{2,1,0:T(8,128)}) fusion(pred[128,512]{0,1:T(8,128)(4,1)S(1)} %broadcast_compare_fusion.2, bf16[512,16,80]{0,2,1:T(8,128)(2,1)} %bitcast.64, bf16[128,16,80]{0,2,1:T(8,128)(2,1)S(1)} %get-tuple-element.431), kind=kOutput, calls=%fused_computation.2.clone.1 | convolution fusion | flops 170915840 | bytes 5906432 | tf_op jit(solution)/shard_map/while/body/eval_jaxpr/qhd,khd->hqk/dot_general | solution.py:61
  209.2 2.4 copy.43
  211.6 4.9 %fusion.54 = f32[128,16,80]{0,2,1:T(8,128)} fusion(bf16[512,16,80]{0,2,1:T(8,128)(2,1)} %bitcast.65, f32[16,512,128]{2,1,0:T(8,128)} %get-tuple-element.395, f32[16,128]{1,0:T(8,128)S(1)} %get-tuple-element.425, pred[128,512]{0,1:T(8,128)(4,1)S(1)} %broadcast_compare_fusion.2, f32[128,16,80]{0,2,1:T(8,128)} %get-tuple-element.414, ...), kind=kOutput, calls=%fused_computation.8.clone.1 | convolution fusion | flops 173506560 | bytes 6897665 | tf_op jit(solution)/shard_map/while/body/eval_jaxpr/hqk,khd->qhd/dot_general | solution.py:75
  216.5 1.0 fusion.52
  217.6 3.5 %constant_dynamic-slice_fusion.3 = (bf16[512,1280]{1,0:T(8,128)(2,1)}, bf16[512,1280]{1,0:T(8,128)(2,1)}) fusion(bf16[1024,1280]{1,0:T(8,128)(2,1)} %get-tuple-element.432, s32[]{:T(128)S(6)} %select_n.85, bf16[1024,1280]{1,0:T(8,128)(2,1)} %get-tuple-element.430), kind=kLoop, calls=%fused_computation.19.clone.1 | loop fusion | bytes 5242884 | tf_op jit(solution)/shard_map/while/body/eval_jaxpr/dynamic_slice | solution.py:148
  221.1 2.4 copy.42
  223.5 0.1 convert_reduce_fusion.3
  223.6 0.1 broadcast_compare_fusion.2
  223.7 4.3 %fusion.50 = (f32[16,128]{1,0:T(8,128)S(1)}, f32[16,512,128]{2,1,0:T(8,128)}) fusion(pred[128,512]{0,1:T(8,128)(4,1)S(1)} %broadcast_compare_fusion.2, bf16[512,16,80]{0,2,1:T(8,128)(2,1)} %bitcast.64, bf16[128,16,80]{0,2,1:T(8,128)(2,1)S(1)} %get-tuple-element.431), kind=kOutput, calls=%fused_computation.2.clone.1 | convolution fusion | flops 170915840 | bytes 5906432 | tf_op jit(solution)/shard_map/while/body/eval_jaxpr/qhd,khd->hqk/dot_general | solution.py:61
  228.0 2.4 copy.43
  230.5 5.0 %fusion.54 = f32[128,16,80]{0,2,1:T(8,128)} fusion(bf16[512,16,80]{0,2,1:T(8,128)(2,1)} %bitcast.65, f32[16,512,128]{2,1,0:T(8,128)} %get-tuple-element.395, f32[16,128]{1,0:T(8,128)S(1)} %get-tuple-element.425, pred[128,512]{0,1:T(8,128)(4,1)S(1)} %broadcast_compare_fusion.2, f32[128,16,80]{0,2,1:T(8,128)} %get-tuple-element.414, ...), kind=kOutput, calls=%fused_computation.8.clone.1 | convolution fusion | flops 173506560 | bytes 6897665 | tf_op jit(solution)/shard_map/while/body/eval_jaxpr/hqk,khd->qhd/dot_general | solution.py:75
  235.5 1.0 fusion.52
  236.5 1.1 divide_convert_fusion
  237.7 39.8 %all-gather.11.cloned.1.call-done = bf16[1280,1280]{1,0:T(8,128)(2,1)} async-done(((bf16[40,1280]{1,0:T(8,128)(2,1)}), bf16[1280,1280]{1,0:T(8,128)(2,1)}) %all-gather.11.cloned.1.call-update) | async-done | bytes 3276816 | tf_op jit(solution)/shard_map/all_gather | solution.py:163
  277.5 0.0 copy-done.8
  277.5 3.4 %fusion.18 = bf16[128,1280]{1,0:T(8,128)(2,1)} fusion(f32[128,1280]{1,0:T(8,128)} %copy-done.2, bf16[128,1280]{0,1:T(8,128)(2,1)S(1)} %bitcast.72, bf16[1280,1280]{1,0:T(8,128)(2,1)} %all-gather.11.cloned.1.call-done, f32[1280]{0:T(1024)S(1)} %copy-done.8), kind=kOutput, calls=%fused_computation.27 | convolution fusion | flops 419921920 | bytes 4592640 | tf_op jit(solution)/shard_map/dot_general | solution.py:161
  (31 shorter events, 0.1 us)
Async XLA Ops:
  6.5 26.2 %copy-start = (bf16[1176,1280]{1,0:T(8,128)(2,1)S(1)}, bf16[1176,1280]{1,0:T(8,128)(2,1)}, u32[]{:S(2)}) copy-start(bf16[1176,1280]{1,0:T(8,128)(2,1)} %param.13) | copy-start | bytes 9031684
  6.5 112.2 %all-gather.5.cloned.1.call-start = ((), (), s32[]{:S(2)}) async-start(), calls=%async_computation.1 | async-start | bytes 10137600 | tf_op jit(solution)/shard_map/all_gather | solution.py:109
  9.4 22.2 %all-to-all-start = ((bf16[32,4,1176]{2,1,0:T(4,128)(2,1)}), bf16[32,4,1176]{2,1,0:T(4,128)(2,1)}, u32[]{:S(2)}, u32[]{:S(2)}) async-start(bf16[32,4,1176]{2,1,0:T(4,128)(2,1)} %all_to_all.8), calls=%async_computation | async-start | bytes 655360 | tf_op jit(solution)/shard_map/all_to_all | solution.py:97
  21.4 146.2 %all-gather.7.cloned.1.call-start = ((), (), s32[]{:S(2)}) async-start(), calls=%async_computation.2 | async-start | bytes 2949120 | tf_op jit(solution)/shard_map/all_gather | solution.py:140
  24.2 94.6 %copy-start.4 = (f32[1280]{0:T(1024)S(1)}, f32[1280]{0:T(1024)}, u32[]{:S(2)}) copy-start(f32[1280]{0:T(1024)} %param.15) | copy-start | bytes 15364
  24.2 94.6 %copy-start.5 = (f32[1280]{0:T(1024)S(1)}, f32[1280]{0:T(1024)}, u32[]{:S(2)}) copy-start(f32[1280]{0:T(1024)} %param.14) | copy-start | bytes 15364
  24.2 94.6 %copy-start.7 = (f32[3840]{0:T(1024)S(1)}, f32[3840]{0:T(1024)}, u32[]{:S(2)}) copy-start(f32[3840]{0:T(1024)} %param.17) | copy-start | bytes 46084
  33.4 0.9 copy-start.2
  124.3 1.3 copy-start.3
  137.9 60.8 %copy-start.6 = (s32[1,3]{1,0:T(1,128)S(1)}, s32[1,3]{1,0:T(1,128)}, u32[]{:S(2)}) copy-start(s32[1,3]{1,0:T(1,128)} %param.20) | copy-start | bytes 40
  140.8 57.9 %all-gather.9.cloned.1.call-start = ((), (), s32[]{:S(2)}) async-start(), calls=%async_computation.3 | async-start | bytes 2949120 | tf_op jit(solution)/shard_map/all_gather | solution.py:141
  142.7 134.8 %all-gather.11.cloned.1.call-start = ((), (), s32[]{:S(2)}) async-start(), calls=%async_computation.4 | async-start | bytes 3379200 | tf_op jit(solution)/shard_map/all_gather | solution.py:163
  198.7 78.8 %copy-start.8 = (f32[1280]{0:T(1024)S(1)}, f32[1280]{0:T(1024)}, u32[]{:S(2)}) copy-start(f32[1280]{0:T(1024)} %param.19) | copy-start | bytes 15364
  211.6 4.9 %copy-start.1 = (f32[16,512,128]{2,1,0:T(8,128)S(1)}, f32[16,512,128]{2,1,0:T(8,128)}, u32[]{:S(2)}) copy-start(f32[16,512,128]{2,1,0:T(8,128)} %get-tuple-element.395) | copy-start | bytes 12582916 | tf_op jit(solution)/shard_map/while
  230.5 5.0 %copy-start.1 = (f32[16,512,128]{2,1,0:T(8,128)S(1)}, f32[16,512,128]{2,1,0:T(8,128)}, u32[]{:S(2)}) copy-start(f32[16,512,128]{2,1,0:T(8,128)} %get-tuple-element.395) | copy-start | bytes 12582916 | tf_op jit(solution)/shard_map/while
Sparse Core Ops, SparseCore 0:
  10.0 108.7 all-gather.4
  140.9 26.6 all-gather.6
  169.4 29.2 all-gather.8
  201.2 76.2 all-gather.10
where the time goes:
time: 291 us; the launch traced here: 287 us
  waiting for transfers between devices  185 us (64%)
  local copies, waits for them, and re-layouts  37.9 us (13%)
  matrix products  28.1 us (10%)
  between operations  13.3 us (5%)
  starting transfers between devices  12.1 us (4%)
  other arithmetic  11.2 us (4%)
    all_gather x1, waiting for transfers between devices, per_device(): lax.all_gather(qkv_weight, 'dp', axis=0, tiled=True)  84.3 us
    all_gather x1, waiting for transfers between devices, per_device(): lax.all_gather(out_weight, 'dp', axis=0, tiled=True)  39.8 us
    all_gather x1, waiting for transfers between devices, per_device(): piece_values = lax.all_gather(values, 'seq', axis=0, tiled=True)  31.1 us
    all_gather x1, waiting for transfers between devices, per_device(): piece_keys = lax.all_gather(key_rows, 'seq', axis=0, tiled=True)  23.1 us
    all_to_all x1, starting transfers between devices, per_device(): lax.all_to_all(pixels, 'dp', split_axis=0, concat_axis=0, tiled=True)  12 us
    dynamic_slice x4, local copies, waits for them, and re-layouts, one_block(): value_block = lax.dynamic_slice_in_dim(piece_values, first_row, length, 0)  11.8 us
    dot_general x2, matrix products, attend_block(): jnp.einsum('hqk,khd->qhd', weights.astype(jnp.bfloat16), value_block.resh...  9.9 us
    dot_general x2, matrix products, attend_block(): jnp.einsum('qhd,khd->hqk', queries3, key_block.reshape(count, HEADS, HDIM...  8.54 us
  transfers between devices with their start and end apart: 5, of which 5 were waited for; matrix products, arithmetic and copies ran while one was open for 17% of the time, Pallas kernels for 0%

commit v1 on v0

v1 whole, which is shorter than its diff:
```python
import functools

import jax
import jax.numpy as jnp
import numpy as np
from jax import lax
from jax.experimental import pallas as pl
from jax.experimental.pallas import tpu as pltpu
from jax.sharding import PartitionSpec as P

HEADS = 16
HDIM = 80
D = 1280
OWN = 2 * HDIM
WIDE = 768
VMEM_LIMIT = 56 * 1024 * 1024
BF16, F32 = jnp.bfloat16, jnp.float32

VM = pl.BlockSpec(memory_space=pltpu.VMEM)
SM = pl.BlockSpec(memory_space=pltpu.SMEM)


def params():
    return pltpu.CompilerParams(vmem_limit_bytes=VMEM_LIMIT)


def seq_shift(dy):
    return [((i + 2 * dy) % 8, i) for i in range(8)]


SWAP = [(i, i ^ 1) for i in range(8)]


def dp_shift(dx, dz):
    return [
        (((x + dx) % 4) * 8 + (z + dz) % 8, x * 8 + z) for x in range(4) for z in range(8)
    ]


def from_seq(value, dy):
    return lax.ppermute(value, "seq", seq_shift(dy))


def swap(value):
    return lax.ppermute(value, "seq", SWAP)


def from_dp(value, dx, dz):
    return lax.ppermute(value, "dp", dp_shift(dx, dz))


def embed_kernel(px, pw, gain, bias, emb_out, norm_out):
    emb = jnp.dot(px[...], pw[...], preferred_element_type=F32).astype(BF16)
    emb_out[...] = emb
    v = emb.astype(F32)
    center = v - jnp.mean(v, axis=-1, keepdims=True)
    var = jnp.mean(center * center, axis=-1, keepdims=True)
    norm_out[...] = (center * lax.rsqrt(var + 1e-06) * gain[...] + bias[...]).astype(BF16)


def lay_kernel(place, *refs):
    blocks, out = refs[:8], refs[8]
    col = lax.broadcasted_iota(jnp.int32, (3 * OWN, WIDE), 0)
    lane = lax.broadcasted_iota(jnp.int32, (3 * OWN, WIDE), 1)
    piece = sum((col >= HDIM * k).astype(jnp.int32) for k in range(1, 5))
    high = ((col - HDIM * piece >= HDIM // 2) & (col < 4 * HDIM)).astype(jnp.int32)
    pick = (lane == col + 48 * piece + 24 * high).astype(F32).astype(BF16)
    x, z = place[0], place[1]
    for dz in range(8):
        wide = jnp.dot(blocks[dz][...], pick, preferred_element_type=F32).astype(BF16)
        for dx in range(4):
            at = lax.rem(x + dx, 4) * 8 + lax.rem(z + dz, 8)
            out[at] = wide[dx * 40 : dx * 40 + 40]


def out_lay_kernel(place, *refs):
    out = refs[8]
    x, z, c = place[0], place[1], place[2]
    for half in range(2):
        first = pl.multiple_of(jnp.bitwise_xor(c, half) * 640, 128)
        for dx in range(4):
            for dz in range(8):
                at = lax.rem(x + dx, 4) * 8 + lax.rem(z + dz, 8)
                out[at, :, pl.ds(first, 640)] = refs[half * 4 + dx][dz]


def attend_kernel(place, *refs):
    shards = refs[:8]
    w, b, cosine, sine = refs[8:12]
    own_out, other_out = refs[12:14]
    qs, ks, vs = refs[14:17]
    scale = float(HDIM**-0.5 * np.log2(np.e))
    y, c, o1, o2 = place[0], place[1], place[2], place[3]

    def first_of(r):
        return (lax.rem(y + r // 2, 4) * 2 + jnp.bitwise_xor(c, r % 2)) * 128

    def image(p):
        return (p >= o1).astype(jnp.int32) + (p >= o2).astype(jnp.int32)

    for blk in range(4):
        rows = pl.ds(blk * 256, 256)
        x = jnp.concatenate([shards[2 * blk][...], shards[2 * blk + 1][...]], axis=0)
        proj = jnp.dot(x, w[...], preferred_element_type=F32) + b[...]
        cs, sn = cosine[rows, :], sine[rows, :]
        for h in range(2):
            for first, dst in ((0, qs), (256, ks)):
                t = proj[:, first + h * 128 : first + h * 128 + 128]
                dst[h, rows, :] = (t * cs + pltpu.roll(t, 64, 1) * sn).astype(BF16)
        vs[rows, :] = proj[:, 512:].astype(BF16)
    lane = lax.broadcasted_iota(jnp.int32, (1, 128), 1)
    key_image = jnp.concatenate([image(lane + first_of(r)) for r in range(8)], axis=1)
    row = lax.broadcasted_iota(jnp.int32, (128, 1), 0)
    wide_lane = lax.broadcasted_iota(jnp.int32, (256, 256), 1)
    for blk in range(4):
        rows = pl.ds(blk * 256, 256)
        query_image = jnp.concatenate(
            [image(row + first_of(2 * blk)), image(row + first_of(2 * blk + 1))], axis=0
        )
        allowed = query_image == key_image
        done = []
        for h in range(2):
            s = lax.dot_general(
                qs[h, rows, :], ks[h], (((1,), (1,)), ((), ())), preferred_element_type=F32
            )
            s = jnp.where(allowed, s, -1e30)
            m = jnp.max(s, axis=1, keepdims=True)
            p = jnp.exp2((s - m) * scale).astype(BF16)
            o = jnp.dot(p, vs[...], preferred_element_type=F32)
            done.append(o / o[:, OWN : OWN + 1])
        att = jnp.where(wide_lane < HDIM, done[0], done[1])[:, :OWN].astype(BF16)
        own_out[blk] = att[:128]
        other_out[blk] = att[128:]


def out_kernel(place, a0, a1, a2, a3, w, emb, bias, out):
    y, c = place[0], place[1]
    acc = emb[...].astype(F32) + bias[...]
    for dy, a in enumerate((a0, a1, a2, a3)):
        for dc in range(2):
            s = lax.rem(y + dy, 4) * 2 + jnp.bitwise_xor(c, dc)
            acc += jnp.dot(a[dc], w[s], preferred_element_type=F32)
    out[...] = acc.astype(BF16)


def halves_apart(piece):
    zero = jnp.zeros(piece.shape[:-1] + (24,), piece.dtype)
    return jnp.concatenate([piece[..., :40], zero, piece[..., 40:], zero], axis=-1)


INVERSE = np.zeros((1, 128), np.float32)
for _l in range(128):
    if _l % 64 < 40:
        INVERSE[0, _l] = 1.0 / 10000.0 ** ((_l % 64 % 20) * 2.0 / 40.0)


def rotation_tables(y, c, starts, widths):
    token = lax.broadcasted_iota(jnp.int32, (1024, 128), 0)
    lane = lax.broadcasted_iota(jnp.int32, (1024, 128), 1)
    r = token // 128
    pos = ((y + r // 2) % 4 * 2 + (c ^ (r % 2))) * 128 + token % 128
    second, third = pos >= starts[1], pos >= starts[2]
    first = jnp.where(third, starts[2], jnp.where(second, starts[1], starts[0]))
    across = jnp.where(third, widths[2], jnp.where(second, widths[1], widths[0]))
    within = pos - first
    row = within // across
    column = within - row * across
    low = lane % 64
    angle = jnp.where(low < 20, row, column).astype(F32) * INVERSE
    sign = jnp.where(lane < 64, -1.0, 1.0)
    return jnp.cos(angle), jnp.sin(angle) * sign


def per_device(
    pixels,
    patch_weight,
    ln_gain,
    ln_bias,
    qkv_weight,
    qkv_bias,
    out_weight,
    out_bias,
    offsets,
    widths,
):
    dp, seq = lax.axis_index("dp"), lax.axis_index("seq")
    x, z, y, c = dp // 8, dp % 8, seq // 2, seq % 2
    rows = jax.ShapeDtypeStruct((128, D), BF16)

    local_pixels = lax.all_to_all(pixels, "dp", split_axis=0, concat_axis=0, tiled=True)

    mine = jnp.concatenate(
        [lax.dynamic_slice_in_dim(qkv_weight, k * D + seq * OWN, OWN, 1) for k in range(3)], axis=1
    )
    xs = [mine] + [from_dp(mine, d, 0) for d in (1, 2, 3)]
    z0 = jnp.concatenate(xs, axis=0)
    z1, z7 = from_dp(z0, 0, 1), from_dp(z0, 0, 7)
    z2, z6 = from_dp(z1, 0, 1), from_dp(z7, 0, 7)
    z3, z5 = from_dp(z2, 0, 1), from_dp(z6, 0, 7)
    z4 = from_dp(z3, 0, 1)
    place_dp = jnp.stack([x, z, c]).astype(jnp.int32)
    laid = pl.pallas_call(
        lay_kernel,
        out_shape=jax.ShapeDtypeStruct((32, 40, WIDE), BF16),
        in_specs=[SM] + [VM] * 8,
        out_specs=VM,
        compiler_params=params(),
        name="lay_qkv",
    )(place_dp, z0, z1, z2, z3, z4, z5, z6, z7).reshape(D, WIDE)

    own_bias = [lax.dynamic_slice_in_dim(qkv_bias, k * D + seq * OWN, OWN, 0) for k in range(3)]
    ones = jnp.ones((1,), F32)
    laid_bias = jnp.concatenate(
        [halves_apart(own_bias[k][h * HDIM : (h + 1) * HDIM]) for k in range(2) for h in range(2)]
        + [own_bias[2], ones, jnp.zeros((95,), F32)]
    )[None]

    half = lax.dynamic_slice_in_dim(out_weight, c * 640, 640, 1)[None]
    h1, h7 = from_dp(half, 0, 1), from_dp(half, 0, 7)
    h234 = from_dp(jnp.concatenate([h7, half, h1]), 0, 3)
    h56 = from_dp(jnp.concatenate([half, h1]), 0, 5)
    column0 = jnp.concatenate([half, h1, h234, h56, h7])
    columns = [column0] + [from_dp(column0, d, 0) for d in (1, 2, 3)]
    others = [swap(v) for v in columns]
    out_laid = pl.pallas_call(
        out_lay_kernel,
        out_shape=jax.ShapeDtypeStruct((32, 40, D), BF16),
        in_specs=[SM] + [VM] * 8,
        out_specs=VM,
        compiler_params=params(),
        name="lay_out",
    )(place_dp, *columns, *others).reshape(8, OWN, D)

    embedded, normed = pl.pallas_call(
        embed_kernel,
        out_shape=(rows, rows),
        in_specs=[VM] * 4,
        out_specs=(VM, VM),
        compiler_params=params(),
        name="embed",
    )(local_pixels, patch_weight, ln_gain[None], ln_bias[None])

    same = [normed] + [from_seq(normed, d) for d in (1, 2, 3)]
    crossed = [swap(v) for v in same]
    shards = [v for pair in zip(same, crossed) for v in pair]

    starts, across = offsets[0], widths[0]
    cosine, sine = rotation_tables(y, c, starts, across)
    place = jnp.stack([y, c, starts[1], starts[2]]).astype(jnp.int32)
    part = jax.ShapeDtypeStruct((4, 128, OWN), BF16)
    own_tokens, other_tokens = pl.pallas_call(
        attend_kernel,
        out_shape=(part, part),
        in_specs=[SM] + [VM] * 12,
        out_specs=(VM, VM),
        scratch_shapes=[
            pltpu.VMEM((2, 1024, 128), BF16),
            pltpu.VMEM((2, 1024, 128), BF16),
            pltpu.VMEM((1024, 256), BF16),
        ],
        compiler_params=params(),
        name="attend",
    )(place, *shards, laid, laid_bias, cosine, sine)

    from_core = swap(other_tokens)
    pairs = [jnp.stack([own_tokens[d], from_core[d]]) for d in range(4)]
    got = [pairs[0]] + [from_seq(pairs[(4 - d) % 4], d) for d in (1, 2, 3)]
    return pl.pallas_call(
        out_kernel,
        out_shape=rows,
        in_specs=[SM] + [VM] * 7,
        out_specs=VM,
        compiler_params=params(),
        name="project",
    )(jnp.stack([y, c]).astype(jnp.int32), *got, out_laid, embedded, out_bias[None])


def solution(mesh):
    in_specs = (
        P(("dp", "seq"), None),
        P(),
        P(),
        P(),
        P("dp", None),
        P(),
        P("dp", None),
        P(),
        P("dp", None),
        P("dp", None),
    )
    out_specs = P(("dp", "seq"), None)
    return jax.shard_map(
        per_device, mesh=mesh, in_specs=in_specs, out_specs=out_specs, check_vma=False
    )
```

time: 291 us -> 150 us (0.52); the launches traced: 287 us -> 150 us
  waiting for transfers between devices: 185 us -> 36.8 us
  starting transfers between devices: 12.1 us -> 51 us
  matrix products: 28.1 us -> 0 us
  Pallas kernels: 0 us -> 24 us
  local copies, waits for them, and re-layouts: 37.9 us -> 15.8 us
  between operations: 13.3 us -> 0.32 us
  other arithmetic: 11.2 us -> 21.6 us
    all_gather x4 -> x0, waiting for transfers between devices: 178 us -> none  [the longest x1 84.3 us: per_device(): lax.all_gather(qkv_weight, 'dp', axis=0, tiled=True)]
    ppermute x0 -> x32, starting transfers between devices: none -> 46.5 us  [the longest x17 28.5 us: from_dp(): return lax.ppermute(value, 'dp', dp_shift(dx, dz))]
    ppermute x0 -> x32, waiting for transfers between devices: none -> 36.8 us  [the longest x6 20.3 us: from_seq(): return lax.ppermute(value, 'seq', seq_shift(dy))]
    dot_general x7 -> x0, matrix products: 28.1 us -> none  [the longest x2 9.9 us: attend_block(): jnp.einsum('hqk,khd->qhd', weights.astype(jnp.bfloat16), value_block.resh...]
    pallas_call x0 -> x5, Pallas kernels: none -> 24 us  [the longest x1 8.86 us: per_device(): pl.pallas_call(attend_kernel, out_shape=(part, part), in_specs=[SM] + [VM...]
    dynamic_slice x6 -> x2, local copies, waits for them, and re-layouts: 16.7 us -> 2.29 us  [the longest x1 1.39 us: per_device(): lax.dynamic_slice_in_dim(qkv_bias, k * D + seq * OWN, OWN, 0)]
    mul x2 -> x1, other arithmetic: 1.23 us -> 15.3 us  [rotation_tables(): return (jnp.cos(angle), jnp.sin(angle) * sign)]
    all_to_all x1, starting transfers between devices: 12 us -> 4.49 us  [per_device(): lax.all_to_all(pixels, 'dp', split_axis=0, concat_axis=0, tiled=True)]
  transfers between devices with their start and end apart: 5 -> 33, of which waited for: 5 -> 9; matrix products, arithmetic and copies ran while one was open for 17% -> 22% of each run, Pallas kernels for 0% -> 8%
where the time goes in v1:
time: 150 us
  starting transfers between devices  51 us (34%)
  waiting for transfers between devices  36.8 us (25%)
  Pallas kernels  24 us (16%)
  other arithmetic  21.6 us (14%)
  local copies, waits for them, and re-layouts  15.8 us (11%)
    ppermute x17, starting transfers between devices, from_dp(): return lax.ppermute(value, 'dp', dp_shift(dx, dz))  28.5 us
    ppermute x6, waiting for transfers between devices, from_seq(): return lax.ppermute(value, 'seq', seq_shift(dy))  20.3 us
    ppermute x17, waiting for transfers between devices, from_dp(): return lax.ppermute(value, 'dp', dp_shift(dx, dz))  16 us
    mul x1, other arithmetic, rotation_tables(): return (jnp.cos(angle), jnp.sin(angle) * sign)  15.3 us
    ppermute x9, starting transfers between devices, swap(): return lax.ppermute(value, 'seq', SWAP)  10.9 us
    pallas_call x1, Pallas kernels, per_device(): pl.pallas_call(attend_kernel, out_shape=(part, part), in_specs=[SM] + [VM...  8.86 us
    ppermute x6, starting transfers between devices, from_seq(): return lax.ppermute(value, 'seq', seq_shift(dy))  7.19 us
    all_to_all x1, starting transfers between devices, per_device(): lax.all_to_all(pixels, 'dp', split_axis=0, concat_axis=0, tiled=True)  4.49 us
  transfers between devices with their start and end apart: 33, of which 9 were waited for; matrix products, arithmetic and copies ran while one was open for 22% of the time, Pallas kernels for 8%

profile of v1, /device:TPU:1, one launch (start us, length us, event | category | flops | bytes accessed | tf_op | source)
XLA Modules:
  0.0 149.5 jit_solution(17724012778731403340)
XLA Ops:
  0.0 0.9 constant_dynamic-slice_fusion.2
  1.0 2.1 %collective-permute-start.9 = (bf16[40,480]{1,0:T(8,128)(2,1)S(1)}, bf16[40,480]{1,0:T(8,128)(2,1)S(1)}, u32[]{:S(2)}, u32[]{:S(2)}) collective-permute-start(bf16[40,480]{1,0:T(8,128)(2,1)S(1)} %pad_maximum_fusion.7), channel_id=1, source_target_pairs={{192,0},{200,8},{208,16},{216,24},{224,32},{232,40},{240,48},{248,... | collective-permute-start | bytes 115208 | tf_op jit(solution)/shard_map/ppermute | solution.py:49
  3.1 2.5 %collective-permute-start.8 = (bf16[40,480]{1,0:T(8,128)(2,1)S(1)}, bf16[40,480]{1,0:T(8,128)(2,1)S(1)}, u32[]{:S(2)}, u32[]{:S(2)}) collective-permute-start(bf16[40,480]{1,0:T(8,128)(2,1)S(1)} %pad_maximum_fusion.7), channel_id=1, source_target_pairs={{128,0},{136,8},{144,16},{152,24},{160,32},{168,40},{176,48},{184,... | collective-permute-start | bytes 115208 | tf_op jit(solution)/shard_map/ppermute | solution.py:49
  5.6 1.2 collective-permute-start.7
  6.7 0.8 constant_dynamic-update-slice_fusion.4
  7.5 5.6 %collective-permute-start.21 = (bf16[1,40,640]{2,1,0:T(8,128)(2,1)S(1)}, bf16[1,40,640]{2,1,0:T(8,128)(2,1)S(1)}, u32[]{:S(2)}, u32[]{:S(2)}) collective-permute-start(bf16[1,40,640]{2,1,0:T(8,128)(2,1)S(1)} %get-tuple-element.14), channel_id=1, source_target_pairs={{8,0},{16,8},{24,16},{32,24},{40,32},{48,40},{56,48},{0,56},{72,64... | collective-permute-start | bytes 153608 | tf_op jit(solution)/shard_map/ppermute | solution.py:49
  13.2 1.1 copy.13
  14.3 0.8 all_to_all.7
  15.1 4.5 %all-to-all-start = ((bf16[32,4,1176]{2,1,0:T(4,128)(2,1)}), bf16[32,4,1176]{2,1,0:T(4,128)(2,1)S(1)}, u32[]{:S(2)}, u32[]{:S(2)}) async-start(bf16[32,4,1176]{2,1,0:T(4,128)(2,1)} %all_to_all.7), calls=%async_computation | async-start | bytes 655360 | tf_op jit(solution)/shard_map/all_to_all | solution.py:190
  19.7 0.6 fusion.16
  20.3 1.4 fusion.24
  21.6 1.4 fusion.21
  23.0 1.4 fusion.25
  24.4 0.6 iota_and_fusion.1
  25.1 2.5 %collective-permute-start.10 = (bf16[160,480]{1,0:T(8,128)(2,1)S(1)}, bf16[160,480]{1,0:T(8,128)(2,1)S(1)}, u32[]{:S(2)}, u32[]{:S(2)}) collective-permute-start(bf16[160,480]{1,0:T(8,128)(2,1)S(1)} %pad_maximum_fusion.refs_0_), channel_id=1, source_target_pairs={{8,0},{16,8},{24,16},{32,24},{40,32},{48,40},{56,48},{0,56},{72,64... | collective-permute-start | bytes 460808 | tf_op jit(solution)/shard_map/ppermute | solution.py:49
  27.7 3.3 %collective-permute-start.23 = (bf16[3,40,640]{2,1,0:T(8,128)(2,1)S(1)}, bf16[3,40,640]{2,1,0:T(8,128)(2,1)S(1)}, u32[]{:S(2)}, u32[]{:S(2)}) collective-permute-start(bf16[3,40,640]{2,1,0:T(8,128)(2,1)S(1)} %pad_maximum_fusion.1), channel_id=1, source_target_pairs={{24,0},{32,8},{40,16},{48,24},{56,32},{0,40},{8,48},{16,56},{88,64... | collective-permute-start | bytes 460808 | tf_op jit(solution)/shard_map/ppermute | solution.py:49
  31.2 3.9 %collective-permute-start.11 = (bf16[160,480]{1,0:T(8,128)(2,1)S(1)}, bf16[160,480]{1,0:T(8,128)(2,1)S(1)}, u32[]{:S(2)}, u32[]{:S(2)}) collective-permute-start(bf16[160,480]{1,0:T(8,128)(2,1)S(1)} %collective-permute-done.10.refs_1_), channel_id=1, source_target_pairs={{8,0},{16,8},{24,16},{32,24},{40,32},{48,40},{56,48},{0,56},{72,64... | collective-permute-start | bytes 460808 | tf_op jit(solution)/shard_map/ppermute | solution.py:49
  35.1 4.5 %collective-permute-done.23 = bf16[3,40,640]{2,1,0:T(8,128)(2,1)S(1)} collective-permute-done((bf16[3,40,640]{2,1,0:T(8,128)(2,1)S(1)}, bf16[3,40,640]{2,1,0:T(8,128)(2,1)S(1)}, u32[]{:S(2)}, u32[]{:S(2)}) %collective-permute-start.23) | collective-permute-done | bytes 153632 | tf_op jit(solution)/shard_map/ppermute | solution.py:49
  39.6 5.1 %collective-permute-done.11.refs_2_ = bf16[160,480]{1,0:T(8,128)(2,1)S(1)} collective-permute-done((bf16[160,480]{1,0:T(8,128)(2,1)S(1)}, bf16[160,480]{1,0:T(8,128)(2,1)S(1)}, u32[]{:S(2)}, u32[]{:S(2)}) %collective-permute-start.11) | collective-permute-done | bytes 153632 | tf_op jit(solution)/shard_map/ppermute | solution.py:49
  44.8 3.6 %collective-permute-start.12 = (bf16[160,480]{1,0:T(8,128)(2,1)S(1)}, bf16[160,480]{1,0:T(8,128)(2,1)}, u32[]{:S(2)}, u32[]{:S(2)}) collective-permute-start(bf16[160,480]{1,0:T(8,128)(2,1)S(1)} %collective-permute-done.11.refs_2_), channel_id=1, source_target_pairs={{8,0},{16,8},{24,16},{32,24},{40,32},{48,40},{56,48},{0,56},{72,64... | collective-permute-start | bytes 460808 | tf_op jit(solution)/shard_map/ppermute | solution.py:49
  48.3 2.5 %collective-permute-start.25 = (bf16[8,40,640]{2,1,0:T(8,128)(2,1)S(1)}, bf16[8,40,640]{2,1,0:T(8,128)(2,1)S(1)}, u32[]{:S(2)}, u32[]{:S(2)}) collective-permute-start(bf16[8,40,640]{2,1,0:T(8,128)(2,1)S(1)} %constant_dynamic-update-slice_fusion.refs_0_), channel_id=1, source_target_pairs={{64,0},{72,8},{80,16},{88,24},{96,32},{104,40},{112,48},{120,56},{... | collective-permute-start | bytes 1228808 | tf_op jit(solution)/shard_map/ppermute | solution.py:49
  50.9 0.5 collective-permute-start.26
  51.4 0.6 compare_select_fusion
  52.0 0.6 collective-permute-start.27
  52.6 3.1 %collective-permute-start.28 = (bf16[8,40,640]{2,1,0:T(8,128)(2,1)S(1)}, bf16[8,40,640]{2,1,0:T(8,128)(2,1)S(1)}, u32[]{:S(2)}, u32[]{:S(2)}) collective-permute-start(bf16[8,40,640]{2,1,0:T(8,128)(2,1)S(1)} %constant_dynamic-update-slice_fusion.refs_0_), channel_id=1, source_target_pairs={{0,1},{1,0},{2,3},{3,2},{4,5},{5,4},{6,7},{7,6},{8,9},{9,8},{10,11... | collective-permute-start | bytes 1228808 | tf_op jit(solution)/shard_map/ppermute | solution.py:45
  55.7 0.6 compare_and_fusion
  56.3 6.4 %collective-permute-done.16.refs_5_ = bf16[160,480]{1,0:T(8,128)(2,1)S(1)} collective-permute-done((bf16[160,480]{1,0:T(8,128)(2,1)S(1)}, bf16[160,480]{1,0:T(8,128)(2,1)S(1)}, u32[]{:S(2)}, u32[]{:S(2)}) %collective-permute-start.16) | collective-permute-done | bytes 153632 | tf_op jit(solution)/shard_map/ppermute | solution.py:49
  62.7 0.6 pad_add_fusion.place
  63.2 0.6 broadcast_in_dim.43.gain
  63.8 0.6 broadcast_in_dim.44.bias
  64.4 4.9 %collective-permute-start.29 = (bf16[8,40,640]{2,1,0:T(8,128)(2,1)S(1)}, bf16[8,40,640]{2,1,0:T(8,128)(2,1)S(1)}, u32[]{:S(2)}, u32[]{:S(2)}) collective-permute-start(bf16[8,40,640]{2,1,0:T(8,128)(2,1)S(1)} %collective-permute-done.25.refs_1_), channel_id=1, source_target_pairs={{0,1},{1,0},{2,3},{3,2},{4,5},{5,4},{6,7},{7,6},{8,9},{9,8},{10,11... | collective-permute-start | bytes 1228808 | tf_op jit(solution)/shard_map/ppermute | solution.py:45
  69.5 1.8 %pad_add_fusion.1.place = s32[4]{0:T(128)} fusion(s32[1]{0:T(128)} %bitcast.3, s32[1]{0:T(128)} %bitcast.2, s32[1]{0:T(128)} %bitcast.1, s32[1]{0:T(128)} %bitcast), kind=kLoop, calls=%fused_computation.62 | loop fusion | flops 12 | bytes 32 | tf_op jit(solution)/shard_map/stack | solution.py:249
  71.3 0.9 all_to_all.9.px
  72.1 3.5 %embed.1 = (bf16[128,1280]{1,0:T(8,128)(2,1)}, bf16[128,1280]{1,0:T(8,128)(2,1)}) custom-call(bf16[128,1176]{1,0:T(8,128)(2,1)} %all_to_all.9.px, bf16[1176,1280]{1,0:T(8,128)(2,1)} %pw.1, f32[1,1280]{1,0:T(1,128)} %broadcast_in_dim.43.gain, f32[1,1280]{1,0:T(1,128)} %broadcast_in_dim.44.bias), custom_call_target="tpu_custom_call" | custom-call | tf_op jit(solution)/shard_map/embed/pallas_call | solution.py:234
  75.6 2.7 %collective-permute-start.1 = (bf16[128,1280]{1,0:T(8,128)(2,1)}, bf16[128,1280]{1,0:T(8,128)(2,1)S(1)}, u32[]{:S(2)}, u32[]{:S(2)}) collective-permute-start(bf16[128,1280]{1,0:T(8,128)(2,1)} %get-tuple-element.9.refs_0_), channel_id=1, source_target_pairs={{2,0},{3,1},{4,2},{5,3},{6,4},{7,5},{0,6},{1,7},{10,8},{11,9},{12,... | collective-permute-start | bytes 983048 | tf_op jit(solution)/shard_map/ppermute | solution.py:41
  78.4 0.4 collective-permute-start.3
  78.7 0.7 collective-permute-start.5
  79.4 0.6 pad_add_fusion.2.place
  80.0 0.7 fusion.22
  80.7 11.6 %collective-permute-done.1.refs_2_ = bf16[128,1280]{1,0:T(8,128)(2,1)S(1)} collective-permute-done((bf16[128,1280]{1,0:T(8,128)(2,1)}, bf16[128,1280]{1,0:T(8,128)(2,1)S(1)}, u32[]{:S(2)}, u32[]{:S(2)}) %collective-permute-start.1) | collective-permute-done | bytes 327712 | tf_op jit(solution)/shard_map/ppermute | solution.py:41
  92.3 1.4 collective-permute-start.31
  93.6 0.5 broadcast_in_dim.45
  94.2 0.8 concatenate.20
  94.9 0.6 broadcast_in_dim.46.refs_9_
  95.5 0.6 broadcast_in_dim.54.bias
  96.2 0.7 collective-permute-done.5.refs_6_
  96.9 0.5 collective-permute-start.2
  97.5 0.4 collective-permute-start.6
  97.9 15.3 %sine_multiply_fusion = (f32[1024,128]{1,0:T(8,128)}, f32[1024,128]{1,0:T(8,128)}) fusion(f32[128]{0:T(128)} %compare_select_fusion, f32[128]{0:T(128)} %constant.157, s32[]{:T(128)} %bitcast.12, s32[]{:T(128)} %bitcast.11, s32[]{:T(128)} %bitcast.10, s32[]{:T(128)} %bitcast.9, s32[]{:T(128)} %bitcast.8, s32[]{:T(128)} %bitcast.7, ...), kind=kLoop, calls=%fused_computation.22 | loop fusion | flops 8126464 | bytes 1069216 | tf_op jit(solution)/shard_map/mul | solution.py:171
  113.2 3.9 %lay_qkv.1 = bf16[32,40,768]{2,1,0:T(8,128)(2,1)} custom-call(s32[3]{0:T(128)} %pad_add_fusion.2.place, bf16[160,480]{1,0:T(8,128)(2,1)} %copy-done, bf16[160,480]{1,0:T(8,128)(2,1)} %copy-done.13, bf16[160,480]{1,0:T(8,128)(2,1)} %copy-done.15, bf16[160,480]{1,0:T(8,128)(2,1)} %collective-permute-done.12.refs_3_, ...), custom_call_target="tpu_custom_call" | custom-call | tf_op jit(solution)/shard_map/lay_qkv/pallas_call | solution.py:202
  117.2 3.9 %lay_out.1 = bf16[32,40,1280]{2,1,0:T(8,128)(2,1)} custom-call(s32[3]{0:T(128)} %pad_add_fusion.2.place, bf16[8,40,640]{2,1,0:T(8,128)(2,1)} %copy-done.1, bf16[8,40,640]{2,1,0:T(8,128)(2,1)} %copy-done.2, bf16[8,40,640]{2,1,0:T(8,128)(2,1)} %copy-done.3, bf16[8,40,640]{2,1,0:T(8,128)(2,1)} %copy-done.4, bf16[8,40,640]{2,1,0:T(8,128)(2,1)} %copy-done.5, ...), custom_call_target="tpu_custom_call" | custom-call | tf_op jit(solution)/shard_map/lay_out/pallas_call | solution.py:225
  121.2 0.7 copy-done.9
  122.2 8.9 %attend.1 = (bf16[4,128,160]{2,1,0:T(8,128)(2,1)}, bf16[4,128,160]{2,1,0:T(8,128)(2,1)}) custom-call(s32[4]{0:T(128)} %pad_add_fusion.1.place, bf16[128,1280]{1,0:T(8,128)(2,1)} %get-tuple-element.9.refs_0_, bf16[128,1280]{1,0:T(8,128)(2,1)} %copy-done.9, bf16[128,1280]{1,0:T(8,128)(2,1)} %copy-done.8, bf16[128,1280]{1,0:T(8,128)(2,1)} %copy-done.10, ...), custom_call_target="tpu_custom_call" | custom-call | tf_op jit(solution)/shard_map/attend/pallas_call | solution.py:251
  131.0 0.3 collective-permute-start.17
  131.4 1.0 fusion.19
  132.3 0.5 collective-permute-done.17
  132.8 2.7 %collective-permute-start.18 = (bf16[2,128,160]{2,1,0:T(8,128)(2,1)S(1)}, bf16[2,128,160]{2,1,0:T(8,128)(2,1)S(1)}, u32[]{:S(2)}, u32[]{:S(2)}) collective-permute-start(bf16[2,128,160]{2,1,0:T(8,128)(2,1)S(1)} %pad_maximum_fusion.3), channel_id=1, source_target_pairs={{2,0},{3,1},{4,2},{5,3},{6,4},{7,5},{0,6},{1,7},{10,8},{11,9},{12,... | collective-permute-start | bytes 245768 | tf_op jit(solution)/shard_map/ppermute | solution.py:41
  135.7 0.7 collective-permute-start.20
  136.3 0.7 pad_maximum_fusion.2.a0
  137.0 3.8 %collective-permute-done.18.a1 = bf16[2,128,160]{2,1,0:T(8,128)(2,1)S(1)} collective-permute-done((bf16[2,128,160]{2,1,0:T(8,128)(2,1)S(1)}, bf16[2,128,160]{2,1,0:T(8,128)(2,1)S(1)}, u32[]{:S(2)}, u32[]{:S(2)}) %collective-permute-start.18) | collective-permute-done | bytes 81952 | tf_op jit(solution)/shard_map/ppermute | solution.py:41
  140.8 0.9 collective-permute-done.19.a2
  141.7 3.4 %collective-permute-done.20.a3 = bf16[2,128,160]{2,1,0:T(8,128)(2,1)S(1)} collective-permute-done((bf16[2,128,160]{2,1,0:T(8,128)(2,1)S(1)}, bf16[2,128,160]{2,1,0:T(8,128)(2,1)S(1)}, u32[]{:S(2)}, u32[]{:S(2)}) %collective-permute-start.20) | collective-permute-done | bytes 81952 | tf_op jit(solution)/shard_map/ppermute | solution.py:41
  145.0 0.6 copy-done.20
  145.7 3.8 %project.1 = bf16[128,1280]{1,0:T(8,128)(2,1)} custom-call(s32[2]{0:T(128)} %pad_add_fusion.place, bf16[2,128,160]{2,1,0:T(8,128)(2,1)} %pad_maximum_fusion.2.a0, bf16[2,128,160]{2,1,0:T(8,128)(2,1)} %copy-done.18, bf16[2,128,160]{2,1,0:T(8,128)(2,1)} %copy-done.19, bf16[2,128,160]{2,1,0:T(8,128)(2,1)} %copy-done.20, bf16[8,160,1280]{2,1,0:T(8,128)(2,1)} %bitcast.17, ...), custom_call_target="tpu_custom_call" | custom-call | tf_op jit(solution)/shard_map/project/pallas_call | solution.py:268
  (95 shorter events, 1.3 us)
Async XLA Ops:
  0.0 63.2 %copy-start.21 = (f32[1280]{0:T(1024)S(1)}, f32[1280]{0:T(1024)}, u32[]{:S(2)}) copy-start(f32[1280]{0:T(1024)} %param.13) | copy-start | bytes 15364
  0.0 63.8 %copy-start.22 = (f32[1280]{0:T(1024)S(1)}, f32[1280]{0:T(1024)}, u32[]{:S(2)}) copy-start(f32[1280]{0:T(1024)} %param.14) | copy-start | bytes 15364
  1.0 24.0 %collective-permute-start.9 = (bf16[40,480]{1,0:T(8,128)(2,1)S(1)}, bf16[40,480]{1,0:T(8,128)(2,1)S(1)}, u32[]{:S(2)}, u32[]{:S(2)}) collective-permute-start(bf16[40,480]{1,0:T(8,128)(2,1)S(1)} %pad_maximum_fusion.7), channel_id=1, source_target_pairs={{192,0},{200,8},{208,16},{216,24},{224,32},{232,40},{240,48},{248,... | collective-permute-start | bytes 115208 | tf_op jit(solution)/shard_map/ppermute | solution.py:49
  3.1 21.9 %collective-permute-start.8 = (bf16[40,480]{1,0:T(8,128)(2,1)S(1)}, bf16[40,480]{1,0:T(8,128)(2,1)S(1)}, u32[]{:S(2)}, u32[]{:S(2)}) collective-permute-start(bf16[40,480]{1,0:T(8,128)(2,1)S(1)} %pad_maximum_fusion.7), channel_id=1, source_target_pairs={{128,0},{136,8},{144,16},{152,24},{160,32},{168,40},{176,48},{184,... | collective-permute-start | bytes 115208 | tf_op jit(solution)/shard_map/ppermute | solution.py:49
  5.6 19.4 %collective-permute-start.7 = (bf16[40,480]{1,0:T(8,128)(2,1)S(1)}, bf16[40,480]{1,0:T(8,128)(2,1)S(1)}, u32[]{:S(2)}, u32[]{:S(2)}) collective-permute-start(bf16[40,480]{1,0:T(8,128)(2,1)S(1)} %pad_maximum_fusion.7), channel_id=1, source_target_pairs={{64,0},{72,8},{80,16},{88,24},{96,32},{104,40},{112,48},{120,56},{... | collective-permute-start | bytes 115208 | tf_op jit(solution)/shard_map/ppermute | solution.py:49
  7.5 20.1 %collective-permute-start.21 = (bf16[1,40,640]{2,1,0:T(8,128)(2,1)S(1)}, bf16[1,40,640]{2,1,0:T(8,128)(2,1)S(1)}, u32[]{:S(2)}, u32[]{:S(2)}) collective-permute-start(bf16[1,40,640]{2,1,0:T(8,128)(2,1)S(1)} %get-tuple-element.14), channel_id=1, source_target_pairs={{8,0},{16,8},{24,16},{32,24},{40,32},{48,40},{56,48},{0,56},{72,64... | collective-permute-start | bytes 153608 | tf_op jit(solution)/shard_map/ppermute | solution.py:49
  13.2 14.5 %collective-permute-start.22 = (bf16[1,40,640]{2,1,0:T(8,128)(2,1)S(1)}, bf16[1,40,640]{2,1,0:T(8,128)(2,1)S(1)}, u32[]{:S(2)}, u32[]{:S(2)}) collective-permute-start(bf16[1,40,640]{2,1,0:T(8,128)(2,1)S(1)} %get-tuple-element.14), channel_id=1, source_target_pairs={{56,0},{0,8},{8,16},{16,24},{24,32},{32,40},{40,48},{48,56},{120,6... | collective-permute-start | bytes 153608 | tf_op jit(solution)/shard_map/ppermute | solution.py:49
  15.1 56.1 %all-to-all-start = ((bf16[32,4,1176]{2,1,0:T(4,128)(2,1)}), bf16[32,4,1176]{2,1,0:T(4,128)(2,1)S(1)}, u32[]{:S(2)}, u32[]{:S(2)}) async-start(bf16[32,4,1176]{2,1,0:T(4,128)(2,1)} %all_to_all.7), calls=%async_computation | async-start | bytes 655360 | tf_op jit(solution)/shard_map/all_to_all | solution.py:190
  19.6 75.9 %copy-start.23 = (f32[1280]{0:T(1024)S(1)}, f32[1280]{0:T(1024)}, u32[]{:S(2)}) copy-start(f32[1280]{0:T(1024)} %param.18) | copy-start | bytes 15364
  25.1 88.1 %copy-start = (bf16[160,480]{1,0:T(8,128)(2,1)}, bf16[160,480]{1,0:T(8,128)(2,1)S(1)}, u32[]{:S(2)}) copy-start(bf16[160,480]{1,0:T(8,128)(2,1)S(1)} %pad_maximum_fusion.refs_0_) | copy-start | bytes 460804
  25.1 6.0 %collective-permute-start.10 = (bf16[160,480]{1,0:T(8,128)(2,1)S(1)}, bf16[160,480]{1,0:T(8,128)(2,1)S(1)}, u32[]{:S(2)}, u32[]{:S(2)}) collective-permute-start(bf16[160,480]{1,0:T(8,128)(2,1)S(1)} %pad_maximum_fusion.refs_0_), channel_id=1, source_target_pairs={{8,0},{16,8},{24,16},{32,24},{40,32},{48,40},{56,48},{0,56},{72,64... | collective-permute-start | bytes 460808 | tf_op jit(solution)/shard_map/ppermute | solution.py:49
  27.6 7.5 %collective-permute-start.14 = (bf16[160,480]{1,0:T(8,128)(2,1)S(1)}, bf16[160,480]{1,0:T(8,128)(2,1)S(1)}, u32[]{:S(2)}, u32[]{:S(2)}) collective-permute-start(bf16[160,480]{1,0:T(8,128)(2,1)S(1)} %pad_maximum_fusion.refs_0_), channel_id=1, source_target_pairs={{56,0},{0,8},{8,16},{16,24},{24,32},{32,40},{40,48},{48,56},{120,6... | collective-permute-start | bytes 460808 | tf_op jit(solution)/shard_map/ppermute | solution.py:49
  27.7 11.9 %collective-permute-start.23 = (bf16[3,40,640]{2,1,0:T(8,128)(2,1)S(1)}, bf16[3,40,640]{2,1,0:T(8,128)(2,1)S(1)}, u32[]{:S(2)}, u32[]{:S(2)}) collective-permute-start(bf16[3,40,640]{2,1,0:T(8,128)(2,1)S(1)} %pad_maximum_fusion.1), channel_id=1, source_target_pairs={{24,0},{32,8},{40,16},{48,24},{56,32},{0,40},{8,48},{16,56},{88,64... | collective-permute-start | bytes 460808 | tf_op jit(solution)/shard_map/ppermute | solution.py:49
  31.0 8.6 %collective-permute-start.24 = (bf16[2,40,640]{2,1,0:T(8,128)(2,1)S(1)}, bf16[2,40,640]{2,1,0:T(8,128)(2,1)S(1)}, u32[]{:S(2)}, u32[]{:S(2)}) collective-permute-start(bf16[2,40,640]{2,1,0:T(8,128)(2,1)S(1)} %pad_maximum_fusion.6), channel_id=1, source_target_pairs={{40,0},{48,8},{56,16},{0,24},{8,32},{16,40},{24,48},{32,56},{104,6... | collective-permute-start | bytes 307208 | tf_op jit(solution)/shard_map/ppermute | solution.py:49
  31.2 82.1 %copy-start.13 = (bf16[160,480]{1,0:T(8,128)(2,1)}, bf16[160,480]{1,0:T(8,128)(2,1)S(1)}, u32[]{:S(2)}) copy-start(bf16[160,480]{1,0:T(8,128)(2,1)S(1)} %collective-permute-done.10.refs_1_) | copy-start | bytes 460804
  31.2 13.6 %collective-permute-start.11 = (bf16[160,480]{1,0:T(8,128)(2,1)S(1)}, bf16[160,480]{1,0:T(8,128)(2,1)S(1)}, u32[]{:S(2)}, u32[]{:S(2)}) collective-permute-start(bf16[160,480]{1,0:T(8,128)(2,1)S(1)} %collective-permute-done.10.refs_1_), channel_id=1, source_target_pairs={{8,0},{16,8},{24,16},{32,24},{40,32},{48,40},{56,48},{0,56},{72,64... | collective-permute-start | bytes 460808 | tf_op jit(solution)/shard_map/ppermute | solution.py:49
  35.1 17.5 %copy-start.14 = (bf16[160,480]{1,0:T(8,128)(2,1)}, bf16[160,480]{1,0:T(8,128)(2,1)S(1)}, u32[]{:S(2)}) copy-start(bf16[160,480]{1,0:T(8,128)(2,1)S(1)} %collective-permute-done.14.refs_7_) | copy-start | bytes 460804
  35.1 17.5 %collective-permute-start.15 = (bf16[160,480]{1,0:T(8,128)(2,1)S(1)}, bf16[160,480]{1,0:T(8,128)(2,1)S(1)}, u32[]{:S(2)}, u32[]{:S(2)}) collective-permute-start(bf16[160,480]{1,0:T(8,128)(2,1)S(1)} %collective-permute-done.14.refs_7_), channel_id=1, source_target_pairs={{56,0},{0,8},{8,16},{16,24},{24,32},{32,40},{40,48},{48,56},{120,6... | collective-permute-start | bytes 460808 | tf_op jit(solution)/shard_map/ppermute | solution.py:49
  44.8 19.7 %copy-start.15 = (bf16[160,480]{1,0:T(8,128)(2,1)}, bf16[160,480]{1,0:T(8,128)(2,1)S(1)}, u32[]{:S(2)}) copy-start(bf16[160,480]{1,0:T(8,128)(2,1)S(1)} %collective-permute-done.11.refs_2_) | copy-start | bytes 460804
  44.8 10.9 %collective-permute-start.12 = (bf16[160,480]{1,0:T(8,128)(2,1)S(1)}, bf16[160,480]{1,0:T(8,128)(2,1)}, u32[]{:S(2)}, u32[]{:S(2)}) collective-permute-start(bf16[160,480]{1,0:T(8,128)(2,1)S(1)} %collective-permute-done.11.refs_2_), channel_id=1, source_target_pairs={{8,0},{16,8},{24,16},{32,24},{40,32},{48,40},{56,48},{0,56},{72,64... | collective-permute-start | bytes 460808 | tf_op jit(solution)/shard_map/ppermute | solution.py:49
  48.3 68.8 %copy-start.1 = (bf16[8,40,640]{2,1,0:T(8,128)(2,1)}, bf16[8,40,640]{2,1,0:T(8,128)(2,1)S(1)}, u32[]{:S(2)}) copy-start(bf16[8,40,640]{2,1,0:T(8,128)(2,1)S(1)} %constant_dynamic-update-slice_fusion.refs_0_) | copy-start | bytes 1228804
  48.3 16.1 %collective-permute-start.25 = (bf16[8,40,640]{2,1,0:T(8,128)(2,1)S(1)}, bf16[8,40,640]{2,1,0:T(8,128)(2,1)S(1)}, u32[]{:S(2)}, u32[]{:S(2)}) collective-permute-start(bf16[8,40,640]{2,1,0:T(8,128)(2,1)S(1)} %constant_dynamic-update-slice_fusion.refs_0_), channel_id=1, source_target_pairs={{64,0},{72,8},{80,16},{88,24},{96,32},{104,40},{112,48},{120,56},{... | collective-permute-start | bytes 1228808 | tf_op jit(solution)/shard_map/ppermute | solution.py:49
  50.9 18.5 %collective-permute-start.26 = (bf16[8,40,640]{2,1,0:T(8,128)(2,1)S(1)}, bf16[8,40,640]{2,1,0:T(8,128)(2,1)S(1)}, u32[]{:S(2)}, u32[]{:S(2)}) collective-permute-start(bf16[8,40,640]{2,1,0:T(8,128)(2,1)S(1)} %constant_dynamic-update-slice_fusion.refs_0_), channel_id=1, source_target_pairs={{128,0},{136,8},{144,16},{152,24},{160,32},{168,40},{176,48},{184,... | collective-permute-start | bytes 1228808 | tf_op jit(solution)/shard_map/ppermute | solution.py:49
  52.0 23.6 %collective-permute-start.27 = (bf16[8,40,640]{2,1,0:T(8,128)(2,1)S(1)}, bf16[8,40,640]{2,1,0:T(8,128)(2,1)S(1)}, u32[]{:S(2)}, u32[]{:S(2)}) collective-permute-start(bf16[8,40,640]{2,1,0:T(8,128)(2,1)S(1)} %constant_dynamic-update-slice_fusion.refs_0_), channel_id=1, source_target_pairs={{192,0},{200,8},{208,16},{216,24},{224,32},{232,40},{240,48},{248,... | collective-permute-start | bytes 1228808 | tf_op jit(solution)/shard_map/ppermute | solution.py:49
  52.6 11.8 %copy-start.16 = (bf16[160,480]{1,0:T(8,128)(2,1)}, bf16[160,480]{1,0:T(8,128)(2,1)S(1)}, u32[]{:S(2)}) copy-start(bf16[160,480]{1,0:T(8,128)(2,1)S(1)} %collective-permute-done.15.refs_6_) | copy-start | bytes 460804
  52.6 25.8 %collective-permute-start.28 = (bf16[8,40,640]{2,1,0:T(8,128)(2,1)S(1)}, bf16[8,40,640]{2,1,0:T(8,128)(2,1)S(1)}, u32[]{:S(2)}, u32[]{:S(2)}) collective-permute-start(bf16[8,40,640]{2,1,0:T(8,128)(2,1)S(1)} %constant_dynamic-update-slice_fusion.refs_0_), channel_id=1, source_target_pairs={{0,1},{1,0},{2,3},{3,2},{4,5},{5,4},{6,7},{7,6},{8,9},{9,8},{10,11... | collective-permute-start | bytes 1228808 | tf_op jit(solution)/shard_map/ppermute | solution.py:45
  55.7 7.0 %collective-permute-start.16 = (bf16[160,480]{1,0:T(8,128)(2,1)S(1)}, bf16[160,480]{1,0:T(8,128)(2,1)S(1)}, u32[]{:S(2)}, u32[]{:S(2)}) collective-permute-start(bf16[160,480]{1,0:T(8,128)(2,1)S(1)} %collective-permute-done.15.refs_6_), channel_id=1, source_target_pairs={{56,0},{0,8},{8,16},{16,24},{24,32},{32,40},{40,48},{48,56},{120,6... | collective-permute-start | bytes 460808 | tf_op jit(solution)/shard_map/ppermute | solution.py:49
  62.6 1.8 %copy-start.17 = (bf16[160,480]{1,0:T(8,128)(2,1)}, bf16[160,480]{1,0:T(8,128)(2,1)S(1)}, u32[]{:S(2)}) copy-start(bf16[160,480]{1,0:T(8,128)(2,1)S(1)} %collective-permute-done.16.refs_5_) | copy-start | bytes 460804
  62.6 16.1 %collective-permute-start.13 = (bf16[160,480]{1,0:T(8,128)(2,1)}, bf16[160,480]{1,0:T(8,128)(2,1)}, u32[]{:S(2)}, u32[]{:S(2)}) collective-permute-start(bf16[160,480]{1,0:T(8,128)(2,1)} %collective-permute-done.12.refs_3_), channel_id=1, source_target_pairs={{8,0},{16,8},{24,16},{32,24},{40,32},{48,40},{56,48},{0,56},{72,64... | collective-permute-start | bytes 460808 | tf_op jit(solution)/shard_map/ppermute | solution.py:49
  64.4 52.7 %copy-start.2 = (bf16[8,40,640]{2,1,0:T(8,128)(2,1)}, bf16[8,40,640]{2,1,0:T(8,128)(2,1)S(1)}, u32[]{:S(2)}) copy-start(bf16[8,40,640]{2,1,0:T(8,128)(2,1)S(1)} %collective-permute-done.25.refs_1_) | copy-start | bytes 1228804
  64.4 32.9 %collective-permute-start.29 = (bf16[8,40,640]{2,1,0:T(8,128)(2,1)S(1)}, bf16[8,40,640]{2,1,0:T(8,128)(2,1)S(1)}, u32[]{:S(2)}, u32[]{:S(2)}) collective-permute-start(bf16[8,40,640]{2,1,0:T(8,128)(2,1)S(1)} %collective-permute-done.25.refs_1_), channel_id=1, source_target_pairs={{0,1},{1,0},{2,3},{3,2},{4,5},{5,4},{6,7},{7,6},{8,9},{9,8},{10,11... | collective-permute-start | bytes 1228808 | tf_op jit(solution)/shard_map/ppermute | solution.py:45
  69.4 47.7 %copy-start.3 = (bf16[8,40,640]{2,1,0:T(8,128)(2,1)}, bf16[8,40,640]{2,1,0:T(8,128)(2,1)S(1)}, u32[]{:S(2)}) copy-start(bf16[8,40,640]{2,1,0:T(8,128)(2,1)S(1)} %collective-permute-done.26.refs_2_) | copy-start | bytes 1228804
  69.4 28.1 %collective-permute-start.30 = (bf16[8,40,640]{2,1,0:T(8,128)(2,1)S(1)}, bf16[8,40,640]{2,1,0:T(8,128)(2,1)S(1)}, u32[]{:S(2)}, u32[]{:S(2)}) collective-permute-start(bf16[8,40,640]{2,1,0:T(8,128)(2,1)S(1)} %collective-permute-done.26.refs_2_), channel_id=1, source_target_pairs={{0,1},{1,0},{2,3},{3,2},{4,5},{5,4},{6,7},{7,6},{8,9},{9,8},{10,11... | collective-permute-start | bytes 1228808 | tf_op jit(solution)/shard_map/ppermute | solution.py:45
  75.6 41.5 %copy-start.4 = (bf16[8,40,640]{2,1,0:T(8,128)(2,1)}, bf16[8,40,640]{2,1,0:T(8,128)(2,1)S(1)}, u32[]{:S(2)}) copy-start(bf16[8,40,640]{2,1,0:T(8,128)(2,1)S(1)} %collective-permute-done.27.refs_3_) | copy-start | bytes 1228804
  75.6 16.6 %collective-permute-start.1 = (bf16[128,1280]{1,0:T(8,128)(2,1)}, bf16[128,1280]{1,0:T(8,128)(2,1)S(1)}, u32[]{:S(2)}, u32[]{:S(2)}) collective-permute-start(bf16[128,1280]{1,0:T(8,128)(2,1)} %get-tuple-element.9.refs_0_), channel_id=1, source_target_pairs={{2,0},{3,1},{4,2},{5,3},{6,4},{7,5},{0,6},{1,7},{10,8},{11,9},{12,... | collective-permute-start | bytes 983048 | tf_op jit(solution)/shard_map/ppermute | solution.py:41
  78.4 38.8 %copy-start.5 = (bf16[8,40,640]{2,1,0:T(8,128)(2,1)}, bf16[8,40,640]{2,1,0:T(8,128)(2,1)S(1)}, u32[]{:S(2)}) copy-start(bf16[8,40,640]{2,1,0:T(8,128)(2,1)S(1)} %collective-permute-done.28.refs_4_) | copy-start | bytes 1228804
  78.4 17.7 %collective-permute-start.3 = (bf16[128,1280]{1,0:T(8,128)(2,1)}, bf16[128,1280]{1,0:T(8,128)(2,1)}, u32[]{:S(2)}, u32[]{:S(2)}) collective-permute-start(bf16[128,1280]{1,0:T(8,128)(2,1)} %get-tuple-element.9.refs_0_), channel_id=1, source_target_pairs={{4,0},{5,1},{6,2},{7,3},{0,4},{1,5},{2,6},{3,7},{12,8},{13,9},{14,... | collective-permute-start | bytes 983048 | tf_op jit(solution)/shard_map/ppermute | solution.py:41
  78.7 18.1 %collective-permute-start.5 = (bf16[128,1280]{1,0:T(8,128)(2,1)}, bf16[128,1280]{1,0:T(8,128)(2,1)}, u32[]{:S(2)}, u32[]{:S(2)}) collective-permute-start(bf16[128,1280]{1,0:T(8,128)(2,1)} %get-tuple-element.9.refs_0_), channel_id=1, source_target_pairs={{6,0},{7,1},{0,2},{1,3},{2,4},{3,5},{4,6},{5,7},{14,8},{15,9},{8,1... | collective-permute-start | bytes 983048 | tf_op jit(solution)/shard_map/ppermute | solution.py:41
  92.3 28.8 %copy-start.8 = (bf16[128,1280]{1,0:T(8,128)(2,1)}, bf16[128,1280]{1,0:T(8,128)(2,1)S(1)}, u32[]{:S(2)}) copy-start(bf16[128,1280]{1,0:T(8,128)(2,1)S(1)} %collective-permute-done.1.refs_2_) | copy-start | bytes 983044
  92.3 24.9 %collective-permute-start.31 = (bf16[8,40,640]{2,1,0:T(8,128)(2,1)S(1)}, bf16[8,40,640]{2,1,0:T(8,128)(2,1)}, u32[]{:S(2)}, u32[]{:S(2)}) collective-permute-start(bf16[8,40,640]{2,1,0:T(8,128)(2,1)S(1)} %collective-permute-done.27.refs_3_), channel_id=1, source_target_pairs={{0,1},{1,0},{2,3},{3,2},{4,5},{5,4},{6,7},{7,6},{8,9},{9,8},{10,11... | collective-permute-start | bytes 1228808 | tf_op jit(solution)/shard_map/ppermute | solution.py:45
  96.1 25.0 %collective-permute-start = (bf16[128,1280]{1,0:T(8,128)(2,1)}, bf16[128,1280]{1,0:T(8,128)(2,1)S(1)}, u32[]{:S(2)}, u32[]{:S(2)}) collective-permute-start(bf16[128,1280]{1,0:T(8,128)(2,1)} %get-tuple-element.9.refs_0_), channel_id=1, source_target_pairs={{0,1},{1,0},{2,3},{3,2},{4,5},{5,4},{6,7},{7,6},{8,9},{9,8},{10,11... | collective-permute-start | bytes 983048 | tf_op jit(solution)/shard_map/ppermute | solution.py:45
  96.9 24.3 %collective-permute-start.2 = (bf16[128,1280]{1,0:T(8,128)(2,1)S(1)}, bf16[128,1280]{1,0:T(8,128)(2,1)S(1)}, u32[]{:S(2)}, u32[]{:S(2)}) collective-permute-start(bf16[128,1280]{1,0:T(8,128)(2,1)S(1)} %collective-permute-done.1.refs_2_), channel_id=1, source_target_pairs={{0,1},{1,0},{2,3},{3,2},{4,5},{5,4},{6,7},{7,6},{8,9},{9,8},{10,11... | collective-permute-start | bytes 983048 | tf_op jit(solution)/shard_map/ppermute | solution.py:45
  97.3 19.8 %copy-start.6 = (bf16[8,40,640]{2,1,0:T(8,128)(2,1)}, bf16[8,40,640]{2,1,0:T(8,128)(2,1)S(1)}, u32[]{:S(2)}) copy-start(bf16[8,40,640]{2,1,0:T(8,128)(2,1)S(1)} %collective-permute-done.29.refs_5_) | copy-start | bytes 1228804
  97.4 23.8 %collective-permute-start.4 = (bf16[128,1280]{1,0:T(8,128)(2,1)}, bf16[128,1280]{1,0:T(8,128)(2,1)S(1)}, u32[]{:S(2)}, u32[]{:S(2)}) collective-permute-start(bf16[128,1280]{1,0:T(8,128)(2,1)} %collective-permute-done.3.refs_4_), channel_id=1, source_target_pairs={{0,1},{1,0},{2,3},{3,2},{4,5},{5,4},{6,7},{7,6},{8,9},{9,8},{10,11... | collective-permute-start | bytes 983048 | tf_op jit(solution)/shard_map/ppermute | solution.py:45
  97.4 19.7 %copy-start.7 = (bf16[8,40,640]{2,1,0:T(8,128)(2,1)}, bf16[8,40,640]{2,1,0:T(8,128)(2,1)S(1)}, u32[]{:S(2)}) copy-start(bf16[8,40,640]{2,1,0:T(8,128)(2,1)S(1)} %collective-permute-done.30.refs_6_) | copy-start | bytes 1228804
  97.5 23.7 %collective-permute-start.6 = (bf16[128,1280]{1,0:T(8,128)(2,1)}, bf16[128,1280]{1,0:T(8,128)(2,1)S(1)}, u32[]{:S(2)}, u32[]{:S(2)}) collective-permute-start(bf16[128,1280]{1,0:T(8,128)(2,1)} %collective-permute-done.5.refs_6_), channel_id=1, source_target_pairs={{0,1},{1,0},{2,3},{3,2},{4,5},{5,4},{6,7},{7,6},{8,9},{9,8},{10,11... | collective-permute-start | bytes 983048 | tf_op jit(solution)/shard_map/ppermute | solution.py:45
  121.1 0.7 copy-start.9
  121.1 0.8 copy-start.10
  121.1 0.9 copy-start.11
  121.2 1.0 copy-start.12
  131.0 1.7 %collective-permute-start.17 = (bf16[4,128,160]{2,1,0:T(8,128)(2,1)}, bf16[4,128,160]{2,1,0:T(8,128)(2,1)S(1)}, u32[]{:S(2)}, u32[]{:S(2)}) collective-permute-start(bf16[4,128,160]{2,1,0:T(8,128)(2,1)} %get-tuple-element.11), channel_id=1, source_target_pairs={{0,1},{1,0},{2,3},{3,2},{4,5},{5,4},{6,7},{7,6},{8,9},{9,8},{10,11... | collective-permute-start | bytes 491528 | tf_op jit(solution)/shard_map/ppermute | solution.py:45
  132.8 8.0 %collective-permute-start.18 = (bf16[2,128,160]{2,1,0:T(8,128)(2,1)S(1)}, bf16[2,128,160]{2,1,0:T(8,128)(2,1)S(1)}, u32[]{:S(2)}, u32[]{:S(2)}) collective-permute-start(bf16[2,128,160]{2,1,0:T(8,128)(2,1)S(1)} %pad_maximum_fusion.3), channel_id=1, source_target_pairs={{2,0},{3,1},{4,2},{5,3},{6,4},{7,5},{0,6},{1,7},{10,8},{11,9},{12,... | collective-permute-start | bytes 245768 | tf_op jit(solution)/shard_map/ppermute | solution.py:41
  135.5 6.1 %collective-permute-start.19 = (bf16[2,128,160]{2,1,0:T(8,128)(2,1)S(1)}, bf16[2,128,160]{2,1,0:T(8,128)(2,1)S(1)}, u32[]{:S(2)}, u32[]{:S(2)}) collective-permute-start(bf16[2,128,160]{2,1,0:T(8,128)(2,1)S(1)} %pad_maximum_fusion.4), channel_id=1, source_target_pairs={{4,0},{5,1},{6,2},{7,3},{0,4},{1,5},{2,6},{3,7},{12,8},{13,9},{14,... | collective-permute-start | bytes 245768 | tf_op jit(solution)/shard_map/ppermute | solution.py:41
  135.7 9.3 %collective-permute-start.20 = (bf16[2,128,160]{2,1,0:T(8,128)(2,1)S(1)}, bf16[2,128,160]{2,1,0:T(8,128)(2,1)S(1)}, u32[]{:S(2)}, u32[]{:S(2)}) collective-permute-start(bf16[2,128,160]{2,1,0:T(8,128)(2,1)S(1)} %pad_maximum_fusion.5), channel_id=1, source_target_pairs={{6,0},{7,1},{0,2},{1,3},{2,4},{3,5},{4,6},{5,7},{14,8},{15,9},{8,1... | collective-permute-start | bytes 245768 | tf_op jit(solution)/shard_map/ppermute | solution.py:41
  140.8 4.2 %copy-start.18 = (bf16[2,128,160]{2,1,0:T(8,128)(2,1)}, bf16[2,128,160]{2,1,0:T(8,128)(2,1)S(1)}, u32[]{:S(2)}) copy-start(bf16[2,128,160]{2,1,0:T(8,128)(2,1)S(1)} %collective-permute-done.18.a1) | copy-start | bytes 245764
  141.7 3.4 %copy-start.19 = (bf16[2,128,160]{2,1,0:T(8,128)(2,1)}, bf16[2,128,160]{2,1,0:T(8,128)(2,1)S(1)}, u32[]{:S(2)}) copy-start(bf16[2,128,160]{2,1,0:T(8,128)(2,1)S(1)} %collective-permute-done.19.a2) | copy-start | bytes 245764
  145.0 0.7 copy-start.20

commit v2 on v1

v2 whole, which is shorter than its diff:
```python
import functools

import jax
import jax.numpy as jnp
import numpy as np
from jax import lax
from jax.experimental import pallas as pl
from jax.experimental.pallas import tpu as pltpu
from jax.sharding import PartitionSpec as P

HEADS = 16
HDIM = 80
D = 1280
OWN = 2 * HDIM
WIDE = 768
BF16, F32 = jnp.bfloat16, jnp.float32

VM = pl.BlockSpec(memory_space=pltpu.VMEM)
SM = pl.BlockSpec(memory_space=pltpu.SMEM)


def params(mib):
    return pltpu.CompilerParams(vmem_limit_bytes=mib * 1024 * 1024)


def after(value, *earlier):
    return lax.optimization_barrier((value, *earlier))[0]


def seq_shift(dy):
    return [((i + 2 * dy) % 8, i) for i in range(8)]


SWAP = [(i, i ^ 1) for i in range(8)]


def dp_shift(dx, dz):
    return [
        (((x + dx) % 4) * 8 + (z + dz) % 8, x * 8 + z) for x in range(4) for z in range(8)
    ]


def from_seq(value, dy):
    return lax.ppermute(value, "seq", seq_shift(dy))


def swap(value):
    return lax.ppermute(value, "seq", SWAP)


def from_dp(value, dx, dz):
    return lax.ppermute(value, "dp", dp_shift(dx, dz))


def embed_kernel(px, pw, gain, bias, emb_out, norm_out):
    emb = jnp.dot(px[...], pw[...], preferred_element_type=F32).astype(BF16)
    emb_out[...] = emb
    v = emb.astype(F32)
    center = v - jnp.mean(v, axis=-1, keepdims=True)
    var = jnp.mean(center * center, axis=-1, keepdims=True)
    scaled = center * lax.rsqrt(var + 1e-06) * gain[...][None]
    norm_out[...] = (scaled + bias[...][None]).astype(BF16)


def lay_kernel(place, *refs):
    blocks, out = refs[:8], refs[8]
    col = lax.broadcasted_iota(jnp.int32, (3 * OWN, WIDE), 0)
    lane = lax.broadcasted_iota(jnp.int32, (3 * OWN, WIDE), 1)
    piece = sum((col >= HDIM * k).astype(jnp.int32) for k in range(1, 5))
    high = ((col - HDIM * piece >= HDIM // 2) & (col < 4 * HDIM)).astype(jnp.int32)
    pick = (lane == col + 48 * piece + 24 * high).astype(F32).astype(BF16)
    x, z = place[0], place[1]
    for dz in range(8):
        wide = jnp.dot(blocks[dz][...], pick, preferred_element_type=F32).astype(BF16)
        for dx in range(4):
            at = lax.rem(x + dx, 4) * 8 + lax.rem(z + dz, 8)
            out[at] = wide[dx * 40 : dx * 40 + 40]


def out_lay_kernel(place, *refs):
    out = refs[8]
    x, z, c = place[0], place[1], place[3]
    for half in range(2):
        first = pl.multiple_of(jnp.bitwise_xor(c, half) * 640, 128)
        for dx in range(4):
            for dz in range(8):
                at = lax.rem(x + dx, 4) * 8 + lax.rem(z + dz, 8)
                out[at, :, pl.ds(first, 640)] = refs[half * 4 + dx][dz]


def tables_kernel(place, inverse, cos_out, sin_out):
    y, c = place[2], place[3]
    o0, o1, o2 = place[4], place[5], place[6]
    lane = lax.broadcasted_iota(jnp.int32, (128, 128), 1)
    sub = lax.broadcasted_iota(jnp.int32, (128, 128), 0)
    low = jnp.bitwise_and(lane, 63)
    angle = jnp.bitwise_and(sub, 63).astype(F32) * inverse[...]
    mine = (low < HDIM // 4) == (sub < 64)
    both = jnp.concatenate(
        [
            jnp.where(mine, jnp.cos(angle), 0.0),
            jnp.where(mine, jnp.sin(angle) * jnp.where(lane < 64, -1.0, 1.0), 0.0),
        ],
        axis=1,
    )
    parts = []
    for _ in range(3):
        parts.append(both.astype(BF16))
        both = both - parts[-1].astype(F32)
    for r in range(8):
        first = (lax.rem(y + r // 2, 4) * 2 + jnp.bitwise_xor(c, r % 2)) * 128
        pos = first + sub
        second, third = pos >= o1, pos >= o2
        start = jnp.where(third, o2, jnp.where(second, o1, o0))
        across = jnp.where(third, place[9], jnp.where(second, place[8], place[7]))
        within = pos - start
        row = ((within.astype(F32) + 0.5) / across.astype(F32)).astype(jnp.int32)
        column = within - row * across
        pick = (jnp.where(lane < 64, row, column + 64) == lane).astype(F32).astype(BF16)
        total = sum(jnp.dot(pick, part, preferred_element_type=F32) for part in parts)
        cos_out[r] = total[:, :128]
        sin_out[r] = total[:, 128:]


def attend_kernel(place, *refs):
    shards = refs[:8]
    w, b, cosine, sine = refs[8:12]
    outs = refs[12:16]
    qs, ks, vs = refs[16:19]
    scale = float(HDIM**-0.5 * np.log2(np.e))
    y, c, o1, o2 = place[2], place[3], place[5], place[6]

    def first_of(r):
        return (lax.rem(y + r // 2, 4) * 2 + jnp.bitwise_xor(c, r % 2)) * 128

    def image(p):
        return (p >= o1).astype(jnp.int32) + (p >= o2).astype(jnp.int32)

    for blk in range(4):
        rows = pl.ds(blk * 256, 256)
        x = jnp.concatenate([shards[2 * blk][...], shards[2 * blk + 1][...]], axis=0)
        proj = jnp.dot(x, w[...], preferred_element_type=F32) + b[...][None]
        cs = cosine[2 * blk : 2 * blk + 2].reshape(256, 128)
        sn = sine[2 * blk : 2 * blk + 2].reshape(256, 128)
        for h in range(2):
            for first, dst in ((0, qs), (256, ks)):
                t = proj[:, first + h * 128 : first + h * 128 + 128]
                dst[h, rows, :] = (t * cs + pltpu.roll(t, 64, 1) * sn).astype(BF16)
        vs[rows, :] = proj[:, 512:].astype(BF16)
    lane = lax.broadcasted_iota(jnp.int32, (1, 128), 1)
    key_image = jnp.concatenate([image(lane + first_of(r)) for r in range(8)], axis=1)
    row = lax.broadcasted_iota(jnp.int32, (128, 1), 0)
    wide_lane = lax.broadcasted_iota(jnp.int32, (256, 256), 1)
    for blk in range(4):
        rows = pl.ds(blk * 256, 256)
        query_image = jnp.concatenate(
            [image(row + first_of(2 * blk)), image(row + first_of(2 * blk + 1))], axis=0
        )
        allowed = query_image == key_image
        done = []
        for h in range(2):
            s = lax.dot_general(
                qs[h, rows, :], ks[h], (((1,), (1,)), ((), ())), preferred_element_type=F32
            )
            s = jnp.where(allowed, s, -1e30)
            m = jnp.max(s, axis=1, keepdims=True)
            p = jnp.exp2((s - m) * scale).astype(BF16)
            o = jnp.dot(p, vs[...], preferred_element_type=F32)
            done.append(o / o[:, OWN : OWN + 1])
        att = jnp.where(wide_lane < HDIM, done[0], done[1])[:, :OWN]
        outs[blk][...] = jnp.concatenate([att[:128], att[128:]], axis=1).astype(BF16)


def out_kernel(place, *refs):
    here, there = refs[:4], refs[4:8]
    w, emb, bias, out = refs[8:]
    y, c = place[2], place[3]
    acc = emb[...].astype(F32) + bias[...][None]
    for dy in range(4):
        chip = lax.rem(y + dy, 4) * 2
        acc += jnp.dot(here[dy][:, :OWN], w[chip + c], preferred_element_type=F32)
        acc += jnp.dot(there[dy][:, OWN:], w[chip + 1 - c], preferred_element_type=F32)
    out[...] = acc.astype(BF16)


def halves_apart(piece):
    zero = jnp.zeros(piece.shape[:-1] + (24,), piece.dtype)
    return jnp.concatenate([piece[..., :40], zero, piece[..., 40:], zero], axis=-1)


INVERSE = np.zeros((1, 128), np.float32)
for _l in range(128):
    if _l % 64 < 40:
        INVERSE[0, _l] = 1.0 / 10000.0 ** ((_l % 64 % 20) * 2.0 / 40.0)


def per_device(
    pixels,
    patch_weight,
    ln_gain,
    ln_bias,
    qkv_weight,
    qkv_bias,
    out_weight,
    out_bias,
    offsets,
    widths,
):
    dp, seq = lax.axis_index("dp"), lax.axis_index("seq")
    x, z, y, c = dp // 8, dp % 8, seq // 2, seq % 2
    rows = jax.ShapeDtypeStruct((128, D), BF16)
    place = jnp.concatenate(
        [jnp.stack([x, z, y, c]).astype(jnp.int32), offsets[0], widths[0], jnp.zeros((6,), jnp.int32)]
    )

    blocks = pixels.reshape(32, 4, -1)
    local_pixels = lax.all_to_all(blocks, "dp", 0, 0, tiled=True).reshape(128, -1)

    slices = [lax.dynamic_slice_in_dim(qkv_weight, k * D + seq * OWN, OWN, 1) for k in range(3)]
    mine = after(jnp.concatenate(slices, axis=1), blocks)
    xs = [mine] + [from_dp(mine, d, 0) for d in (1, 2, 3)]
    z0 = jnp.concatenate(xs, axis=0)
    z1, z7 = from_dp(z0, 0, 1), from_dp(z0, 0, 7)
    z2, z6 = from_dp(z1, 0, 1), from_dp(z7, 0, 7)

    half = after(lax.dynamic_slice_in_dim(out_weight, c * 640, 640, 1)[None], z0)
    h1, h7 = from_dp(half, 0, 1), from_dp(half, 0, 7)

    cosine, sine = pl.pallas_call(
        tables_kernel,
        out_shape=(jax.ShapeDtypeStruct((8, 128, 128), F32),) * 2,
        in_specs=[SM, VM],
        out_specs=(VM, VM),
        compiler_params=params(6),
        name="tables",
    )(place, jnp.asarray(INVERSE))

    embedded, normed = pl.pallas_call(
        embed_kernel,
        out_shape=(rows, rows),
        in_specs=[VM] * 4,
        out_specs=(VM, VM),
        compiler_params=params(12),
        name="embed",
    )(local_pixels, patch_weight, ln_gain, ln_bias)

    same = [normed] + [from_seq(normed, d) for d in (1, 2, 3)]
    crossed = [swap(v) for v in same]
    shards = [v for pair in zip(same, crossed) for v in pair]

    z2, z6 = after(z2, normed), after(z6, normed)
    z3, z5 = from_dp(z2, 0, 1), from_dp(z6, 0, 7)
    z4 = from_dp(z3, 0, 1)
    laid = pl.pallas_call(
        lay_kernel,
        out_shape=jax.ShapeDtypeStruct((32, 40, WIDE), BF16),
        in_specs=[SM] + [VM] * 8,
        out_specs=VM,
        compiler_params=params(12),
        name="lay_qkv",
    )(place, z0, z1, z2, z3, z4, z5, z6, z7).reshape(D, WIDE)

    own_bias = [lax.dynamic_slice_in_dim(qkv_bias, k * D + seq * OWN, OWN, 0) for k in range(3)]
    ones = jnp.ones((1,), F32)
    laid_bias = jnp.concatenate(
        [halves_apart(own_bias[k][h * HDIM : (h + 1) * HDIM]) for k in range(2) for h in range(2)]
        + [own_bias[2], ones, jnp.zeros((95,), F32)]
    )

    half, h1, h7 = (after(v, normed) for v in (half, h1, h7))
    h234 = from_dp(jnp.concatenate([h7, half, h1]), 0, 3)
    h56 = from_dp(jnp.concatenate([half, h1]), 0, 5)
    column0 = jnp.concatenate([half, h1, h234, h56, h7])
    columns = [column0] + [from_dp(column0, d, 0) for d in (1, 2, 3)]

    parts = pl.pallas_call(
        attend_kernel,
        out_shape=(jax.ShapeDtypeStruct((128, 2 * OWN), BF16),) * 4,
        in_specs=[SM] + [VM] * 12,
        out_specs=(VM,) * 4,
        scratch_shapes=[
            pltpu.VMEM((2, 1024, 128), BF16),
            pltpu.VMEM((2, 1024, 128), BF16),
            pltpu.VMEM((1024, 256), BF16),
        ],
        compiler_params=params(28),
        name="attend",
    )(place, *shards, laid, laid_bias, cosine, sine)

    got = [parts[0]] + [from_seq(parts[(4 - d) % 4], d) for d in (1, 2, 3)]
    got_other = [swap(v) for v in got]

    others = [swap(after(v, parts[0])) for v in columns]
    out_laid = pl.pallas_call(
        out_lay_kernel,
        out_shape=jax.ShapeDtypeStruct((32, 40, D), BF16),
        in_specs=[SM] + [VM] * 8,
        out_specs=VM,
        compiler_params=params(12),
        name="lay_out",
    )(place, *columns, *others).reshape(8, OWN, D)

    return pl.pallas_call(
        out_kernel,
        out_shape=rows,
        in_specs=[SM] + [VM] * 11,
        out_specs=VM,
        compiler_params=params(12),
        name="project",
    )(place, *got, *got_other, out_laid, embedded, out_bias)


def solution(mesh):
    in_specs = (
        P(("dp", "seq"), None),
        P(),
        P(),
        P(),
        P("dp", None),
        P(),
        P("dp", None),
        P(),
        P("dp", None),
        P("dp", None),
    )
    out_specs = P(("dp", "seq"), None)
    return jax.shard_map(
        per_device, mesh=mesh, in_specs=in_specs, out_specs=out_specs, check_vma=False
    )
```

time: 150 us -> 112 us (0.75)
  other arithmetic: 21.6 us -> 1.76 us
  waiting for transfers between devices: 36.8 us -> 24.9 us
  Pallas kernels: 24 us -> 15.5 us
  starting transfers between devices: 51 us -> 56.1 us
  local copies, waits for them, and re-layouts: 15.8 us -> 11.9 us
    mul x1 -> x0, other arithmetic: 15.3 us -> none  [rotation_tables(): return (jnp.cos(angle), jnp.sin(angle) * sign)]
    ppermute x6, waiting for transfers between devices: 20.3 us -> 9.42 us  [from_seq(): return lax.ppermute(value, 'seq', seq_shift(dy))]
    all_to_all x1, starting transfers between devices: 4.49 us -> 10.5 us  [per_device(): lax.all_to_all(blocks, 'dp', 0, 0, tiled=True).reshape(128, -1)]
    ppermute x17, starting transfers between devices: 28.5 us -> 23.7 us  [from_dp(): return lax.ppermute(value, 'dp', dp_shift(dx, dz))]
    slice x4 -> x0, local copies, waits for them, and re-layouts: 3.75 us -> none  [the longest x1 1.42 us: rotation_tables(): widths[2]]
    another operation x7 -> x0, other arithmetic: 3.72 us -> none  [the longest x1 1.8 us: per_device(): place = jnp.stack([y, c, starts[1], starts[2]]).astype(jnp.int32)]
    unnamed x53 -> x44, local copies, waits for them, and re-layouts: 3.74 us -> 7.17 us
    ppermute x9 -> x12, starting transfers between devices: 10.9 us -> 14.1 us  [swap(): return lax.ppermute(value, 'seq', SWAP)]
  transfers between devices with their start and end apart: 33 -> 36, of which waited for: 9 -> 8; matrix products, arithmetic and copies ran while one was open for 22% -> 5% of each run, Pallas kernels for 8% -> 12%
where the time goes in v2:
time: 112 us; the launch traced here: 111 us
  starting transfers between devices  56.1 us (50%)
  waiting for transfers between devices  24.9 us (22%)
  Pallas kernels  15.5 us (14%)
  local copies, waits for them, and re-layouts  11.9 us (11%)
  other arithmetic  1.76 us (2%)
    ppermute x17, starting transfers between devices, from_dp(): return lax.ppermute(value, 'dp', dp_shift(dx, dz))  23.7 us
    ppermute x17, waiting for transfers between devices, from_dp(): return lax.ppermute(value, 'dp', dp_shift(dx, dz))  15.2 us
    ppermute x12, starting transfers between devices, swap(): return lax.ppermute(value, 'seq', SWAP)  14.1 us
    all_to_all x1, starting transfers between devices, per_device(): lax.all_to_all(blocks, 'dp', 0, 0, tiled=True).reshape(128, -1)  10.5 us
    ppermute x6, waiting for transfers between devices, from_seq(): return lax.ppermute(value, 'seq', seq_shift(dy))  9.42 us
    ppermute x6, starting transfers between devices, from_seq(): return lax.ppermute(value, 'seq', seq_shift(dy))  7.93 us
    unnamed x44, local copies, waits for them, and re-layouts  7.17 us
    pallas_call x1, Pallas kernels, per_device(): pl.pallas_call(attend_kernel, out_shape=(jax.ShapeDtypeStruct((128, 2 * O...  7.11 us
  transfers between devices with their start and end apart: 36, of which 8 were waited for; matrix products, arithmetic and copies ran while one was open for 5% of the time, Pallas kernels for 12%

profile of v2, /device:TPU:1, one launch (start us, length us, event | category | flops | bytes accessed | tf_op | source)
XLA Modules:
  0.0 110.6 jit_solution(17782527248402566930)
XLA Ops:
  0.0 1.3 %copy.13 = bf16[128,1176]{1,0:T(8,128)(2,1)S(1)} copy(bf16[128,1176]{0,1:T(8,128)(2,1)} %param.11) | data formatting | bytes 602112 | tf_op args[0]
  1.3 0.8 reshape.12
  2.1 0.9 constant_dynamic-slice_fusion.2
  3.0 0.1 pad_maximum_fusion.2
  3.1 3.4 %collective-permute-start.7 = (bf16[40,480]{1,0:T(8,128)(2,1)S(1)}, bf16[40,480]{1,0:T(8,128)(2,1)S(1)}, u32[]{:S(2)}, u32[]{:S(2)}) collective-permute-start(bf16[40,480]{1,0:T(8,128)(2,1)S(1)} %pad_maximum_fusion.2), channel_id=1, source_target_pairs={{64,0},{72,8},{80,16},{88,24},{96,32},{104,40},{112,48},{120,56},{... | collective-permute-start | bytes 115208 | tf_op jit(solution)/shard_map/ppermute | solution.py:52
  6.5 0.5 collective-permute-start.8
  7.0 0.6 collective-permute-start.9
  7.6 10.5 %all-to-all-start = ((bf16[32,4,1176]{2,1,0:T(4,128)(2,1)}), bf16[32,4,1176]{2,1,0:T(4,128)(2,1)}, u32[]{:S(2)}, u32[]{:S(2)}) async-start(bf16[32,4,1176]{2,1,0:T(4,128)(2,1)} %reshape.12), calls=%async_computation | async-start | bytes 655360 | tf_op jit(solution)/shard_map/all_to_all | solution.py:217
  18.2 1.2 %collective-permute-start.14 = (bf16[160,480]{1,0:T(8,128)(2,1)S(1)}, bf16[160,480]{1,0:T(8,128)(2,1)}, u32[]{:S(2)}, u32[]{:S(2)}) collective-permute-start(bf16[160,480]{1,0:T(8,128)(2,1)S(1)} %constant_dynamic-update-slice_fusion.refs_0_), channel_id=1, source_target_pairs={{56,0},{0,8},{8,16},{16,24},{24,32},{32,40},{40,48},{48,56},{120,6... | collective-permute-start | bytes 460808 | tf_op jit(solution)/shard_map/ppermute | solution.py:52
  19.5 1.5 %collective-permute-start.10 = (bf16[160,480]{1,0:T(8,128)(2,1)S(1)}, bf16[160,480]{1,0:T(8,128)(2,1)}, u32[]{:S(2)}, u32[]{:S(2)}) collective-permute-start(bf16[160,480]{1,0:T(8,128)(2,1)S(1)} %constant_dynamic-update-slice_fusion.refs_0_), channel_id=1, source_target_pairs={{8,0},{16,8},{24,16},{32,24},{40,32},{48,40},{56,48},{0,56},{72,64... | collective-permute-start | bytes 460808 | tf_op jit(solution)/shard_map/ppermute | solution.py:52
  21.0 0.6 copy-done.4
  21.7 1.2 %collective-permute-start.24 = (bf16[1,40,640]{2,1,0:T(8,128)(2,1)S(1)}, bf16[1,40,640]{2,1,0:T(8,128)(2,1)}, u32[]{:S(2)}, u32[]{:S(2)}) collective-permute-start(bf16[1,40,640]{2,1,0:T(8,128)(2,1)S(1)} %dynamic-slice_bitcast_fusion), channel_id=1, source_target_pairs={{8,0},{16,8},{24,16},{32,24},{40,32},{48,40},{56,48},{0,56},{72,64... | collective-permute-start | bytes 153608 | tf_op jit(solution)/shard_map/ppermute | solution.py:52
  22.9 0.3 collective-permute-start.25
  23.2 7.4 %collective-permute-done.14.refs_7_ = bf16[160,480]{1,0:T(8,128)(2,1)} collective-permute-done((bf16[160,480]{1,0:T(8,128)(2,1)S(1)}, bf16[160,480]{1,0:T(8,128)(2,1)}, u32[]{:S(2)}, u32[]{:S(2)}) %collective-permute-start.14) | collective-permute-done | bytes 153632 | tf_op jit(solution)/shard_map/ppermute | solution.py:52
  30.6 2.7 %collective-permute-start.11 = (bf16[160,480]{1,0:T(8,128)(2,1)}, bf16[160,480]{1,0:T(8,128)(2,1)}, u32[]{:S(2)}, u32[]{:S(2)}) collective-permute-start(bf16[160,480]{1,0:T(8,128)(2,1)} %collective-permute-done.10.refs_1_), channel_id=1, source_target_pairs={{8,0},{16,8},{24,16},{32,24},{40,32},{48,40},{56,48},{0,56},{72,64... | collective-permute-start | bytes 460808 | tf_op jit(solution)/shard_map/ppermute | solution.py:52
  33.3 1.1 reshape.13.px
  34.4 1.6 %embed.1 = (bf16[128,1280]{1,0:T(8,128)(2,1)S(1)}, bf16[128,1280]{1,0:T(8,128)(2,1)}) custom-call(bf16[128,1176]{1,0:T(8,128)(2,1)S(1)} %reshape.13.px, bf16[1176,1280]{1,0:T(8,128)(2,1)S(1)} %copy-done.1, f32[1280]{0:T(1024)S(1)} %copy-done.12, f32[1280]{0:T(1024)S(1)} %copy-done.13), custom_call_target="tpu_custom_call" | custom-call | tf_op jit(solution)/shard_map/embed/pallas_call | solution.py:238
  36.1 2.7 %collective-permute-start.1 = (bf16[128,1280]{1,0:T(8,128)(2,1)}, bf16[128,1280]{1,0:T(8,128)(2,1)S(1)}, u32[]{:S(2)}, u32[]{:S(2)}) collective-permute-start(bf16[128,1280]{1,0:T(8,128)(2,1)} %get-tuple-element.24.refs_0_), channel_id=1, source_target_pairs={{2,0},{3,1},{4,2},{5,3},{6,4},{7,5},{0,6},{1,7},{10,8},{11,9},{12,... | collective-permute-start | bytes 983048 | tf_op jit(solution)/shard_map/ppermute | solution.py:44
  38.8 0.9 pad_maximum_fusion
  39.6 0.8 pad_maximum_fusion.1
  40.5 2.4 %collective-permute-start.26 = (bf16[3,40,640]{2,1,0:T(8,128)(2,1)S(1)}, bf16[3,40,640]{2,1,0:T(8,128)(2,1)S(1)}, u32[]{:S(2)}, u32[]{:S(2)}) collective-permute-start(bf16[3,40,640]{2,1,0:T(8,128)(2,1)S(1)} %pad_maximum_fusion), channel_id=1, source_target_pairs={{24,0},{32,8},{40,16},{48,24},{56,32},{0,40},{8,48},{16,56},{88,64... | collective-permute-start | bytes 460808 | tf_op jit(solution)/shard_map/ppermute | solution.py:52
  42.8 1.9 %collective-permute-start.27 = (bf16[2,40,640]{2,1,0:T(8,128)(2,1)S(1)}, bf16[2,40,640]{2,1,0:T(8,128)(2,1)S(1)}, u32[]{:S(2)}, u32[]{:S(2)}) collective-permute-start(bf16[2,40,640]{2,1,0:T(8,128)(2,1)S(1)} %pad_maximum_fusion.1), channel_id=1, source_target_pairs={{40,0},{48,8},{56,16},{0,24},{8,32},{16,40},{24,48},{32,56},{104,6... | collective-permute-start | bytes 307208 | tf_op jit(solution)/shard_map/ppermute | solution.py:52
  44.7 1.8 %collective-permute-start.12 = (bf16[160,480]{1,0:T(8,128)(2,1)}, bf16[160,480]{1,0:T(8,128)(2,1)S(1)}, u32[]{:S(2)}, u32[]{:S(2)}) collective-permute-start(bf16[160,480]{1,0:T(8,128)(2,1)} %collective-permute-done.11.refs_2_), channel_id=1, source_target_pairs={{8,0},{16,8},{24,16},{32,24},{40,32},{48,40},{56,48},{0,56},{72,64... | collective-permute-start | bytes 460808 | tf_op jit(solution)/shard_map/ppermute | solution.py:52
  46.5 0.8 constant_dynamic-update-slice_fusion.7
  47.3 2.7 %collective-permute-done.27 = bf16[2,40,640]{2,1,0:T(8,128)(2,1)S(1)} collective-permute-done((bf16[2,40,640]{2,1,0:T(8,128)(2,1)S(1)}, bf16[2,40,640]{2,1,0:T(8,128)(2,1)S(1)}, u32[]{:S(2)}, u32[]{:S(2)}) %collective-permute-start.27) | collective-permute-done | bytes 102432 | tf_op jit(solution)/shard_map/ppermute | solution.py:52
  50.0 0.3 collective-permute-start.3
  50.3 0.6 collective-permute-done.26
  50.9 0.1 collective-permute-start.5
  51.0 7.1 %collective-permute-start = (bf16[128,1280]{1,0:T(8,128)(2,1)}, bf16[128,1280]{1,0:T(8,128)(2,1)}, u32[]{:S(2)}, u32[]{:S(2)}) collective-permute-start(bf16[128,1280]{1,0:T(8,128)(2,1)} %get-tuple-element.24.refs_0_), channel_id=1, source_target_pairs={{0,1},{1,0},{2,3},{3,2},{4,5},{5,4},{6,7},{7,6},{8,9},{9,8},{10,11... | collective-permute-start | bytes 983048 | tf_op jit(solution)/shard_map/ppermute | solution.py:48
  58.2 0.1 collective-permute-start.2
  58.3 1.4 %collective-permute-start.13 = (bf16[160,480]{1,0:T(8,128)(2,1)S(1)}, bf16[160,480]{1,0:T(8,128)(2,1)S(1)}, u32[]{:S(2)}, u32[]{:S(2)}) collective-permute-start(bf16[160,480]{1,0:T(8,128)(2,1)S(1)} %collective-permute-done.12.refs_3_), channel_id=1, source_target_pairs={{8,0},{16,8},{24,16},{32,24},{40,32},{48,40},{56,48},{0,56},{72,64... | collective-permute-start | bytes 460808 | tf_op jit(solution)/shard_map/ppermute | solution.py:52
  59.7 0.8 constant_dynamic-update-slice_fusion.4.refs_0_
  60.5 4.5 %collective-permute-done.13.refs_4_ = bf16[160,480]{1,0:T(8,128)(2,1)S(1)} collective-permute-done((bf16[160,480]{1,0:T(8,128)(2,1)S(1)}, bf16[160,480]{1,0:T(8,128)(2,1)S(1)}, u32[]{:S(2)}, u32[]{:S(2)}) %collective-permute-start.13) | collective-permute-done | bytes 153632 | tf_op jit(solution)/shard_map/ppermute | solution.py:52
  65.1 0.7 copy-done.10
  65.7 1.2 %collective-permute-start.30 = (bf16[8,40,640]{2,1,0:T(8,128)(2,1)S(1)}, bf16[8,40,640]{2,1,0:T(8,128)(2,1)S(1)}, u32[]{:S(2)}, u32[]{:S(2)}) collective-permute-start(bf16[8,40,640]{2,1,0:T(8,128)(2,1)S(1)} %constant_dynamic-update-slice_fusion.4.refs_0_), channel_id=1, source_target_pairs={{192,0},{200,8},{208,16},{216,24},{224,32},{232,40},{240,48},{248,... | collective-permute-start | bytes 1228808 | tf_op jit(solution)/shard_map/ppermute | solution.py:52
  66.9 2.5 %collective-permute-start.29 = (bf16[8,40,640]{2,1,0:T(8,128)(2,1)S(1)}, bf16[8,40,640]{2,1,0:T(8,128)(2,1)S(1)}, u32[]{:S(2)}, u32[]{:S(2)}) collective-permute-start(bf16[8,40,640]{2,1,0:T(8,128)(2,1)S(1)} %constant_dynamic-update-slice_fusion.4.refs_0_), channel_id=1, source_target_pairs={{128,0},{136,8},{144,16},{152,24},{160,32},{168,40},{176,48},{184,... | collective-permute-start | bytes 1228808 | tf_op jit(solution)/shard_map/ppermute | solution.py:52
  69.4 1.1 %collective-permute-start.28 = (bf16[8,40,640]{2,1,0:T(8,128)(2,1)S(1)}, bf16[8,40,640]{2,1,0:T(8,128)(2,1)S(1)}, u32[]{:S(2)}, u32[]{:S(2)}) collective-permute-start(bf16[8,40,640]{2,1,0:T(8,128)(2,1)S(1)} %constant_dynamic-update-slice_fusion.4.refs_0_), channel_id=1, source_target_pairs={{64,0},{72,8},{80,16},{88,24},{96,32},{104,40},{112,48},{120,56},{... | collective-permute-start | bytes 1228808 | tf_op jit(solution)/shard_map/ppermute | solution.py:52
  70.6 1.4 %tables.1 = (f32[8,128,128]{2,1,0:T(8,128)S(1)}, f32[8,128,128]{2,1,0:T(8,128)S(1)}) custom-call(s32[16]{0:T(128)S(1)} %concatenate.21.place, f32[1,128]{1,0:T(1,128)S(1)} %copy-done.15), custom_call_target="tpu_custom_call" | custom-call | tf_op jit(solution)/shard_map/tables/pallas_call | solution.py:229
  72.0 1.7 %collective-permute-start.4 = (bf16[128,1280]{1,0:T(8,128)(2,1)S(1)}, bf16[128,1280]{1,0:T(8,128)(2,1)}, u32[]{:S(2)}, u32[]{:S(2)}) collective-permute-start(bf16[128,1280]{1,0:T(8,128)(2,1)S(1)} %collective-permute-done.3.refs_4_), channel_id=1, source_target_pairs={{0,1},{1,0},{2,3},{3,2},{4,5},{5,4},{6,7},{7,6},{8,9},{9,8},{10,11... | collective-permute-start | bytes 983048 | tf_op jit(solution)/shard_map/ppermute | solution.py:48
  73.8 0.1 collective-permute-start.6
  73.9 0.8 fusion
  74.8 0.1 concatenate.24.refs_9_
  74.9 0.9 copy-done.5
  75.8 0.9 copy-done.7
  76.8 0.9 copy-done.9
  77.7 0.9 copy-done.11
  78.6 2.3 %lay_qkv.1 = bf16[32,40,768]{2,1,0:T(8,128)(2,1)S(1)} custom-call(s32[16]{0:T(128)S(1)} %concatenate.21.place, bf16[160,480]{1,0:T(8,128)(2,1)S(1)} %copy-done.5, bf16[160,480]{1,0:T(8,128)(2,1)} %collective-permute-done.10.refs_1_, bf16[160,480]{1,0:T(8,128)(2,1)} %collective-permute-done.11.refs_2_, bf16[160,480]{1,0:T(8,128)(2,1)S(1)} %copy-done.9, ...), custom_call_target="tpu_custom_call" | custom-call | tf_op jit(solution)/shard_map/lay_qkv/pallas_call | solution.py:254
  81.0 7.1 %attend.1 = (bf16[128,320]{1,0:T(8,128)(2,1)S(1)}, bf16[128,320]{1,0:T(8,128)(2,1)S(1)}, bf16[128,320]{1,0:T(8,128)(2,1)S(1)}, bf16[128,320]{1,0:T(8,128)(2,1)S(1)}) custom-call(s32[16]{0:T(128)S(1)} %concatenate.21.place, bf16[128,1280]{1,0:T(8,128)(2,1)} %get-tuple-element.24.refs_0_, bf16[128,1280]{1,0:T(8,128)(2,1)} %collective-permute-done.refs_1_, ...), custom_call_target="tpu_custom_call" | custom-call | tf_op jit(solution)/shard_map/attend/pallas_call | solution.py:276
  88.1 0.5 collective-permute-start.34
  88.6 0.1 collective-permute-start.33
  88.7 0.4 collective-permute-start.32
  89.1 0.1 collective-permute-start.31
  89.2 2.0 %collective-permute-start.17 = (bf16[128,320]{1,0:T(8,128)(2,1)S(1)}, bf16[128,320]{1,0:T(8,128)(2,1)S(1)}, u32[]{:S(2)}, u32[]{:S(2)}) collective-permute-start(bf16[128,320]{1,0:T(8,128)(2,1)S(1)} %get-tuple-element.31), channel_id=1, source_target_pairs={{2,0},{3,1},{4,2},{5,3},{6,4},{7,5},{0,6},{1,7},{10,8},{11,9},{12,... | collective-permute-start | bytes 245768 | tf_op jit(solution)/shard_map/ppermute | solution.py:44
  91.2 2.3 %collective-permute-done.17.refs_1_ = bf16[128,320]{1,0:T(8,128)(2,1)S(1)} collective-permute-done((bf16[128,320]{1,0:T(8,128)(2,1)S(1)}, bf16[128,320]{1,0:T(8,128)(2,1)S(1)}, u32[]{:S(2)}, u32[]{:S(2)}) %collective-permute-start.17) | collective-permute-done | bytes 81952 | tf_op jit(solution)/shard_map/ppermute | solution.py:44
  93.5 1.4 %collective-permute-start.18 = (bf16[128,320]{1,0:T(8,128)(2,1)S(1)}, bf16[128,320]{1,0:T(8,128)(2,1)S(1)}, u32[]{:S(2)}, u32[]{:S(2)}) collective-permute-start(bf16[128,320]{1,0:T(8,128)(2,1)S(1)} %get-tuple-element.32), channel_id=1, source_target_pairs={{4,0},{5,1},{6,2},{7,3},{0,4},{1,5},{2,6},{3,7},{12,8},{13,9},{14,... | collective-permute-start | bytes 245768 | tf_op jit(solution)/shard_map/ppermute | solution.py:44
  94.9 3.5 %collective-permute-done.18.refs_2_ = bf16[128,320]{1,0:T(8,128)(2,1)S(1)} collective-permute-done((bf16[128,320]{1,0:T(8,128)(2,1)S(1)}, bf16[128,320]{1,0:T(8,128)(2,1)S(1)}, u32[]{:S(2)}, u32[]{:S(2)}) %collective-permute-start.18) | collective-permute-done | bytes 81952 | tf_op jit(solution)/shard_map/ppermute | solution.py:44
  98.5 1.3 %collective-permute-start.19 = (bf16[128,320]{1,0:T(8,128)(2,1)S(1)}, bf16[128,320]{1,0:T(8,128)(2,1)S(1)}, u32[]{:S(2)}, u32[]{:S(2)}) collective-permute-start(bf16[128,320]{1,0:T(8,128)(2,1)S(1)} %get-tuple-element.33), channel_id=1, source_target_pairs={{6,0},{7,1},{0,2},{1,3},{2,4},{3,5},{4,6},{5,7},{14,8},{15,9},{8,1... | collective-permute-start | bytes 245768 | tf_op jit(solution)/shard_map/ppermute | solution.py:44
  99.8 3.6 %collective-permute-done.19.refs_3_ = bf16[128,320]{1,0:T(8,128)(2,1)S(1)} collective-permute-done((bf16[128,320]{1,0:T(8,128)(2,1)S(1)}, bf16[128,320]{1,0:T(8,128)(2,1)S(1)}, u32[]{:S(2)}, u32[]{:S(2)}) %collective-permute-start.19) | collective-permute-done | bytes 81952 | tf_op jit(solution)/shard_map/ppermute | solution.py:44
  103.4 3.3 %collective-permute-start.20 = (bf16[128,320]{1,0:T(8,128)(2,1)S(1)}, bf16[128,320]{1,0:T(8,128)(2,1)S(1)}, u32[]{:S(2)}, u32[]{:S(2)}) collective-permute-start(bf16[128,320]{1,0:T(8,128)(2,1)S(1)} %get-tuple-element.30.refs_0_), channel_id=1, source_target_pairs={{0,1},{1,0},{2,3},{3,2},{4,5},{5,4},{6,7},{7,6},{8,9},{9,8},{10,11... | collective-permute-start | bytes 245768 | tf_op jit(solution)/shard_map/ppermute | solution.py:48
  106.6 0.5 collective-permute-start.22
  107.1 0.1 collective-permute-start.23
  107.2 0.9 lay_out.1
  108.2 0.3 collective-permute-done.23.refs_7_
  108.4 2.1 %project.1 = bf16[128,1280]{1,0:T(8,128)(2,1)} custom-call(s32[16]{0:T(128)S(1)} %concatenate.21.place, bf16[128,320]{1,0:T(8,128)(2,1)S(1)} %get-tuple-element.30.refs_0_, bf16[128,320]{1,0:T(8,128)(2,1)S(1)} %collective-permute-done.17.refs_1_, bf16[128,320]{1,0:T(8,128)(2,1)S(1)} %collective-permute-done.18.refs_2_, ...), custom_call_target="tpu_custom_call" | custom-call | tf_op jit(solution)/shard_map/project/pallas_call | solution.py:303
  (74 shorter events, 0.4 us)
Async XLA Ops:
  0.0 21.6 %copy-start = (bf16[40,1280]{1,0:T(8,128)(2,1)S(1)}, bf16[40,1280]{1,0:T(8,128)(2,1)}, u32[]{:S(2)}) copy-start(bf16[40,1280]{1,0:T(8,128)(2,1)} %param.17) | copy-start | bytes 307204
  0.0 34.4 %copy-start.1 = (bf16[1176,1280]{1,0:T(8,128)(2,1)S(1)}, bf16[1176,1280]{1,0:T(8,128)(2,1)}, u32[]{:S(2)}) copy-start(bf16[1176,1280]{1,0:T(8,128)(2,1)} %pw.1) | copy-start | bytes 9031684
  0.0 34.4 %copy-start.12 = (f32[1280]{0:T(1024)S(1)}, f32[1280]{0:T(1024)}, u32[]{:S(2)}) copy-start(f32[1280]{0:T(1024)} %gain.1) | copy-start | bytes 15364
  0.0 34.4 %copy-start.13 = (f32[1280]{0:T(1024)S(1)}, f32[1280]{0:T(1024)}, u32[]{:S(2)}) copy-start(f32[1280]{0:T(1024)} %bias.1) | copy-start | bytes 15364
  3.1 15.1 %collective-permute-start.7 = (bf16[40,480]{1,0:T(8,128)(2,1)S(1)}, bf16[40,480]{1,0:T(8,128)(2,1)S(1)}, u32[]{:S(2)}, u32[]{:S(2)}) collective-permute-start(bf16[40,480]{1,0:T(8,128)(2,1)S(1)} %pad_maximum_fusion.2), channel_id=1, source_target_pairs={{64,0},{72,8},{80,16},{88,24},{96,32},{104,40},{112,48},{120,56},{... | collective-permute-start | bytes 115208 | tf_op jit(solution)/shard_map/ppermute | solution.py:52
  6.5 11.7 %collective-permute-start.8 = (bf16[40,480]{1,0:T(8,128)(2,1)S(1)}, bf16[40,480]{1,0:T(8,128)(2,1)S(1)}, u32[]{:S(2)}, u32[]{:S(2)}) collective-permute-start(bf16[40,480]{1,0:T(8,128)(2,1)S(1)} %pad_maximum_fusion.2), channel_id=1, source_target_pairs={{128,0},{136,8},{144,16},{152,24},{160,32},{168,40},{176,48},{184,... | collective-permute-start | bytes 115208 | tf_op jit(solution)/shard_map/ppermute | solution.py:52
  7.0 11.2 %collective-permute-start.9 = (bf16[40,480]{1,0:T(8,128)(2,1)S(1)}, bf16[40,480]{1,0:T(8,128)(2,1)S(1)}, u32[]{:S(2)}, u32[]{:S(2)}) collective-permute-start(bf16[40,480]{1,0:T(8,128)(2,1)S(1)} %pad_maximum_fusion.2), channel_id=1, source_target_pairs={{192,0},{200,8},{208,16},{216,24},{224,32},{232,40},{240,48},{248,... | collective-permute-start | bytes 115208 | tf_op jit(solution)/shard_map/ppermute | solution.py:52
  7.6 25.7 %all-to-all-start = ((bf16[32,4,1176]{2,1,0:T(4,128)(2,1)}), bf16[32,4,1176]{2,1,0:T(4,128)(2,1)}, u32[]{:S(2)}, u32[]{:S(2)}) async-start(bf16[32,4,1176]{2,1,0:T(4,128)(2,1)} %reshape.12), calls=%async_computation | async-start | bytes 655360 | tf_op jit(solution)/shard_map/all_to_all | solution.py:217
  18.1 52.4 %copy-start.16 = (s32[1,3]{1,0:T(1,128)S(1)}, s32[1,3]{1,0:T(1,128)}, u32[]{:S(2)}) copy-start(s32[1,3]{1,0:T(1,128)} %param.19) | copy-start | bytes 40
  18.1 52.4 %copy-start.17 = (s32[1,3]{1,0:T(1,128)S(1)}, s32[1,3]{1,0:T(1,128)}, u32[]{:S(2)}) copy-start(s32[1,3]{1,0:T(1,128)} %param.20) | copy-start | bytes 40
  18.1 52.5 %copy-start.15 = (f32[1,128]{1,0:T(1,128)S(1)}, f32[1,128]{1,0:T(1,128)}, u32[]{:S(2)}) copy-start(f32[1,128]{1,0:T(1,128)} %constant.75.clone.inverse) | copy-start | bytes 1540
  18.2 12.4 %collective-permute-start.14 = (bf16[160,480]{1,0:T(8,128)(2,1)S(1)}, bf16[160,480]{1,0:T(8,128)(2,1)}, u32[]{:S(2)}, u32[]{:S(2)}) collective-permute-start(bf16[160,480]{1,0:T(8,128)(2,1)S(1)} %constant_dynamic-update-slice_fusion.refs_0_), channel_id=1, source_target_pairs={{56,0},{0,8},{8,16},{16,24},{24,32},{32,40},{40,48},{48,56},{120,6... | collective-permute-start | bytes 460808 | tf_op jit(solution)/shard_map/ppermute | solution.py:52
  19.5 11.2 %collective-permute-start.10 = (bf16[160,480]{1,0:T(8,128)(2,1)S(1)}, bf16[160,480]{1,0:T(8,128)(2,1)}, u32[]{:S(2)}, u32[]{:S(2)}) collective-permute-start(bf16[160,480]{1,0:T(8,128)(2,1)S(1)} %constant_dynamic-update-slice_fusion.refs_0_), channel_id=1, source_target_pairs={{8,0},{16,8},{24,16},{32,24},{40,32},{48,40},{56,48},{0,56},{72,64... | collective-permute-start | bytes 460808 | tf_op jit(solution)/shard_map/ppermute | solution.py:52
  21.0 0.6 copy-start.4
  21.7 17.1 %collective-permute-start.24 = (bf16[1,40,640]{2,1,0:T(8,128)(2,1)S(1)}, bf16[1,40,640]{2,1,0:T(8,128)(2,1)}, u32[]{:S(2)}, u32[]{:S(2)}) collective-permute-start(bf16[1,40,640]{2,1,0:T(8,128)(2,1)S(1)} %dynamic-slice_bitcast_fusion), channel_id=1, source_target_pairs={{8,0},{16,8},{24,16},{32,24},{40,32},{48,40},{56,48},{0,56},{72,64... | collective-permute-start | bytes 153608 | tf_op jit(solution)/shard_map/ppermute | solution.py:52
  22.9 15.9 %collective-permute-start.25 = (bf16[1,40,640]{2,1,0:T(8,128)(2,1)S(1)}, bf16[1,40,640]{2,1,0:T(8,128)(2,1)}, u32[]{:S(2)}, u32[]{:S(2)}) collective-permute-start(bf16[1,40,640]{2,1,0:T(8,128)(2,1)S(1)} %dynamic-slice_bitcast_fusion), channel_id=1, source_target_pairs={{56,0},{0,8},{8,16},{16,24},{24,32},{32,40},{40,48},{48,56},{120,6... | collective-permute-start | bytes 153608 | tf_op jit(solution)/shard_map/ppermute | solution.py:52
  30.6 12.2 %collective-permute-start.15 = (bf16[160,480]{1,0:T(8,128)(2,1)}, bf16[160,480]{1,0:T(8,128)(2,1)}, u32[]{:S(2)}, u32[]{:S(2)}) collective-permute-start(bf16[160,480]{1,0:T(8,128)(2,1)} %collective-permute-done.14.refs_7_), channel_id=1, source_target_pairs={{56,0},{0,8},{8,16},{16,24},{24,32},{32,40},{40,48},{48,56},{120,6... | collective-permute-start | bytes 460808 | tf_op jit(solution)/shard_map/ppermute | solution.py:52
  30.6 14.1 %collective-permute-start.11 = (bf16[160,480]{1,0:T(8,128)(2,1)}, bf16[160,480]{1,0:T(8,128)(2,1)}, u32[]{:S(2)}, u32[]{:S(2)}) collective-permute-start(bf16[160,480]{1,0:T(8,128)(2,1)} %collective-permute-done.10.refs_1_), channel_id=1, source_target_pairs={{8,0},{16,8},{24,16},{32,24},{40,32},{48,40},{56,48},{0,56},{72,64... | collective-permute-start | bytes 460808 | tf_op jit(solution)/shard_map/ppermute | solution.py:52
  36.1 33.3 %copy-start.2 = (bf16[128,1280]{1,0:T(8,128)(2,1)}, bf16[128,1280]{1,0:T(8,128)(2,1)S(1)}, u32[]{:S(2)}) copy-start(bf16[128,1280]{1,0:T(8,128)(2,1)S(1)} %get-tuple-element.42.refs_9_) | copy-start | bytes 983044
  36.1 22.1 %collective-permute-start.1 = (bf16[128,1280]{1,0:T(8,128)(2,1)}, bf16[128,1280]{1,0:T(8,128)(2,1)S(1)}, u32[]{:S(2)}, u32[]{:S(2)}) collective-permute-start(bf16[128,1280]{1,0:T(8,128)(2,1)} %get-tuple-element.24.refs_0_), channel_id=1, source_target_pairs={{2,0},{3,1},{4,2},{5,3},{6,4},{7,5},{0,6},{1,7},{10,8},{11,9},{12,... | collective-permute-start | bytes 983048 | tf_op jit(solution)/shard_map/ppermute | solution.py:44
  40.5 10.4 %collective-permute-start.26 = (bf16[3,40,640]{2,1,0:T(8,128)(2,1)S(1)}, bf16[3,40,640]{2,1,0:T(8,128)(2,1)S(1)}, u32[]{:S(2)}, u32[]{:S(2)}) collective-permute-start(bf16[3,40,640]{2,1,0:T(8,128)(2,1)S(1)} %pad_maximum_fusion), channel_id=1, source_target_pairs={{24,0},{32,8},{40,16},{48,24},{56,32},{0,40},{8,48},{16,56},{88,64... | collective-permute-start | bytes 460808 | tf_op jit(solution)/shard_map/ppermute | solution.py:52
  42.8 8.2 %collective-permute-start.16 = (bf16[160,480]{1,0:T(8,128)(2,1)}, bf16[160,480]{1,0:T(8,128)(2,1)S(1)}, u32[]{:S(2)}, u32[]{:S(2)}) collective-permute-start(bf16[160,480]{1,0:T(8,128)(2,1)} %collective-permute-done.15.refs_6_), channel_id=1, source_target_pairs={{56,0},{0,8},{8,16},{16,24},{24,32},{32,40},{40,48},{48,56},{120,6... | collective-permute-start | bytes 460808 | tf_op jit(solution)/shard_map/ppermute | solution.py:52
  42.8 7.1 %collective-permute-start.27 = (bf16[2,40,640]{2,1,0:T(8,128)(2,1)S(1)}, bf16[2,40,640]{2,1,0:T(8,128)(2,1)S(1)}, u32[]{:S(2)}, u32[]{:S(2)}) collective-permute-start(bf16[2,40,640]{2,1,0:T(8,128)(2,1)S(1)} %pad_maximum_fusion.1), channel_id=1, source_target_pairs={{40,0},{48,8},{56,16},{0,24},{8,32},{16,40},{24,48},{32,56},{104,6... | collective-permute-start | bytes 307208 | tf_op jit(solution)/shard_map/ppermute | solution.py:52
  44.7 13.6 %collective-permute-start.12 = (bf16[160,480]{1,0:T(8,128)(2,1)}, bf16[160,480]{1,0:T(8,128)(2,1)S(1)}, u32[]{:S(2)}, u32[]{:S(2)}) collective-permute-start(bf16[160,480]{1,0:T(8,128)(2,1)} %collective-permute-done.11.refs_2_), channel_id=1, source_target_pairs={{8,0},{16,8},{24,16},{32,24},{40,32},{48,40},{56,48},{0,56},{72,64... | collective-permute-start | bytes 460808 | tf_op jit(solution)/shard_map/ppermute | solution.py:52
  50.0 16.9 %collective-permute-start.3 = (bf16[128,1280]{1,0:T(8,128)(2,1)}, bf16[128,1280]{1,0:T(8,128)(2,1)S(1)}, u32[]{:S(2)}, u32[]{:S(2)}) collective-permute-start(bf16[128,1280]{1,0:T(8,128)(2,1)} %get-tuple-element.24.refs_0_), channel_id=1, source_target_pairs={{4,0},{5,1},{6,2},{7,3},{0,4},{1,5},{2,6},{3,7},{12,8},{13,9},{14,... | collective-permute-start | bytes 983048 | tf_op jit(solution)/shard_map/ppermute | solution.py:44
  50.9 18.5 %collective-permute-start.5 = (bf16[128,1280]{1,0:T(8,128)(2,1)}, bf16[128,1280]{1,0:T(8,128)(2,1)}, u32[]{:S(2)}, u32[]{:S(2)}) collective-permute-start(bf16[128,1280]{1,0:T(8,128)(2,1)} %get-tuple-element.24.refs_0_), channel_id=1, source_target_pairs={{6,0},{7,1},{0,2},{1,3},{2,4},{3,5},{4,6},{5,7},{14,8},{15,9},{8,1... | collective-permute-start | bytes 983048 | tf_op jit(solution)/shard_map/ppermute | solution.py:44
  51.0 19.5 %copy-start.6 = (bf16[160,480]{1,0:T(8,128)(2,1)}, bf16[160,480]{1,0:T(8,128)(2,1)S(1)}, u32[]{:S(2)}) copy-start(bf16[160,480]{1,0:T(8,128)(2,1)S(1)} %collective-permute-done.16.refs_5_) | copy-start | bytes 460804
  51.0 21.0 %collective-permute-start = (bf16[128,1280]{1,0:T(8,128)(2,1)}, bf16[128,1280]{1,0:T(8,128)(2,1)}, u32[]{:S(2)}, u32[]{:S(2)}) collective-permute-start(bf16[128,1280]{1,0:T(8,128)(2,1)} %get-tuple-element.24.refs_0_), channel_id=1, source_target_pairs={{0,1},{1,0},{2,3},{3,2},{4,5},{5,4},{6,7},{7,6},{8,9},{9,8},{10,11... | collective-permute-start | bytes 983048 | tf_op jit(solution)/shard_map/ppermute | solution.py:48
  58.2 15.6 %collective-permute-start.2 = (bf16[128,1280]{1,0:T(8,128)(2,1)S(1)}, bf16[128,1280]{1,0:T(8,128)(2,1)}, u32[]{:S(2)}, u32[]{:S(2)}) collective-permute-start(bf16[128,1280]{1,0:T(8,128)(2,1)S(1)} %collective-permute-done.1.refs_2_), channel_id=1, source_target_pairs={{0,1},{1,0},{2,3},{3,2},{4,5},{5,4},{6,7},{7,6},{8,9},{9,8},{10,11... | collective-permute-start | bytes 983048 | tf_op jit(solution)/shard_map/ppermute | solution.py:48
  58.3 12.2 %copy-start.8 = (bf16[160,480]{1,0:T(8,128)(2,1)}, bf16[160,480]{1,0:T(8,128)(2,1)S(1)}, u32[]{:S(2)}) copy-start(bf16[160,480]{1,0:T(8,128)(2,1)S(1)} %collective-permute-done.12.refs_3_) | copy-start | bytes 460804
  58.3 6.7 %collective-permute-start.13 = (bf16[160,480]{1,0:T(8,128)(2,1)S(1)}, bf16[160,480]{1,0:T(8,128)(2,1)S(1)}, u32[]{:S(2)}, u32[]{:S(2)}) collective-permute-start(bf16[160,480]{1,0:T(8,128)(2,1)S(1)} %collective-permute-done.12.refs_3_), channel_id=1, source_target_pairs={{8,0},{16,8},{24,16},{32,24},{40,32},{48,40},{56,48},{0,56},{72,64... | collective-permute-start | bytes 460808 | tf_op jit(solution)/shard_map/ppermute | solution.py:52
  65.1 0.7 copy-start.10
  65.7 22.4 %collective-permute-start.30 = (bf16[8,40,640]{2,1,0:T(8,128)(2,1)S(1)}, bf16[8,40,640]{2,1,0:T(8,128)(2,1)S(1)}, u32[]{:S(2)}, u32[]{:S(2)}) collective-permute-start(bf16[8,40,640]{2,1,0:T(8,128)(2,1)S(1)} %constant_dynamic-update-slice_fusion.4.refs_0_), channel_id=1, source_target_pairs={{192,0},{200,8},{208,16},{216,24},{224,32},{232,40},{240,48},{248,... | collective-permute-start | bytes 1228808 | tf_op jit(solution)/shard_map/ppermute | solution.py:52
  66.9 21.7 %collective-permute-start.29 = (bf16[8,40,640]{2,1,0:T(8,128)(2,1)S(1)}, bf16[8,40,640]{2,1,0:T(8,128)(2,1)S(1)}, u32[]{:S(2)}, u32[]{:S(2)}) collective-permute-start(bf16[8,40,640]{2,1,0:T(8,128)(2,1)S(1)} %constant_dynamic-update-slice_fusion.4.refs_0_), channel_id=1, source_target_pairs={{128,0},{136,8},{144,16},{152,24},{160,32},{168,40},{176,48},{184,... | collective-permute-start | bytes 1228808 | tf_op jit(solution)/shard_map/ppermute | solution.py:52
  69.4 19.3 %collective-permute-start.28 = (bf16[8,40,640]{2,1,0:T(8,128)(2,1)S(1)}, bf16[8,40,640]{2,1,0:T(8,128)(2,1)S(1)}, u32[]{:S(2)}, u32[]{:S(2)}) collective-permute-start(bf16[8,40,640]{2,1,0:T(8,128)(2,1)S(1)} %constant_dynamic-update-slice_fusion.4.refs_0_), channel_id=1, source_target_pairs={{64,0},{72,8},{80,16},{88,24},{96,32},{104,40},{112,48},{120,56},{... | collective-permute-start | bytes 1228808 | tf_op jit(solution)/shard_map/ppermute | solution.py:52
  72.0 8.9 %collective-permute-start.4 = (bf16[128,1280]{1,0:T(8,128)(2,1)S(1)}, bf16[128,1280]{1,0:T(8,128)(2,1)}, u32[]{:S(2)}, u32[]{:S(2)}) collective-permute-start(bf16[128,1280]{1,0:T(8,128)(2,1)S(1)} %collective-permute-done.3.refs_4_), channel_id=1, source_target_pairs={{0,1},{1,0},{2,3},{3,2},{4,5},{5,4},{6,7},{7,6},{8,9},{9,8},{10,11... | collective-permute-start | bytes 983048 | tf_op jit(solution)/shard_map/ppermute | solution.py:48
  73.8 7.2 %collective-permute-start.6 = (bf16[128,1280]{1,0:T(8,128)(2,1)}, bf16[128,1280]{1,0:T(8,128)(2,1)}, u32[]{:S(2)}, u32[]{:S(2)}) collective-permute-start(bf16[128,1280]{1,0:T(8,128)(2,1)} %collective-permute-done.5.refs_6_), channel_id=1, source_target_pairs={{0,1},{1,0},{2,3},{3,2},{4,5},{5,4},{6,7},{7,6},{8,9},{9,8},{10,11... | collective-permute-start | bytes 983048 | tf_op jit(solution)/shard_map/ppermute | solution.py:48
  74.9 0.9 copy-start.5
  75.8 0.9 copy-start.7
  76.8 0.9 copy-start.9
  77.7 0.9 copy-start.11
  88.1 18.5 %collective-permute-start.34 = (bf16[8,40,640]{2,1,0:T(8,128)(2,1)S(1)}, bf16[8,40,640]{2,1,0:T(8,128)(2,1)S(1)}, u32[]{:S(2)}, u32[]{:S(2)}) collective-permute-start(bf16[8,40,640]{2,1,0:T(8,128)(2,1)S(1)} %collective-permute-done.30.refs_3_), channel_id=1, source_target_pairs={{0,1},{1,0},{2,3},{3,2},{4,5},{5,4},{6,7},{7,6},{8,9},{9,8},{10,11... | collective-permute-start | bytes 1228808 | tf_op jit(solution)/shard_map/ppermute | solution.py:48
  88.6 18.0 %collective-permute-start.33 = (bf16[8,40,640]{2,1,0:T(8,128)(2,1)S(1)}, bf16[8,40,640]{2,1,0:T(8,128)(2,1)S(1)}, u32[]{:S(2)}, u32[]{:S(2)}) collective-permute-start(bf16[8,40,640]{2,1,0:T(8,128)(2,1)S(1)} %collective-permute-done.29.refs_2_), channel_id=1, source_target_pairs={{0,1},{1,0},{2,3},{3,2},{4,5},{5,4},{6,7},{7,6},{8,9},{9,8},{10,11... | collective-permute-start | bytes 1228808 | tf_op jit(solution)/shard_map/ppermute | solution.py:48
  88.7 18.4 %collective-permute-start.32 = (bf16[8,40,640]{2,1,0:T(8,128)(2,1)S(1)}, bf16[8,40,640]{2,1,0:T(8,128)(2,1)S(1)}, u32[]{:S(2)}, u32[]{:S(2)}) collective-permute-start(bf16[8,40,640]{2,1,0:T(8,128)(2,1)S(1)} %collective-permute-done.28.refs_1_), channel_id=1, source_target_pairs={{0,1},{1,0},{2,3},{3,2},{4,5},{5,4},{6,7},{7,6},{8,9},{9,8},{10,11... | collective-permute-start | bytes 1228808 | tf_op jit(solution)/shard_map/ppermute | solution.py:48
  89.1 18.1 %collective-permute-start.31 = (bf16[8,40,640]{2,1,0:T(8,128)(2,1)S(1)}, bf16[8,40,640]{2,1,0:T(8,128)(2,1)S(1)}, u32[]{:S(2)}, u32[]{:S(2)}) collective-permute-start(bf16[8,40,640]{2,1,0:T(8,128)(2,1)S(1)} %constant_dynamic-update-slice_fusion.4.refs_0_), channel_id=1, source_target_pairs={{0,1},{1,0},{2,3},{3,2},{4,5},{5,4},{6,7},{7,6},{8,9},{9,8},{10,11... | collective-permute-start | bytes 1228808 | tf_op jit(solution)/shard_map/ppermute | solution.py:48
  89.2 4.3 %collective-permute-start.17 = (bf16[128,320]{1,0:T(8,128)(2,1)S(1)}, bf16[128,320]{1,0:T(8,128)(2,1)S(1)}, u32[]{:S(2)}, u32[]{:S(2)}) collective-permute-start(bf16[128,320]{1,0:T(8,128)(2,1)S(1)} %get-tuple-element.31), channel_id=1, source_target_pairs={{2,0},{3,1},{4,2},{5,3},{6,4},{7,5},{0,6},{1,7},{10,8},{11,9},{12,... | collective-permute-start | bytes 245768 | tf_op jit(solution)/shard_map/ppermute | solution.py:44
  93.5 5.0 %collective-permute-start.18 = (bf16[128,320]{1,0:T(8,128)(2,1)S(1)}, bf16[128,320]{1,0:T(8,128)(2,1)S(1)}, u32[]{:S(2)}, u32[]{:S(2)}) collective-permute-start(bf16[128,320]{1,0:T(8,128)(2,1)S(1)} %get-tuple-element.32), channel_id=1, source_target_pairs={{4,0},{5,1},{6,2},{7,3},{0,4},{1,5},{2,6},{3,7},{12,8},{13,9},{14,... | collective-permute-start | bytes 245768 | tf_op jit(solution)/shard_map/ppermute | solution.py:44
  98.5 10.0 %copy-start.3 = (bf16[128,1280]{1,0:T(8,128)(2,1)S(1)}, bf16[128,1280]{1,0:T(8,128)(2,1)}, u32[]{:S(2)}) copy-start(bf16[128,1280]{1,0:T(8,128)(2,1)} %copy-done.2) | copy-start | bytes 983044
  98.5 10.0 %copy-start.14 = (f32[1280]{0:T(1024)S(1)}, f32[1280]{0:T(1024)}, u32[]{:S(2)}) copy-start(f32[1280]{0:T(1024)} %refs_10_.1) | copy-start | bytes 15364
  98.5 4.9 %collective-permute-start.19 = (bf16[128,320]{1,0:T(8,128)(2,1)S(1)}, bf16[128,320]{1,0:T(8,128)(2,1)S(1)}, u32[]{:S(2)}, u32[]{:S(2)}) collective-permute-start(bf16[128,320]{1,0:T(8,128)(2,1)S(1)} %get-tuple-element.33), channel_id=1, source_target_pairs={{6,0},{7,1},{0,2},{1,3},{2,4},{3,5},{4,6},{5,7},{14,8},{15,9},{8,1... | collective-permute-start | bytes 245768 | tf_op jit(solution)/shard_map/ppermute | solution.py:44
  103.4 4.8 %collective-permute-start.20 = (bf16[128,320]{1,0:T(8,128)(2,1)S(1)}, bf16[128,320]{1,0:T(8,128)(2,1)S(1)}, u32[]{:S(2)}, u32[]{:S(2)}) collective-permute-start(bf16[128,320]{1,0:T(8,128)(2,1)S(1)} %get-tuple-element.30.refs_0_), channel_id=1, source_target_pairs={{0,1},{1,0},{2,3},{3,2},{4,5},{5,4},{6,7},{7,6},{8,9},{9,8},{10,11... | collective-permute-start | bytes 245768 | tf_op jit(solution)/shard_map/ppermute | solution.py:48
  106.6 1.5 %collective-permute-start.21 = (bf16[128,320]{1,0:T(8,128)(2,1)S(1)}, bf16[128,320]{1,0:T(8,128)(2,1)S(1)}, u32[]{:S(2)}, u32[]{:S(2)}) collective-permute-start(bf16[128,320]{1,0:T(8,128)(2,1)S(1)} %collective-permute-done.17.refs_1_), channel_id=1, source_target_pairs={{0,1},{1,0},{2,3},{3,2},{4,5},{5,4},{6,7},{7,6},{8,9},{9,8},{10,11... | collective-permute-start | bytes 245768 | tf_op jit(solution)/shard_map/ppermute | solution.py:48
  106.6 1.5 %collective-permute-start.22 = (bf16[128,320]{1,0:T(8,128)(2,1)S(1)}, bf16[128,320]{1,0:T(8,128)(2,1)S(1)}, u32[]{:S(2)}, u32[]{:S(2)}) collective-permute-start(bf16[128,320]{1,0:T(8,128)(2,1)S(1)} %collective-permute-done.18.refs_2_), channel_id=1, source_target_pairs={{0,1},{1,0},{2,3},{3,2},{4,5},{5,4},{6,7},{7,6},{8,9},{9,8},{10,11... | collective-permute-start | bytes 245768 | tf_op jit(solution)/shard_map/ppermute | solution.py:48
  107.1 1.3 %collective-permute-start.23 = (bf16[128,320]{1,0:T(8,128)(2,1)S(1)}, bf16[128,320]{1,0:T(8,128)(2,1)S(1)}, u32[]{:S(2)}, u32[]{:S(2)}) collective-permute-start(bf16[128,320]{1,0:T(8,128)(2,1)S(1)} %collective-permute-done.19.refs_3_), channel_id=1, source_target_pairs={{0,1},{1,0},{2,3},{3,2},{4,5},{5,4},{6,7},{7,6},{8,9},{9,8},{10,11... | collective-permute-start | bytes 245768 | tf_op jit(solution)/shard_map/ppermute | solution.py:48

commit v3 on v2

--- a/solution.py
+++ b/solution.py
@@ -17,10 +17,15 @@
 
 VM = pl.BlockSpec(memory_space=pltpu.VMEM)
 SM = pl.BlockSpec(memory_space=pltpu.SMEM)
+BLK = pl.BlockSpec()
 
 
 def params(mib):
     return pltpu.CompilerParams(vmem_limit_bytes=mib * 1024 * 1024)
+
+
+def weight(us):
+    return pl.CostEstimate(flops=us * 10**9, bytes_accessed=0, transcendentals=0)
 
 
 def after(value, *earlier):
@@ -38,6 +43,20 @@
     return [
         (((x + dx) % 4) * 8 + (z + dz) % 8, x * 8 + z) for x in range(4) for z in range(8)
     ]
+
+
+X_GROUPS = [[x * 8 + z for x in range(4)] for z in range(8)]
+
+
+Z_GROUPS = [[x * 8 + z for z in range(8)] for x in range(4)]
+
+
+def for_each(value, groups):
+    return jnp.broadcast_to(value[None], (len(groups[0]), *value.shape))
+
+
+def exchange(value, groups):
+    return lax.all_to_all(value, "dp", 0, 0, tiled=True, axis_index_groups=groups)
 
 
 def from_seq(value, dy):
@@ -62,33 +81,12 @@
     norm_out[...] = (scaled + bias[...][None]).astype(BF16)
 
 
-def lay_kernel(place, *refs):
-    blocks, out = refs[:8], refs[8]
-    col = lax.broadcasted_iota(jnp.int32, (3 * OWN, WIDE), 0)
-    lane = lax.broadcasted_iota(jnp.int32, (3 * OWN, WIDE), 1)
-    piece = sum((col >= HDIM * k).astype(jnp.int32) for k in range(1, 5))
-    high = ((col - HDIM * piece >= HDIM // 2) & (col < 4 * HDIM)).astype(jnp.int32)
-    pick = (lane == col + 48 * piece + 24 * high).astype(F32).astype(BF16)
-    x, z = place[0], place[1]
-    for dz in range(8):
-        wide = jnp.dot(blocks[dz][...], pick, preferred_element_type=F32).astype(BF16)
-        for dx in range(4):
-            at = lax.rem(x + dx, 4) * 8 + lax.rem(z + dz, 8)
-            out[at] = wide[dx * 40 : dx * 40 + 40]
-
-
-def out_lay_kernel(place, *refs):
-    out = refs[8]
-    x, z, c = place[0], place[1], place[3]
-    for half in range(2):
-        first = pl.multiple_of(jnp.bitwise_xor(c, half) * 640, 128)
-        for dx in range(4):
-            for dz in range(8):
-                at = lax.rem(x + dx, 4) * 8 + lax.rem(z + dz, 8)
-                out[at, :, pl.ds(first, 640)] = refs[half * 4 + dx][dz]
-
-
-def tables_kernel(place, inverse, cos_out, sin_out):
+def stack_kernel(b0, b1, b2, b3, out):
+    blocks = [b[...].astype(F32) for b in (b0, b1, b2, b3)]
+    out[...] = jnp.concatenate(blocks, axis=0).astype(BF16)
+
+
+def write_tables(place, inverse, cos_out, sin_out):
     y, c = place[2], place[3]
     o0, o1, o2 = place[4], place[5], place[6]
     lane = lax.broadcasted_iota(jnp.int32, (128, 128), 1)
@@ -120,6 +118,22 @@
         total = sum(jnp.dot(pick, part, preferred_element_type=F32) for part in parts)
         cos_out[r] = total[:, :128]
         sin_out[r] = total[:, 128:]
+
+
+def lay_kernel(place, inverse, *refs):
+    blocks, (out, cos_out, sin_out) = refs[:8], refs[8:]
+    col = lax.broadcasted_iota(jnp.int32, (3 * OWN, WIDE), 0)
+    lane = lax.broadcasted_iota(jnp.int32, (3 * OWN, WIDE), 1)
+    piece = sum((col >= HDIM * k).astype(jnp.int32) for k in range(1, 5))
+    high = ((col - HDIM * piece >= HDIM // 2) & (col < 4 * HDIM)).astype(jnp.int32)
+    pick = (lane == col + 48 * piece + 24 * high).astype(F32).astype(BF16)
+    x, z = place[0], place[1]
+    for dz in range(8):
+        wide = jnp.dot(blocks[dz][...], pick, preferred_element_type=F32).astype(BF16)
+        for dx in range(4):
+            at = lax.rem(x + dx, 4) * 8 + lax.rem(z + dz, 8)
+            out[at] = wide[dx * 40 : dx * 40 + 40]
+    write_tables(place, inverse, cos_out, sin_out)
 
 
 def attend_kernel(place, *refs):
@@ -173,14 +187,16 @@
 
 def out_kernel(place, *refs):
     here, there = refs[:4], refs[4:8]
-    w, emb, bias, out = refs[8:]
+    w_own, w_other, emb, bias, out, mixed = refs[8:]
     y, c = place[2], place[3]
-    acc = emb[...].astype(F32) + bias[...][None]
-    for dy in range(4):
-        chip = lax.rem(y + dy, 4) * 2
-        acc += jnp.dot(here[dy][:, :OWN], w[chip + c], preferred_element_type=F32)
-        acc += jnp.dot(there[dy][:, OWN:], w[chip + 1 - c], preferred_element_type=F32)
-    out[...] = acc.astype(BF16)
+    for w, half in ((w_own, c), (w_other, 1 - c)):
+        acc = jnp.zeros((128, 640), F32)
+        for dy in range(4):
+            chip = lax.rem(y + dy, 4) * 2
+            acc += jnp.dot(here[dy][:, :OWN], w[chip + c], preferred_element_type=F32)
+            acc += jnp.dot(there[dy][:, OWN:], w[chip + 1 - c], preferred_element_type=F32)
+        mixed[:, pl.ds(pl.multiple_of(half * 640, 128), 640)] = acc
+    out[...] = (emb[...].astype(F32) + mixed[...] + bias[...][None]).astype(BF16)
 
 
 def halves_apart(piece):
@@ -219,21 +235,16 @@
     slices = [lax.dynamic_slice_in_dim(qkv_weight, k * D + seq * OWN, OWN, 1) for k in range(3)]
     mine = after(jnp.concatenate(slices, axis=1), blocks)
     xs = [mine] + [from_dp(mine, d, 0) for d in (1, 2, 3)]
-    z0 = jnp.concatenate(xs, axis=0)
+    z0 = pl.pallas_call(
+        stack_kernel,
+        out_shape=jax.ShapeDtypeStruct((160, 3 * OWN), BF16),
+        in_specs=[BLK] * 4,
+        out_specs=VM,
+        compiler_params=params(4),
+        name="stack",
+    )(*xs)
     z1, z7 = from_dp(z0, 0, 1), from_dp(z0, 0, 7)
     z2, z6 = from_dp(z1, 0, 1), from_dp(z7, 0, 7)
-
-    half = after(lax.dynamic_slice_in_dim(out_weight, c * 640, 640, 1)[None], z0)
-    h1, h7 = from_dp(half, 0, 1), from_dp(half, 0, 7)
-
-    cosine, sine = pl.pallas_call(
-        tables_kernel,
-        out_shape=(jax.ShapeDtypeStruct((8, 128, 128), F32),) * 2,
-        in_specs=[SM, VM],
-        out_specs=(VM, VM),
-        compiler_params=params(6),
-        name="tables",
-    )(place, jnp.asarray(INVERSE))
 
     embedded, normed = pl.pallas_call(
         embed_kernel,
@@ -251,14 +262,24 @@
     z2, z6 = after(z2, normed), after(z6, normed)
     z3, z5 = from_dp(z2, 0, 1), from_dp(z6, 0, 7)
     z4 = from_dp(z3, 0, 1)
-    laid = pl.pallas_call(
+    half = for_each(lax.dynamic_slice_in_dim(out_weight, c * 640, 640, 1), Z_GROUPS)
+    column = exchange(after(half, normed, z1, z7), Z_GROUPS)
+    column = for_each(column.reshape(320, 640), X_GROUPS)
+    o_own = exchange(column, X_GROUPS).reshape(8, OWN, 640)
+
+    laid, cosine, sine = pl.pallas_call(
         lay_kernel,
-        out_shape=jax.ShapeDtypeStruct((32, 40, WIDE), BF16),
-        in_specs=[SM] + [VM] * 8,
-        out_specs=VM,
+        out_shape=(
+            jax.ShapeDtypeStruct((32, 40, WIDE), BF16),
+            jax.ShapeDtypeStruct((8, 128, 128), F32),
+            jax.ShapeDtypeStruct((8, 128, 128), F32),
+        ),
+        in_specs=[SM] + [BLK] * 9,
+        out_specs=(VM,) * 3,
         compiler_params=params(12),
-        name="lay_qkv",
-    )(place, z0, z1, z2, z3, z4, z5, z6, z7).reshape(D, WIDE)
+        name="lay",
+    )(place, jnp.asarray(INVERSE), after(z0, column), z1, z2, z3, z4, z5, z6, z7)
+    laid = laid.reshape(D, WIDE)
 
     own_bias = [lax.dynamic_slice_in_dim(qkv_bias, k * D + seq * OWN, OWN, 0) for k in range(3)]
     ones = jnp.ones((1,), F32)
@@ -267,47 +288,35 @@
         + [own_bias[2], ones, jnp.zeros((95,), F32)]
     )
 
-    half, h1, h7 = (after(v, normed) for v in (half, h1, h7))
-    h234 = from_dp(jnp.concatenate([h7, half, h1]), 0, 3)
-    h56 = from_dp(jnp.concatenate([half, h1]), 0, 5)
-    column0 = jnp.concatenate([half, h1, h234, h56, h7])
-    columns = [column0] + [from_dp(column0, d, 0) for d in (1, 2, 3)]
-
     parts = pl.pallas_call(
         attend_kernel,
         out_shape=(jax.ShapeDtypeStruct((128, 2 * OWN), BF16),) * 4,
-        in_specs=[SM] + [VM] * 12,
+        in_specs=[SM] + [BLK] * 12,
         out_specs=(VM,) * 4,
         scratch_shapes=[
             pltpu.VMEM((2, 1024, 128), BF16),
             pltpu.VMEM((2, 1024, 128), BF16),
             pltpu.VMEM((1024, 256), BF16),
         ],
-        compiler_params=params(28),
+        compiler_params=params(18),
+        cost_estimate=weight(60),
         name="attend",
     )(place, *shards, laid, laid_bias, cosine, sine)
 
     got = [parts[0]] + [from_seq(parts[(4 - d) % 4], d) for d in (1, 2, 3)]
     got_other = [swap(v) for v in got]
 
-    others = [swap(after(v, parts[0])) for v in columns]
-    out_laid = pl.pallas_call(
-        out_lay_kernel,
-        out_shape=jax.ShapeDtypeStruct((32, 40, D), BF16),
-        in_specs=[SM] + [VM] * 8,
-        out_specs=VM,
-        compiler_params=params(12),
-        name="lay_out",
-    )(place, *columns, *others).reshape(8, OWN, D)
+    o_other = swap(after(o_own, *got[1:]))
 
     return pl.pallas_call(
         out_kernel,
         out_shape=rows,
-        in_specs=[SM] + [VM] * 11,
+        in_specs=[SM] + [BLK] * 12,
         out_specs=VM,
+        scratch_shapes=[pltpu.VMEM((128, D), F32)],
         compiler_params=params(12),
         name="project",
-    )(place, *got, *got_other, out_laid, embedded, out_bias)
+    )(place, *got, *got_other, o_own, o_other, embedded, out_bias)
 
 
 def solution(mesh):

time: 112 us -> 98.9 us (0.88)
  starting transfers between devices: 56.1 us -> 51 us
  local copies, waits for them, and re-layouts: 11.9 us -> 8.76 us
  other arithmetic: 1.76 us -> 0.09 us
  Pallas kernels: 15.5 us -> 14 us
    ppermute x17 -> x10, starting transfers between devices: 23.7 us -> 15.7 us  [from_dp(): return lax.ppermute(value, 'dp', dp_shift(dx, dz))]
    all_to_all x0 -> x2, starting transfers between devices: none -> 7.53 us  [exchange(): lax.all_to_all(value, 'dp', 0, 0, tiled=True, axis_index_groups=groups)]
    ppermute x12 -> x9, starting transfers between devices: 14.1 us -> 8.35 us  [swap(): return lax.ppermute(value, 'seq', SWAP)]
    unnamed x44 -> x25, local copies, waits for them, and re-layouts: 7.17 us -> 2.77 us
    ppermute x6, waiting for transfers between devices: 9.42 us -> 6.11 us  [from_seq(): return lax.ppermute(value, 'seq', seq_shift(dy))]
    ppermute x12 -> x9, waiting for transfers between devices: 0.3 us -> 2.68 us  [swap(): return lax.ppermute(value, 'seq', SWAP)]
    broadcast_in_dim x1 -> x2, local copies, waits for them, and re-layouts: 0.01 us -> 2.09 us  [for_each(): return jnp.broadcast_to(value[None], (len(groups[0]), *value.shape))]
    concatenate x2 -> x0, other arithmetic: 1.67 us -> none  [the longest x1 0.85 us: per_device(): h234 = from_dp(jnp.concatenate([h7, half, h1]), 0, 3)]
  transfers between devices with their start and end apart: 36 -> 28, of which waited for: 8 -> 14; matrix products, arithmetic and copies ran while one was open for 5% -> 5% of each run, Pallas kernels for 12% -> 12%
where the time goes in v3:
time: 98.9 us; the launch traced here: 98.4 us
  starting transfers between devices  51 us (52%)
  waiting for transfers between devices  24.3 us (25%)
  Pallas kernels  14 us (14%)
  local copies, waits for them, and re-layouts  8.76 us (9%)
    ppermute x10, starting transfers between devices, from_dp(): return lax.ppermute(value, 'dp', dp_shift(dx, dz))  15.7 us
    ppermute x10, waiting for transfers between devices, from_dp(): return lax.ppermute(value, 'dp', dp_shift(dx, dz))  14.4 us
    all_to_all x1, starting transfers between devices, per_device(): lax.all_to_all(blocks, 'dp', 0, 0, tiled=True).reshape(128, -1)  12 us
    ppermute x9, starting transfers between devices, swap(): return lax.ppermute(value, 'seq', SWAP)  8.35 us
    all_to_all x2, starting transfers between devices, exchange(): lax.all_to_all(value, 'dp', 0, 0, tiled=True, axis_index_groups=groups)  7.53 us
    ppermute x6, starting transfers between devices, from_seq(): return lax.ppermute(value, 'seq', seq_shift(dy))  7.39 us
    pallas_call x1, Pallas kernels, per_device(): pl.pallas_call(attend_kernel, out_shape=(jax.ShapeDtypeStruct((128, 2 * O...  7.06 us
    ppermute x6, waiting for transfers between devices, from_seq(): return lax.ppermute(value, 'seq', seq_shift(dy))  6.11 us
  transfers between devices with their start and end apart: 28, of which 14 were waited for; matrix products, arithmetic and copies ran while one was open for 5% of the time, Pallas kernels for 12%

profile of v3, /device:TPU:1, one launch (start us, length us, event | category | flops | bytes accessed | tf_op | source)
XLA Modules:
  0.0 98.4 jit_solution(6733701068223521525)
XLA Ops:
  0.0 1.3 %copy.13 = bf16[128,1176]{1,0:T(8,128)(2,1)S(1)} copy(bf16[128,1176]{0,1:T(8,128)(2,1)} %param.11) | data formatting | bytes 602112 | tf_op args[0]
  1.3 0.8 reshape.14
  2.1 12.0 %all-to-all-start = ((bf16[32,4,1176]{2,1,0:T(4,128)(2,1)}), bf16[32,4,1176]{2,1,0:T(4,128)(2,1)}, u32[]{:S(2)}, u32[]{:S(2)}) async-start(bf16[32,4,1176]{2,1,0:T(4,128)(2,1)} %reshape.14), calls=%async_computation | async-start | bytes 655360 | tf_op jit(solution)/shard_map/all_to_all | solution.py:233
  14.1 0.9 constant_dynamic-slice_fusion.3
  15.0 0.1 pad_maximum_fusion.b0
  15.1 2.5 %collective-permute-start.7 = (bf16[40,480]{1,0:T(8,128)(2,1)S(1)}, bf16[40,480]{1,0:T(8,128)(2,1)S(1)}, u32[]{:S(2)}, u32[]{:S(2)}) collective-permute-start(bf16[40,480]{1,0:T(8,128)(2,1)S(1)} %pad_maximum_fusion.b0), channel_id=1, source_target_pairs={{64,0},{72,8},{80,16},{88,24},{96,32},{104,40},{112,48},{120,56},{... | collective-permute-start | bytes 115208 | tf_op jit(solution)/shard_map/ppermute | solution.py:71
  17.6 0.5 collective-permute-start.8
  18.1 0.6 collective-permute-start.9
  18.7 4.1 %collective-permute-done.8.b2 = bf16[40,480]{1,0:T(8,128)(2,1)S(1)} collective-permute-done((bf16[40,480]{1,0:T(8,128)(2,1)S(1)}, bf16[40,480]{1,0:T(8,128)(2,1)S(1)}, u32[]{:S(2)}, u32[]{:S(2)}) %collective-permute-start.8) | collective-permute-done | bytes 38432 | tf_op jit(solution)/shard_map/ppermute | solution.py:71
  22.8 0.7 collective-permute-done.9.b3
  23.5 0.7 stack.17.refs_0_
  24.2 2.8 %collective-permute-start.10 = (bf16[160,480]{1,0:T(8,128)(2,1)}, bf16[160,480]{1,0:T(8,128)(2,1)}, u32[]{:S(2)}, u32[]{:S(2)}) collective-permute-start(bf16[160,480]{1,0:T(8,128)(2,1)} %stack.17.refs_0_), channel_id=1, source_target_pairs={{8,0},{16,8},{24,16},{32,24},{40,32},{48,40},{56,48},{0,56},{72,64... | collective-permute-start | bytes 460808 | tf_op jit(solution)/shard_map/ppermute | solution.py:71
  27.0 0.0 all-to-all-done
  27.0 1.1 %reshape.15.px = bf16[128,1176]{1,0:T(8,128)(2,1)S(1)} reshape(bf16[32,4,1176]{2,1,0:T(4,128)(2,1)} %all-to-all-done) | data formatting | bytes 602112 | tf_op jit(solution)/shard_map/reshape | solution.py:233
  28.1 0.0 copy-start.10
  28.1 0.0 copy-start.11
  28.1 0.9 embed.1
  29.0 0.7 copy-done.2
  29.7 0.7 copy-done.8
  30.5 2.2 %collective-permute-done.11.refs_7_ = bf16[160,480]{1,0:T(8,128)(2,1)} collective-permute-done((bf16[160,480]{1,0:T(8,128)(2,1)}, bf16[160,480]{1,0:T(8,128)(2,1)}, u32[]{:S(2)}, u32[]{:S(2)}) %collective-permute-start.11) | collective-permute-done | bytes 153632 | tf_op jit(solution)/shard_map/ppermute | solution.py:71
  32.6 0.8 broadcast_in_dim.16
  33.4 3.8 %all-to-all-start.1 = ((bf16[8,40,640]{2,1,0:T(8,128)(2,1)}), bf16[8,40,640]{2,1,0:T(8,128)(2,1)S(1)}, u32[]{:S(2)}, u32[]{:S(2)}) async-start(bf16[8,40,640]{2,1,0:T(8,128)(2,1)} %broadcast_in_dim.16), calls=%async_computation.1 | async-start | bytes 819200 | tf_op jit(solution)/shard_map/all_to_all | solution.py:59
  37.3 2.7 %collective-permute-start.1 = (bf16[128,1280]{1,0:T(8,128)(2,1)}, bf16[128,1280]{1,0:T(8,128)(2,1)S(1)}, u32[]{:S(2)}, u32[]{:S(2)}) collective-permute-start(bf16[128,1280]{1,0:T(8,128)(2,1)} %copy-done.8), channel_id=1, source_target_pairs={{2,0},{3,1},{4,2},{5,3},{6,4},{7,5},{0,6},{1,7},{10,8},{11,9},{12,... | collective-permute-start | bytes 983048 | tf_op jit(solution)/shard_map/ppermute | solution.py:63
  40.0 0.3 collective-permute-start.3
  40.3 0.7 collective-permute-start.5
  41.0 2.7 %collective-permute-start.12 = (bf16[160,480]{1,0:T(8,128)(2,1)}, bf16[160,480]{1,0:T(8,128)(2,1)S(1)}, u32[]{:S(2)}, u32[]{:S(2)}) collective-permute-start(bf16[160,480]{1,0:T(8,128)(2,1)} %collective-permute-done.10.refs_1_), channel_id=1, source_target_pairs={{8,0},{16,8},{24,16},{32,24},{40,32},{48,40},{56,48},{0,56},{72,64... | collective-permute-start | bytes 460808 | tf_op jit(solution)/shard_map/ppermute | solution.py:71
  43.7 4.5 %collective-permute-done.12.refs_2_ = bf16[160,480]{1,0:T(8,128)(2,1)S(1)} collective-permute-done((bf16[160,480]{1,0:T(8,128)(2,1)}, bf16[160,480]{1,0:T(8,128)(2,1)S(1)}, u32[]{:S(2)}, u32[]{:S(2)}) %collective-permute-start.12) | collective-permute-done | bytes 153632 | tf_op jit(solution)/shard_map/ppermute | solution.py:71
  48.2 3.2 %collective-permute-start.13 = (bf16[160,480]{1,0:T(8,128)(2,1)S(1)}, bf16[160,480]{1,0:T(8,128)(2,1)S(1)}, u32[]{:S(2)}, u32[]{:S(2)}) collective-permute-start(bf16[160,480]{1,0:T(8,128)(2,1)S(1)} %collective-permute-done.12.refs_2_), channel_id=1, source_target_pairs={{8,0},{16,8},{24,16},{32,24},{40,32},{48,40},{56,48},{0,56},{72,64... | collective-permute-start | bytes 460808 | tf_op jit(solution)/shard_map/ppermute | solution.py:71
  51.4 0.7 collective-permute-done.15.refs_6_
  52.1 0.0 collective-permute-start.16
  52.1 0.1 concatenate.9.place
  52.2 2.2 %collective-permute-done.13.refs_3_ = bf16[160,480]{1,0:T(8,128)(2,1)S(1)} collective-permute-done((bf16[160,480]{1,0:T(8,128)(2,1)S(1)}, bf16[160,480]{1,0:T(8,128)(2,1)S(1)}, u32[]{:S(2)}, u32[]{:S(2)}) %collective-permute-start.13) | collective-permute-done | bytes 153632 | tf_op jit(solution)/shard_map/ppermute | solution.py:71
  54.4 5.2 %collective-permute-start = (bf16[128,1280]{1,0:T(8,128)(2,1)}, bf16[128,1280]{1,0:T(8,128)(2,1)}, u32[]{:S(2)}, u32[]{:S(2)}) collective-permute-start(bf16[128,1280]{1,0:T(8,128)(2,1)} %copy-done.8), channel_id=1, source_target_pairs={{0,1},{1,0},{2,3},{3,2},{4,5},{5,4},{6,7},{7,6},{8,9},{9,8},{10,11... | collective-permute-start | bytes 983048 | tf_op jit(solution)/shard_map/ppermute | solution.py:67
  59.6 0.0 collective-permute-start.2
  59.6 0.0 collective-permute-done.3.refs_4_
  59.6 0.5 collective-permute-start.4
  60.1 0.0 collective-permute-done.5.refs_6_
  60.1 0.3 collective-permute-start.6
  60.4 0.8 fusion
  61.2 0.0 collective-permute-done.16.refs_5_
  61.2 3.4 %collective-permute-start.14 = (bf16[160,480]{1,0:T(8,128)(2,1)S(1)}, bf16[160,480]{1,0:T(8,128)(2,1)S(1)}, u32[]{:S(2)}, u32[]{:S(2)}) collective-permute-start(bf16[160,480]{1,0:T(8,128)(2,1)S(1)} %collective-permute-done.13.refs_3_), channel_id=1, source_target_pairs={{8,0},{16,8},{24,16},{32,24},{40,32},{48,40},{56,48},{0,56},{72,64... | collective-permute-start | bytes 460808 | tf_op jit(solution)/shard_map/ppermute | solution.py:71
  64.7 0.1 fusion.1
  64.8 0.1 concatenate.11.refs_9_
  64.9 1.3 %broadcast_in_dim.18 = bf16[4,320,640]{2,1,0:T(8,128)(2,1)} broadcast(bf16[320,640]{1,0:T(8,128)(2,1)S(1)} %bitcast.12), dimensions={1,2} | broadcast | bytes 2048000 | tf_op jit(solution)/shard_map/broadcast_in_dim | solution.py:55
  66.2 3.7 %all-to-all-start.2 = ((bf16[4,320,640]{2,1,0:T(8,128)(2,1)}), bf16[4,320,640]{2,1,0:T(8,128)(2,1)S(1)}, u32[]{:S(2)}, u32[]{:S(2)}) async-start(bf16[4,320,640]{2,1,0:T(8,128)(2,1)} %broadcast_in_dim.18), calls=%async_computation.2 | async-start | bytes 3276800 | tf_op jit(solution)/shard_map/all_to_all | solution.py:59
  69.9 2.9 %lay.1 = (bf16[32,40,768]{2,1,0:T(8,128)(2,1)S(1)}, f32[8,128,128]{2,1,0:T(8,128)S(1)}, f32[8,128,128]{2,1,0:T(8,128)S(1)}) custom-call(s32[16]{0:T(128)S(1)} %concatenate.9.place, f32[1,128]{1,0:T(1,128)S(1)} %copy-done.7, bf16[160,480]{1,0:T(8,128)(2,1)} %stack.17.refs_0_, bf16[160,480]{1,0:T(8,128)(2,1)} %collective-permute-done.10.refs_1_, ...), custom_call_target="tpu_custom_call" | custom-call | tf_op jit(solution)/shard_map/lay/pallas_call | solution.py:270
  72.9 0.0 copy-start.6
  72.9 7.1 %attend.1 = (bf16[128,320]{1,0:T(8,128)(2,1)S(1)}, bf16[128,320]{1,0:T(8,128)(2,1)S(1)}, bf16[128,320]{1,0:T(8,128)(2,1)S(1)}, bf16[128,320]{1,0:T(8,128)(2,1)S(1)}) custom-call(s32[16]{0:T(128)S(1)} %concatenate.9.place, bf16[128,1280]{1,0:T(8,128)(2,1)S(1)} %copy-done.9, bf16[128,1280]{1,0:T(8,128)(2,1)} %collective-permute-done.refs_1_, ...), custom_call_target="tpu_custom_call" | custom-call | flops 60000002048 | tf_op jit(solution)/shard_map/attend/pallas_call | solution.py:291
  80.0 1.8 %collective-permute-start.17 = (bf16[128,320]{1,0:T(8,128)(2,1)S(1)}, bf16[128,320]{1,0:T(8,128)(2,1)S(1)}, u32[]{:S(2)}, u32[]{:S(2)}) collective-permute-start(bf16[128,320]{1,0:T(8,128)(2,1)S(1)} %get-tuple-element.30), channel_id=1, source_target_pairs={{2,0},{3,1},{4,2},{5,3},{6,4},{7,5},{0,6},{1,7},{10,8},{11,9},{12,... | collective-permute-start | bytes 245768 | tf_op jit(solution)/shard_map/ppermute | solution.py:63
  81.8 1.8 %collective-permute-start.18 = (bf16[128,320]{1,0:T(8,128)(2,1)S(1)}, bf16[128,320]{1,0:T(8,128)(2,1)S(1)}, u32[]{:S(2)}, u32[]{:S(2)}) collective-permute-start(bf16[128,320]{1,0:T(8,128)(2,1)S(1)} %get-tuple-element.31), channel_id=1, source_target_pairs={{4,0},{5,1},{6,2},{7,3},{0,4},{1,5},{2,6},{3,7},{12,8},{13,9},{14,... | collective-permute-start | bytes 245768 | tf_op jit(solution)/shard_map/ppermute | solution.py:63
  83.6 0.9 collective-permute-done.17.refs_1_
  84.5 2.5 %collective-permute-done.18.refs_2_ = bf16[128,320]{1,0:T(8,128)(2,1)S(1)} collective-permute-done((bf16[128,320]{1,0:T(8,128)(2,1)S(1)}, bf16[128,320]{1,0:T(8,128)(2,1)S(1)}, u32[]{:S(2)}, u32[]{:S(2)}) %collective-permute-start.18) | collective-permute-done | bytes 81952 | tf_op jit(solution)/shard_map/ppermute | solution.py:63
  87.0 2.7 %collective-permute-done.19.refs_3_ = bf16[128,320]{1,0:T(8,128)(2,1)S(1)} collective-permute-done((bf16[128,320]{1,0:T(8,128)(2,1)S(1)}, bf16[128,320]{1,0:T(8,128)(2,1)S(1)}, u32[]{:S(2)}, u32[]{:S(2)}) %collective-permute-start.19) | collective-permute-done | bytes 81952 | tf_op jit(solution)/shard_map/ppermute | solution.py:63
  89.7 1.1 %all-to-all-done.2 = bf16[4,320,640]{2,1,0:T(8,128)(2,1)S(1)} async-done(((bf16[4,320,640]{2,1,0:T(8,128)(2,1)}), bf16[4,320,640]{2,1,0:T(8,128)(2,1)S(1)}, u32[]{:S(2)}, u32[]{:S(2)}) %all-to-all-start.2) | async-done | bytes 1638432 | tf_op jit(solution)/shard_map/all_to_all | solution.py:59
  90.8 1.4 %collective-permute-start.24 = (bf16[8,160,640]{2,1,0:T(8,128)(2,1)S(1)}, bf16[8,160,640]{2,1,0:T(8,128)(2,1)S(1)}, u32[]{:S(2)}, u32[]{:S(2)}) collective-permute-start(bf16[8,160,640]{2,1,0:T(8,128)(2,1)S(1)} %bitcast.9), channel_id=1, source_target_pairs={{0,1},{1,0},{2,3},{3,2},{4,5},{5,4},{6,7},{7,6},{8,9},{9,8},{10,11... | collective-permute-start | bytes 4915208 | tf_op jit(solution)/shard_map/ppermute | solution.py:67
  92.2 0.0 collective-permute-start.20
  92.2 0.5 collective-permute-start.21
  92.7 0.0 collective-permute-start.22
  92.7 0.5 collective-permute-start.23
  93.2 2.2 %collective-permute-done.20.refs_4_ = bf16[128,320]{1,0:T(8,128)(2,1)S(1)} collective-permute-done((bf16[128,320]{1,0:T(8,128)(2,1)S(1)}, bf16[128,320]{1,0:T(8,128)(2,1)S(1)}, u32[]{:S(2)}, u32[]{:S(2)}) %collective-permute-start.20) | collective-permute-done | bytes 81952 | tf_op jit(solution)/shard_map/ppermute | solution.py:67
  95.5 0.1 collective-permute-done.21.refs_5_
  95.6 0.1 collective-permute-done.22.refs_6_
  95.8 0.1 collective-permute-done.23.refs_7_
  95.9 2.4 %project.1 = bf16[128,1280]{1,0:T(8,128)(2,1)} custom-call(s32[16]{0:T(128)S(1)} %concatenate.9.place, bf16[128,320]{1,0:T(8,128)(2,1)S(1)} %get-tuple-element.29.refs_0_, bf16[128,320]{1,0:T(8,128)(2,1)S(1)} %collective-permute-done.17.refs_1_, bf16[128,320]{1,0:T(8,128)(2,1)S(1)} %collective-permute-done.18.refs_2_, ...), custom_call_target="tpu_custom_call" | custom-call | tf_op jit(solution)/shard_map/project/pallas_call | solution.py:311
  (36 shorter events, 0.1 us)
Async XLA Ops:
  0.0 27.0 %copy-start = (bf16[40,1280]{1,0:T(8,128)(2,1)S(1)}, bf16[40,1280]{1,0:T(8,128)(2,1)}, u32[]{:S(2)}) copy-start(bf16[40,1280]{1,0:T(8,128)(2,1)} %param.17) | copy-start | bytes 307204
  0.0 28.1 %copy-start.1 = (bf16[1176,1280]{1,0:T(8,128)(2,1)S(1)}, bf16[1176,1280]{1,0:T(8,128)(2,1)}, u32[]{:S(2)}) copy-start(bf16[1176,1280]{1,0:T(8,128)(2,1)} %pw.1) | copy-start | bytes 9031684
  0.0 28.1 %copy-start.4 = (f32[1280]{0:T(1024)S(1)}, f32[1280]{0:T(1024)}, u32[]{:S(2)}) copy-start(f32[1280]{0:T(1024)} %gain.1) | copy-start | bytes 15364
  0.0 28.1 %copy-start.5 = (f32[1280]{0:T(1024)S(1)}, f32[1280]{0:T(1024)}, u32[]{:S(2)}) copy-start(f32[1280]{0:T(1024)} %bias.1) | copy-start | bytes 15364
  2.1 24.8 %all-to-all-start = ((bf16[32,4,1176]{2,1,0:T(4,128)(2,1)}), bf16[32,4,1176]{2,1,0:T(4,128)(2,1)}, u32[]{:S(2)}, u32[]{:S(2)}) async-start(bf16[32,4,1176]{2,1,0:T(4,128)(2,1)} %reshape.14), calls=%async_computation | async-start | bytes 655360 | tf_op jit(solution)/shard_map/all_to_all | solution.py:233
  15.1 3.6 %collective-permute-start.7 = (bf16[40,480]{1,0:T(8,128)(2,1)S(1)}, bf16[40,480]{1,0:T(8,128)(2,1)S(1)}, u32[]{:S(2)}, u32[]{:S(2)}) collective-permute-start(bf16[40,480]{1,0:T(8,128)(2,1)S(1)} %pad_maximum_fusion.b0), channel_id=1, source_target_pairs={{64,0},{72,8},{80,16},{88,24},{96,32},{104,40},{112,48},{120,56},{... | collective-permute-start | bytes 115208 | tf_op jit(solution)/shard_map/ppermute | solution.py:71
  17.6 5.2 %collective-permute-start.8 = (bf16[40,480]{1,0:T(8,128)(2,1)S(1)}, bf16[40,480]{1,0:T(8,128)(2,1)S(1)}, u32[]{:S(2)}, u32[]{:S(2)}) collective-permute-start(bf16[40,480]{1,0:T(8,128)(2,1)S(1)} %pad_maximum_fusion.b0), channel_id=1, source_target_pairs={{128,0},{136,8},{144,16},{152,24},{160,32},{168,40},{176,48},{184,... | collective-permute-start | bytes 115208 | tf_op jit(solution)/shard_map/ppermute | solution.py:71
  18.1 5.4 %collective-permute-start.9 = (bf16[40,480]{1,0:T(8,128)(2,1)S(1)}, bf16[40,480]{1,0:T(8,128)(2,1)S(1)}, u32[]{:S(2)}, u32[]{:S(2)}) collective-permute-start(bf16[40,480]{1,0:T(8,128)(2,1)S(1)} %pad_maximum_fusion.b0), channel_id=1, source_target_pairs={{192,0},{200,8},{208,16},{216,24},{224,32},{232,40},{240,48},{248,... | collective-permute-start | bytes 115208 | tf_op jit(solution)/shard_map/ppermute | solution.py:71
  24.2 6.3 %collective-permute-start.10 = (bf16[160,480]{1,0:T(8,128)(2,1)}, bf16[160,480]{1,0:T(8,128)(2,1)}, u32[]{:S(2)}, u32[]{:S(2)}) collective-permute-start(bf16[160,480]{1,0:T(8,128)(2,1)} %stack.17.refs_0_), channel_id=1, source_target_pairs={{8,0},{16,8},{24,16},{32,24},{40,32},{48,40},{56,48},{0,56},{72,64... | collective-permute-start | bytes 460808 | tf_op jit(solution)/shard_map/ppermute | solution.py:71
  27.0 5.7 %collective-permute-start.11 = (bf16[160,480]{1,0:T(8,128)(2,1)}, bf16[160,480]{1,0:T(8,128)(2,1)}, u32[]{:S(2)}, u32[]{:S(2)}) collective-permute-start(bf16[160,480]{1,0:T(8,128)(2,1)} %stack.17.refs_0_), channel_id=1, source_target_pairs={{56,0},{0,8},{8,16},{16,24},{24,32},{32,40},{40,48},{48,56},{120,6... | collective-permute-start | bytes 460808 | tf_op jit(solution)/shard_map/ppermute | solution.py:71
  28.1 24.0 %copy-start.10 = (s32[1,3]{1,0:T(1,128)S(1)}, s32[1,3]{1,0:T(1,128)}, u32[]{:S(2)}) copy-start(s32[1,3]{1,0:T(1,128)} %param.19) | copy-start | bytes 40
  28.1 24.0 %copy-start.11 = (s32[1,3]{1,0:T(1,128)S(1)}, s32[1,3]{1,0:T(1,128)}, u32[]{:S(2)}) copy-start(s32[1,3]{1,0:T(1,128)} %param.20) | copy-start | bytes 40
  29.0 0.7 copy-start.2
  29.7 0.7 copy-start.8
  33.4 31.4 %all-to-all-start.1 = ((bf16[8,40,640]{2,1,0:T(8,128)(2,1)}), bf16[8,40,640]{2,1,0:T(8,128)(2,1)S(1)}, u32[]{:S(2)}, u32[]{:S(2)}) async-start(bf16[8,40,640]{2,1,0:T(8,128)(2,1)} %broadcast_in_dim.16), calls=%async_computation.1 | async-start | bytes 819200 | tf_op jit(solution)/shard_map/all_to_all | solution.py:59
  37.3 22.3 %collective-permute-start.1 = (bf16[128,1280]{1,0:T(8,128)(2,1)}, bf16[128,1280]{1,0:T(8,128)(2,1)S(1)}, u32[]{:S(2)}, u32[]{:S(2)}) collective-permute-start(bf16[128,1280]{1,0:T(8,128)(2,1)} %copy-done.8), channel_id=1, source_target_pairs={{2,0},{3,1},{4,2},{5,3},{6,4},{7,5},{0,6},{1,7},{10,8},{11,9},{12,... | collective-permute-start | bytes 983048 | tf_op jit(solution)/shard_map/ppermute | solution.py:63
  40.0 19.6 %collective-permute-start.3 = (bf16[128,1280]{1,0:T(8,128)(2,1)}, bf16[128,1280]{1,0:T(8,128)(2,1)S(1)}, u32[]{:S(2)}, u32[]{:S(2)}) collective-permute-start(bf16[128,1280]{1,0:T(8,128)(2,1)} %copy-done.8), channel_id=1, source_target_pairs={{4,0},{5,1},{6,2},{7,3},{0,4},{1,5},{2,6},{3,7},{12,8},{13,9},{14,... | collective-permute-start | bytes 983048 | tf_op jit(solution)/shard_map/ppermute | solution.py:63
  40.3 19.8 %collective-permute-start.5 = (bf16[128,1280]{1,0:T(8,128)(2,1)}, bf16[128,1280]{1,0:T(8,128)(2,1)}, u32[]{:S(2)}, u32[]{:S(2)}) collective-permute-start(bf16[128,1280]{1,0:T(8,128)(2,1)} %copy-done.8), channel_id=1, source_target_pairs={{6,0},{7,1},{0,2},{1,3},{2,4},{3,5},{4,6},{5,7},{14,8},{15,9},{8,1... | collective-permute-start | bytes 983048 | tf_op jit(solution)/shard_map/ppermute | solution.py:63
  41.0 7.2 %collective-permute-start.12 = (bf16[160,480]{1,0:T(8,128)(2,1)}, bf16[160,480]{1,0:T(8,128)(2,1)S(1)}, u32[]{:S(2)}, u32[]{:S(2)}) collective-permute-start(bf16[160,480]{1,0:T(8,128)(2,1)} %collective-permute-done.10.refs_1_), channel_id=1, source_target_pairs={{8,0},{16,8},{24,16},{32,24},{40,32},{48,40},{56,48},{0,56},{72,64... | collective-permute-start | bytes 460808 | tf_op jit(solution)/shard_map/ppermute | solution.py:71
  43.7 8.4 %collective-permute-start.15 = (bf16[160,480]{1,0:T(8,128)(2,1)}, bf16[160,480]{1,0:T(8,128)(2,1)S(1)}, u32[]{:S(2)}, u32[]{:S(2)}) collective-permute-start(bf16[160,480]{1,0:T(8,128)(2,1)} %collective-permute-done.11.refs_7_), channel_id=1, source_target_pairs={{56,0},{0,8},{8,16},{16,24},{24,32},{32,40},{40,48},{48,56},{120,6... | collective-permute-start | bytes 460808 | tf_op jit(solution)/shard_map/ppermute | solution.py:71
  48.2 6.2 %collective-permute-start.13 = (bf16[160,480]{1,0:T(8,128)(2,1)S(1)}, bf16[160,480]{1,0:T(8,128)(2,1)S(1)}, u32[]{:S(2)}, u32[]{:S(2)}) collective-permute-start(bf16[160,480]{1,0:T(8,128)(2,1)S(1)} %collective-permute-done.12.refs_2_), channel_id=1, source_target_pairs={{8,0},{16,8},{24,16},{32,24},{40,32},{48,40},{56,48},{0,56},{72,64... | collective-permute-start | bytes 460808 | tf_op jit(solution)/shard_map/ppermute | solution.py:71
  52.1 9.1 %collective-permute-start.16 = (bf16[160,480]{1,0:T(8,128)(2,1)S(1)}, bf16[160,480]{1,0:T(8,128)(2,1)S(1)}, u32[]{:S(2)}, u32[]{:S(2)}) collective-permute-start(bf16[160,480]{1,0:T(8,128)(2,1)S(1)} %collective-permute-done.15.refs_6_), channel_id=1, source_target_pairs={{56,0},{0,8},{8,16},{16,24},{24,32},{32,40},{40,48},{48,56},{120,6... | collective-permute-start | bytes 460808 | tf_op jit(solution)/shard_map/ppermute | solution.py:71
  54.4 18.4 %collective-permute-start = (bf16[128,1280]{1,0:T(8,128)(2,1)}, bf16[128,1280]{1,0:T(8,128)(2,1)}, u32[]{:S(2)}, u32[]{:S(2)}) collective-permute-start(bf16[128,1280]{1,0:T(8,128)(2,1)} %copy-done.8), channel_id=1, source_target_pairs={{0,1},{1,0},{2,3},{3,2},{4,5},{5,4},{6,7},{7,6},{8,9},{9,8},{10,11... | collective-permute-start | bytes 983048 | tf_op jit(solution)/shard_map/ppermute | solution.py:67
  59.6 13.3 %collective-permute-start.2 = (bf16[128,1280]{1,0:T(8,128)(2,1)S(1)}, bf16[128,1280]{1,0:T(8,128)(2,1)}, u32[]{:S(2)}, u32[]{:S(2)}) collective-permute-start(bf16[128,1280]{1,0:T(8,128)(2,1)S(1)} %collective-permute-done.1.refs_2_), channel_id=1, source_target_pairs={{0,1},{1,0},{2,3},{3,2},{4,5},{5,4},{6,7},{7,6},{8,9},{9,8},{10,11... | collective-permute-start | bytes 983048 | tf_op jit(solution)/shard_map/ppermute | solution.py:67
  59.6 13.3 %collective-permute-start.4 = (bf16[128,1280]{1,0:T(8,128)(2,1)S(1)}, bf16[128,1280]{1,0:T(8,128)(2,1)}, u32[]{:S(2)}, u32[]{:S(2)}) collective-permute-start(bf16[128,1280]{1,0:T(8,128)(2,1)S(1)} %collective-permute-done.3.refs_4_), channel_id=1, source_target_pairs={{0,1},{1,0},{2,3},{3,2},{4,5},{5,4},{6,7},{7,6},{8,9},{9,8},{10,11... | collective-permute-start | bytes 983048 | tf_op jit(solution)/shard_map/ppermute | solution.py:67
  60.1 12.8 %collective-permute-start.6 = (bf16[128,1280]{1,0:T(8,128)(2,1)}, bf16[128,1280]{1,0:T(8,128)(2,1)}, u32[]{:S(2)}, u32[]{:S(2)}) collective-permute-start(bf16[128,1280]{1,0:T(8,128)(2,1)} %collective-permute-done.5.refs_6_), channel_id=1, source_target_pairs={{0,1},{1,0},{2,3},{3,2},{4,5},{5,4},{6,7},{7,6},{8,9},{9,8},{10,11... | collective-permute-start | bytes 983048 | tf_op jit(solution)/shard_map/ppermute | solution.py:67
  61.2 8.6 %collective-permute-start.14 = (bf16[160,480]{1,0:T(8,128)(2,1)S(1)}, bf16[160,480]{1,0:T(8,128)(2,1)S(1)}, u32[]{:S(2)}, u32[]{:S(2)}) collective-permute-start(bf16[160,480]{1,0:T(8,128)(2,1)S(1)} %collective-permute-done.13.refs_3_), channel_id=1, source_target_pairs={{8,0},{16,8},{24,16},{32,24},{40,32},{48,40},{56,48},{0,56},{72,64... | collective-permute-start | bytes 460808 | tf_op jit(solution)/shard_map/ppermute | solution.py:71
  66.2 3.7 %copy-start.7 = (f32[1,128]{1,0:T(1,128)S(1)}, f32[1,128]{1,0:T(1,128)}, u32[]{:S(2)}) copy-start(f32[1,128]{1,0:T(1,128)} %constant.75.clone.inverse) | copy-start | bytes 1540
  66.2 6.7 %copy-start.9 = (bf16[128,1280]{1,0:T(8,128)(2,1)S(1)}, bf16[128,1280]{1,0:T(8,128)(2,1)}, u32[]{:S(2)}) copy-start(bf16[128,1280]{1,0:T(8,128)(2,1)} %copy-done.8) | copy-start | bytes 983044
  66.2 24.7 %all-to-all-start.2 = ((bf16[4,320,640]{2,1,0:T(8,128)(2,1)}), bf16[4,320,640]{2,1,0:T(8,128)(2,1)S(1)}, u32[]{:S(2)}, u32[]{:S(2)}) async-start(bf16[4,320,640]{2,1,0:T(8,128)(2,1)} %broadcast_in_dim.18), calls=%async_computation.2 | async-start | bytes 3276800 | tf_op jit(solution)/shard_map/all_to_all | solution.py:59
  72.9 23.0 %copy-start.3 = (bf16[128,1280]{1,0:T(8,128)(2,1)S(1)}, bf16[128,1280]{1,0:T(8,128)(2,1)}, u32[]{:S(2)}) copy-start(bf16[128,1280]{1,0:T(8,128)(2,1)} %copy-done.2) | copy-start | bytes 983044
  72.9 23.0 %copy-start.6 = (f32[1280]{0:T(1024)S(1)}, f32[1280]{0:T(1024)}, u32[]{:S(2)}) copy-start(f32[1280]{0:T(1024)} %refs_11_.1) | copy-start | bytes 15364
  80.0 4.5 %collective-permute-start.17 = (bf16[128,320]{1,0:T(8,128)(2,1)S(1)}, bf16[128,320]{1,0:T(8,128)(2,1)S(1)}, u32[]{:S(2)}, u32[]{:S(2)}) collective-permute-start(bf16[128,320]{1,0:T(8,128)(2,1)S(1)} %get-tuple-element.30), channel_id=1, source_target_pairs={{2,0},{3,1},{4,2},{5,3},{6,4},{7,5},{0,6},{1,7},{10,8},{11,9},{12,... | collective-permute-start | bytes 245768 | tf_op jit(solution)/shard_map/ppermute | solution.py:63
  81.8 5.3 %collective-permute-start.18 = (bf16[128,320]{1,0:T(8,128)(2,1)S(1)}, bf16[128,320]{1,0:T(8,128)(2,1)S(1)}, u32[]{:S(2)}, u32[]{:S(2)}) collective-permute-start(bf16[128,320]{1,0:T(8,128)(2,1)S(1)} %get-tuple-element.31), channel_id=1, source_target_pairs={{4,0},{5,1},{6,2},{7,3},{0,4},{1,5},{2,6},{3,7},{12,8},{13,9},{14,... | collective-permute-start | bytes 245768 | tf_op jit(solution)/shard_map/ppermute | solution.py:63
  83.6 6.1 %collective-permute-start.19 = (bf16[128,320]{1,0:T(8,128)(2,1)S(1)}, bf16[128,320]{1,0:T(8,128)(2,1)S(1)}, u32[]{:S(2)}, u32[]{:S(2)}) collective-permute-start(bf16[128,320]{1,0:T(8,128)(2,1)S(1)} %get-tuple-element.32), channel_id=1, source_target_pairs={{6,0},{7,1},{0,2},{1,3},{2,4},{3,5},{4,6},{5,7},{14,8},{15,9},{8,1... | collective-permute-start | bytes 245768 | tf_op jit(solution)/shard_map/ppermute | solution.py:63
  90.8 5.1 %collective-permute-start.24 = (bf16[8,160,640]{2,1,0:T(8,128)(2,1)S(1)}, bf16[8,160,640]{2,1,0:T(8,128)(2,1)S(1)}, u32[]{:S(2)}, u32[]{:S(2)}) collective-permute-start(bf16[8,160,640]{2,1,0:T(8,128)(2,1)S(1)} %bitcast.9), channel_id=1, source_target_pairs={{0,1},{1,0},{2,3},{3,2},{4,5},{5,4},{6,7},{7,6},{8,9},{9,8},{10,11... | collective-permute-start | bytes 4915208 | tf_op jit(solution)/shard_map/ppermute | solution.py:67
  92.2 3.3 %collective-permute-start.20 = (bf16[128,320]{1,0:T(8,128)(2,1)S(1)}, bf16[128,320]{1,0:T(8,128)(2,1)S(1)}, u32[]{:S(2)}, u32[]{:S(2)}) collective-permute-start(bf16[128,320]{1,0:T(8,128)(2,1)S(1)} %get-tuple-element.29.refs_0_), channel_id=1, source_target_pairs={{0,1},{1,0},{2,3},{3,2},{4,5},{5,4},{6,7},{7,6},{8,9},{9,8},{10,11... | collective-permute-start | bytes 245768 | tf_op jit(solution)/shard_map/ppermute | solution.py:67
  92.2 3.4 %collective-permute-start.21 = (bf16[128,320]{1,0:T(8,128)(2,1)S(1)}, bf16[128,320]{1,0:T(8,128)(2,1)S(1)}, u32[]{:S(2)}, u32[]{:S(2)}) collective-permute-start(bf16[128,320]{1,0:T(8,128)(2,1)S(1)} %collective-permute-done.17.refs_1_), channel_id=1, source_target_pairs={{0,1},{1,0},{2,3},{3,2},{4,5},{5,4},{6,7},{7,6},{8,9},{9,8},{10,11... | collective-permute-start | bytes 245768 | tf_op jit(solution)/shard_map/ppermute | solution.py:67
  92.7 3.0 %collective-permute-start.22 = (bf16[128,320]{1,0:T(8,128)(2,1)S(1)}, bf16[128,320]{1,0:T(8,128)(2,1)S(1)}, u32[]{:S(2)}, u32[]{:S(2)}) collective-permute-start(bf16[128,320]{1,0:T(8,128)(2,1)S(1)} %collective-permute-done.18.refs_2_), channel_id=1, source_target_pairs={{0,1},{1,0},{2,3},{3,2},{4,5},{5,4},{6,7},{7,6},{8,9},{9,8},{10,11... | collective-permute-start | bytes 245768 | tf_op jit(solution)/shard_map/ppermute | solution.py:67
  92.7 3.2 %collective-permute-start.23 = (bf16[128,320]{1,0:T(8,128)(2,1)S(1)}, bf16[128,320]{1,0:T(8,128)(2,1)S(1)}, u32[]{:S(2)}, u32[]{:S(2)}) collective-permute-start(bf16[128,320]{1,0:T(8,128)(2,1)S(1)} %collective-permute-done.19.refs_3_), channel_id=1, source_target_pairs={{0,1},{1,0},{2,3},{3,2},{4,5},{5,4},{6,7},{7,6},{8,9},{9,8},{10,11... | collective-permute-start | bytes 245768 | tf_op jit(solution)/shard_map/ppermute | solution.py:67

commit v4 on v3

--- a/solution.py
+++ b/solution.py
@@ -72,7 +72,7 @@
 
 
 def embed_kernel(px, pw, gain, bias, emb_out, norm_out):
-    emb = jnp.dot(px[...], pw[...], preferred_element_type=F32).astype(BF16)
+    emb = jnp.dot(px[...].reshape(128, 1176), pw[...], preferred_element_type=F32).astype(BF16)
     emb_out[...] = emb
     v = emb.astype(F32)
     center = v - jnp.mean(v, axis=-1, keepdims=True)
@@ -81,9 +81,11 @@
     norm_out[...] = (scaled + bias[...][None]).astype(BF16)
 
 
-def stack_kernel(b0, b1, b2, b3, out):
+def stack_kernel(b0, b1, b2, b3, half, out, half_out):
     blocks = [b[...].astype(F32) for b in (b0, b1, b2, b3)]
     out[...] = jnp.concatenate(blocks, axis=0).astype(BF16)
+    for k in range(8):
+        half_out[k] = half[...]
 
 
 def write_tables(place, inverse, cos_out, sin_out):
@@ -105,6 +107,7 @@
     for _ in range(3):
         parts.append(both.astype(BF16))
         both = both - parts[-1].astype(F32)
+    picks = []
     for r in range(8):
         first = (lax.rem(y + r // 2, 4) * 2 + jnp.bitwise_xor(c, r % 2)) * 128
         pos = first + sub
@@ -114,10 +117,12 @@
         within = pos - start
         row = ((within.astype(F32) + 0.5) / across.astype(F32)).astype(jnp.int32)
         column = within - row * across
-        pick = (jnp.where(lane < 64, row, column + 64) == lane).astype(F32).astype(BF16)
-        total = sum(jnp.dot(pick, part, preferred_element_type=F32) for part in parts)
-        cos_out[r] = total[:, :128]
-        sin_out[r] = total[:, 128:]
+        picks.append((jnp.where(lane < 64, row, column + 64) == lane).astype(F32).astype(BF16))
+    pick = jnp.concatenate(picks, axis=0)
+    total = sum(jnp.dot(pick, part, preferred_element_type=F32) for part in parts)
+    for r in range(8):
+        cos_out[r] = total[r * 128 : r * 128 + 128, :128]
+        sin_out[r] = total[r * 128 : r * 128 + 128, 128:]
 
 
 def lay_kernel(place, inverse, *refs):
@@ -128,11 +133,13 @@
     high = ((col - HDIM * piece >= HDIM // 2) & (col < 4 * HDIM)).astype(jnp.int32)
     pick = (lane == col + 48 * piece + 24 * high).astype(F32).astype(BF16)
     x, z = place[0], place[1]
+    rows = jnp.concatenate([block[...] for block in blocks], axis=0)
+    wide = jnp.dot(rows, pick, preferred_element_type=F32)
     for dz in range(8):
-        wide = jnp.dot(blocks[dz][...], pick, preferred_element_type=F32).astype(BF16)
         for dx in range(4):
             at = lax.rem(x + dx, 4) * 8 + lax.rem(z + dz, 8)
-            out[at] = wide[dx * 40 : dx * 40 + 40]
+            first = dz * 160 + dx * 40
+            out[at] = wide[first : first + 40].astype(BF16)
     write_tables(place, inverse, cos_out, sin_out)
 
 
@@ -230,19 +237,23 @@
     )
 
     blocks = pixels.reshape(32, 4, -1)
-    local_pixels = lax.all_to_all(blocks, "dp", 0, 0, tiled=True).reshape(128, -1)
+    local_pixels = lax.all_to_all(blocks, "dp", 0, 0, tiled=True)
 
     slices = [lax.dynamic_slice_in_dim(qkv_weight, k * D + seq * OWN, OWN, 1) for k in range(3)]
     mine = after(jnp.concatenate(slices, axis=1), blocks)
     xs = [mine] + [from_dp(mine, d, 0) for d in (1, 2, 3)]
-    z0 = pl.pallas_call(
+    half = lax.dynamic_slice_in_dim(out_weight, c * 640, 640, 1)
+    z0, half = pl.pallas_call(
         stack_kernel,
-        out_shape=jax.ShapeDtypeStruct((160, 3 * OWN), BF16),
-        in_specs=[BLK] * 4,
-        out_specs=VM,
+        out_shape=(
+            jax.ShapeDtypeStruct((160, 3 * OWN), BF16),
+            jax.ShapeDtypeStruct((8, 40, 640), BF16),
+        ),
+        in_specs=[BLK] * 5,
+        out_specs=(VM,) * 2,
         compiler_params=params(4),
         name="stack",
-    )(*xs)
+    )(*xs, half)
     z1, z7 = from_dp(z0, 0, 1), from_dp(z0, 0, 7)
     z2, z6 = from_dp(z1, 0, 1), from_dp(z7, 0, 7)
 
@@ -262,7 +273,6 @@
     z2, z6 = after(z2, normed), after(z6, normed)
     z3, z5 = from_dp(z2, 0, 1), from_dp(z6, 0, 7)
     z4 = from_dp(z3, 0, 1)
-    half = for_each(lax.dynamic_slice_in_dim(out_weight, c * 640, 640, 1), Z_GROUPS)
     column = exchange(after(half, normed, z1, z7), Z_GROUPS)
     column = for_each(column.reshape(320, 640), X_GROUPS)
     o_own = exchange(column, X_GROUPS).reshape(8, OWN, 640)

time: 98.9 us -> 97.4 us (0.985)
  local copies, waits for them, and re-layouts: 8.76 us -> 7.17 us
    reshape x1 -> x0, local copies, waits for them, and re-layouts: 1.1 us -> none  [per_device(): lax.all_to_all(blocks, 'dp', 0, 0, tiled=True).reshape(128, -1)]
    broadcast_in_dim x2 -> x1, local copies, waits for them, and re-layouts: 2.09 us -> 1.34 us  [for_each(): return jnp.broadcast_to(value[None], (len(groups[0]), *value.shape))]
    unnamed x25 -> x17, local copies, waits for them, and re-layouts: 2.77 us -> 3.04 us
  transfers between devices with their start and end apart: 28 -> 28, of which waited for: 14 -> 14; matrix products, arithmetic and copies ran while one was open for 5% -> 4% of each run, Pallas kernels for 12% -> 12%
where the time goes in v4:
time: 97.4 us; the launch traced here: 96.9 us
  starting transfers between devices  51.1 us (52%)
  waiting for transfers between devices  23.9 us (25%)
  Pallas kernels  14.4 us (15%)
  local copies, waits for them, and re-layouts  7.17 us (7%)
    ppermute x10, starting transfers between devices, from_dp(): return lax.ppermute(value, 'dp', dp_shift(dx, dz))  15.8 us
    ppermute x10, waiting for transfers between devices, from_dp(): return lax.ppermute(value, 'dp', dp_shift(dx, dz))  13.8 us
    all_to_all x1, starting transfers between devices, per_device(): local_pixels = lax.all_to_all(blocks, 'dp', 0, 0, tiled=True)  11.9 us
    ppermute x9, starting transfers between devices, swap(): return lax.ppermute(value, 'seq', SWAP)  8.26 us
    ppermute x6, starting transfers between devices, from_seq(): return lax.ppermute(value, 'seq', seq_shift(dy))  7.64 us
    all_to_all x2, starting transfers between devices, exchange(): lax.all_to_all(value, 'dp', 0, 0, tiled=True, axis_index_groups=groups)  7.54 us
    pallas_call x1, Pallas kernels, per_device(): pl.pallas_call(attend_kernel, out_shape=(jax.ShapeDtypeStruct((128, 2 * O...  7.34 us
    ppermute x6, waiting for transfers between devices, from_seq(): return lax.ppermute(value, 'seq', seq_shift(dy))  6.1 us
  transfers between devices with their start and end apart: 28, of which 14 were waited for; matrix products, arithmetic and copies ran while one was open for 4% of the time, Pallas kernels for 12%

profile of v4, /device:TPU:1, one launch (start us, length us, event | category | flops | bytes accessed | tf_op | source)
XLA Modules:
  0.0 96.9 jit_solution(2741567192886521647)
XLA Ops:
  0.0 1.2 %copy.13 = bf16[128,1176]{1,0:T(8,128)(2,1)S(1)} copy(bf16[128,1176]{0,1:T(8,128)(2,1)} %param.11) | data formatting | bytes 602112 | tf_op args[0]
  1.2 0.8 reshape.10
  2.0 11.9 %all-to-all-start = ((bf16[32,4,1176]{2,1,0:T(4,128)(2,1)}), bf16[32,4,1176]{2,1,0:T(4,128)(2,1)S(1)}, u32[]{:S(2)}, u32[]{:S(2)}) async-start(bf16[32,4,1176]{2,1,0:T(4,128)(2,1)} %reshape.10), calls=%async_computation | async-start | bytes 655360 | tf_op jit(solution)/shard_map/all_to_all | solution.py:240
  13.9 0.9 constant_dynamic-slice_fusion.3
  14.8 0.1 pad_maximum_fusion.b0
  14.9 2.6 %collective-permute-start.7 = (bf16[40,480]{1,0:T(8,128)(2,1)S(1)}, bf16[40,480]{1,0:T(8,128)(2,1)S(1)}, u32[]{:S(2)}, u32[]{:S(2)}) collective-permute-start(bf16[40,480]{1,0:T(8,128)(2,1)S(1)} %pad_maximum_fusion.b0), channel_id=1, source_target_pairs={{64,0},{72,8},{80,16},{88,24},{96,32},{104,40},{112,48},{120,56},{... | collective-permute-start | bytes 115208 | tf_op jit(solution)/shard_map/ppermute | solution.py:71
  17.4 0.5 collective-permute-start.8
  18.0 0.6 collective-permute-start.9
  18.6 3.8 %collective-permute-done.8.b2 = bf16[40,480]{1,0:T(8,128)(2,1)S(1)} collective-permute-done((bf16[40,480]{1,0:T(8,128)(2,1)S(1)}, bf16[40,480]{1,0:T(8,128)(2,1)S(1)}, u32[]{:S(2)}, u32[]{:S(2)}) %collective-permute-start.8) | collective-permute-done | bytes 38432 | tf_op jit(solution)/shard_map/ppermute | solution.py:71
  22.4 0.8 collective-permute-done.9.b3
  23.2 0.8 stack.17
  24.0 2.8 %collective-permute-start.10 = (bf16[160,480]{1,0:T(8,128)(2,1)S(1)}, bf16[160,480]{1,0:T(8,128)(2,1)S(1)}, u32[]{:S(2)}, u32[]{:S(2)}) collective-permute-start(bf16[160,480]{1,0:T(8,128)(2,1)S(1)} %get-tuple-element.27.refs_0_), channel_id=1, source_target_pairs={{8,0},{16,8},{24,16},{32,24},{40,32},{48,40},{56,48},{0,56},{72,64... | collective-permute-start | bytes 460808 | tf_op jit(solution)/shard_map/ppermute | solution.py:71
  26.8 0.0 collective-permute-start.11
  26.8 0.0 all-to-all-done.px
  26.9 0.0 copy-start.1
  26.9 1.8 %copy-done.1 = bf16[1176,1280]{1,0:T(8,128)(2,1)S(1)} copy-done((bf16[1176,1280]{1,0:T(8,128)(2,1)S(1)}, bf16[1176,1280]{1,0:T(8,128)(2,1)}, u32[]{:S(2)}) %copy-start.1) | copy-done | bytes 3010584
  28.7 1.6 %embed.1 = (bf16[128,1280]{1,0:T(8,128)(2,1)S(1)}, bf16[128,1280]{1,0:T(8,128)(2,1)}) custom-call(bf16[32,4,1176]{2,1,0:T(4,128)(2,1)S(1)} %all-to-all-done.px, bf16[1176,1280]{1,0:T(8,128)(2,1)S(1)} %copy-done.1, f32[1280]{0:T(1024)S(1)} %copy-done.2, f32[1280]{0:T(1024)S(1)} %copy-done.3), custom_call_target="tpu_custom_call" | custom-call | tf_op jit(solution)/shard_map/embed/pallas_call | solution.py:260
  30.3 0.0 collective-permute-done.10.refs_1_
  30.3 1.9 %collective-permute-done.11.refs_7_ = bf16[160,480]{1,0:T(8,128)(2,1)S(1)} collective-permute-done((bf16[160,480]{1,0:T(8,128)(2,1)S(1)}, bf16[160,480]{1,0:T(8,128)(2,1)S(1)}, u32[]{:S(2)}, u32[]{:S(2)}) %collective-permute-start.11) | collective-permute-done | bytes 153632 | tf_op jit(solution)/shard_map/ppermute | solution.py:71
  32.2 3.8 %all-to-all-start.1 = ((bf16[8,40,640]{2,1,0:T(8,128)(2,1)}), bf16[8,40,640]{2,1,0:T(8,128)(2,1)S(1)}, u32[]{:S(2)}, u32[]{:S(2)}) async-start(bf16[8,40,640]{2,1,0:T(8,128)(2,1)} %get-tuple-element.26), calls=%async_computation.1 | async-start | bytes 819200 | tf_op jit(solution)/shard_map/all_to_all | solution.py:59
  36.1 2.7 %collective-permute-start.1 = (bf16[128,1280]{1,0:T(8,128)(2,1)}, bf16[128,1280]{1,0:T(8,128)(2,1)}, u32[]{:S(2)}, u32[]{:S(2)}) collective-permute-start(bf16[128,1280]{1,0:T(8,128)(2,1)} %get-tuple-element.22.refs_0_), channel_id=1, source_target_pairs={{2,0},{3,1},{4,2},{5,3},{6,4},{7,5},{0,6},{1,7},{10,8},{11,9},{12,... | collective-permute-start | bytes 983048 | tf_op jit(solution)/shard_map/ppermute | solution.py:63
  38.8 0.3 collective-permute-start.3
  39.1 0.7 collective-permute-start.5
  39.8 2.7 %collective-permute-start.12 = (bf16[160,480]{1,0:T(8,128)(2,1)S(1)}, bf16[160,480]{1,0:T(8,128)(2,1)S(1)}, u32[]{:S(2)}, u32[]{:S(2)}) collective-permute-start(bf16[160,480]{1,0:T(8,128)(2,1)S(1)} %collective-permute-done.10.refs_1_), channel_id=1, source_target_pairs={{8,0},{16,8},{24,16},{32,24},{40,32},{48,40},{56,48},{0,56},{72,64... | collective-permute-start | bytes 460808 | tf_op jit(solution)/shard_map/ppermute | solution.py:71
  42.5 4.5 %collective-permute-done.12.refs_2_ = bf16[160,480]{1,0:T(8,128)(2,1)S(1)} collective-permute-done((bf16[160,480]{1,0:T(8,128)(2,1)S(1)}, bf16[160,480]{1,0:T(8,128)(2,1)S(1)}, u32[]{:S(2)}, u32[]{:S(2)}) %collective-permute-start.12) | collective-permute-done | bytes 153632 | tf_op jit(solution)/shard_map/ppermute | solution.py:71
  47.0 3.2 %collective-permute-start.13 = (bf16[160,480]{1,0:T(8,128)(2,1)S(1)}, bf16[160,480]{1,0:T(8,128)(2,1)S(1)}, u32[]{:S(2)}, u32[]{:S(2)}) collective-permute-start(bf16[160,480]{1,0:T(8,128)(2,1)S(1)} %collective-permute-done.12.refs_2_), channel_id=1, source_target_pairs={{8,0},{16,8},{24,16},{32,24},{40,32},{48,40},{56,48},{0,56},{72,64... | collective-permute-start | bytes 460808 | tf_op jit(solution)/shard_map/ppermute | solution.py:71
  50.2 0.5 collective-permute-done.15.refs_6_
  50.8 0.1 concatenate.9.place
  50.8 2.3 %collective-permute-done.13.refs_3_ = bf16[160,480]{1,0:T(8,128)(2,1)S(1)} collective-permute-done((bf16[160,480]{1,0:T(8,128)(2,1)S(1)}, bf16[160,480]{1,0:T(8,128)(2,1)S(1)}, u32[]{:S(2)}, u32[]{:S(2)}) %collective-permute-start.13) | collective-permute-done | bytes 153632 | tf_op jit(solution)/shard_map/ppermute | solution.py:71
  53.1 5.1 %collective-permute-start = (bf16[128,1280]{1,0:T(8,128)(2,1)}, bf16[128,1280]{1,0:T(8,128)(2,1)}, u32[]{:S(2)}, u32[]{:S(2)}) collective-permute-start(bf16[128,1280]{1,0:T(8,128)(2,1)} %get-tuple-element.22.refs_0_), channel_id=1, source_target_pairs={{0,1},{1,0},{2,3},{3,2},{4,5},{5,4},{6,7},{7,6},{8,9},{9,8},{10,11... | collective-permute-start | bytes 983048 | tf_op jit(solution)/shard_map/ppermute | solution.py:67
  58.2 0.0 collective-permute-done.1.refs_2_
  58.2 0.0 collective-permute-start.2
  58.2 0.0 collective-permute-done.3.refs_4_
  58.2 0.5 collective-permute-start.4
  58.7 0.3 collective-permute-start.6
  59.0 0.8 fusion
  59.8 0.0 collective-permute-done.16.refs_5_
  59.9 3.3 %collective-permute-start.14 = (bf16[160,480]{1,0:T(8,128)(2,1)S(1)}, bf16[160,480]{1,0:T(8,128)(2,1)S(1)}, u32[]{:S(2)}, u32[]{:S(2)}) collective-permute-start(bf16[160,480]{1,0:T(8,128)(2,1)S(1)} %collective-permute-done.13.refs_3_), channel_id=1, source_target_pairs={{8,0},{16,8},{24,16},{32,24},{40,32},{48,40},{56,48},{0,56},{72,64... | collective-permute-start | bytes 460808 | tf_op jit(solution)/shard_map/ppermute | solution.py:71
  63.2 0.1 fusion.1
  63.3 0.1 concatenate.11.refs_9_
  63.4 0.0 all-to-all-done.1
  63.4 1.3 %broadcast_in_dim.11 = bf16[4,320,640]{2,1,0:T(8,128)(2,1)} broadcast(bf16[320,640]{1,0:T(8,128)(2,1)S(1)} %bitcast.12), dimensions={1,2} | broadcast | bytes 2048000 | tf_op jit(solution)/shard_map/broadcast_in_dim | solution.py:55
  64.7 3.7 %all-to-all-start.2 = ((bf16[4,320,640]{2,1,0:T(8,128)(2,1)}), bf16[4,320,640]{2,1,0:T(8,128)(2,1)S(1)}, u32[]{:S(2)}, u32[]{:S(2)}) async-start(bf16[4,320,640]{2,1,0:T(8,128)(2,1)} %broadcast_in_dim.11), calls=%async_computation.2 | async-start | bytes 3276800 | tf_op jit(solution)/shard_map/all_to_all | solution.py:59
  68.4 2.3 %lay.1 = (bf16[32,40,768]{2,1,0:T(8,128)(2,1)S(1)}, f32[8,128,128]{2,1,0:T(8,128)S(1)}, f32[8,128,128]{2,1,0:T(8,128)S(1)}) custom-call(s32[16]{0:T(128)S(1)} %concatenate.9.place, f32[1,128]{1,0:T(1,128)S(1)} %copy-done.5, bf16[160,480]{1,0:T(8,128)(2,1)S(1)} %get-tuple-element.27.refs_0_, bf16[160,480]{1,0:T(8,128)(2,1)S(1)} %collective-permute-done.10.refs_1_, ...), custom_call_target="tpu_custom_call" | custom-call | tf_op jit(solution)/shard_map/lay/pallas_call | solution.py:280
  70.7 0.0 collective-permute-done.refs_1_
  70.7 0.0 collective-permute-done.6.refs_7_
  70.7 0.0 copy-start.4
  70.7 7.3 %attend.1 = (bf16[128,320]{1,0:T(8,128)(2,1)S(1)}, bf16[128,320]{1,0:T(8,128)(2,1)S(1)}, bf16[128,320]{1,0:T(8,128)(2,1)S(1)}, bf16[128,320]{1,0:T(8,128)(2,1)S(1)}) custom-call(s32[16]{0:T(128)S(1)} %concatenate.9.place, bf16[128,1280]{1,0:T(8,128)(2,1)} %get-tuple-element.22.refs_0_, bf16[128,1280]{1,0:T(8,128)(2,1)} %collective-permute-done.refs_1_, ...), custom_call_target="tpu_custom_call" | custom-call | flops 60000002048 | tf_op jit(solution)/shard_map/attend/pallas_call | solution.py:301
  78.1 1.9 %collective-permute-start.17 = (bf16[128,320]{1,0:T(8,128)(2,1)S(1)}, bf16[128,320]{1,0:T(8,128)(2,1)S(1)}, u32[]{:S(2)}, u32[]{:S(2)}) collective-permute-start(bf16[128,320]{1,0:T(8,128)(2,1)S(1)} %get-tuple-element.34), channel_id=1, source_target_pairs={{2,0},{3,1},{4,2},{5,3},{6,4},{7,5},{0,6},{1,7},{10,8},{11,9},{12,... | collective-permute-start | bytes 245768 | tf_op jit(solution)/shard_map/ppermute | solution.py:63
  80.0 2.0 %collective-permute-start.18 = (bf16[128,320]{1,0:T(8,128)(2,1)S(1)}, bf16[128,320]{1,0:T(8,128)(2,1)S(1)}, u32[]{:S(2)}, u32[]{:S(2)}) collective-permute-start(bf16[128,320]{1,0:T(8,128)(2,1)S(1)} %get-tuple-element.35), channel_id=1, source_target_pairs={{4,0},{5,1},{6,2},{7,3},{0,4},{1,5},{2,6},{3,7},{12,8},{13,9},{14,... | collective-permute-start | bytes 245768 | tf_op jit(solution)/shard_map/ppermute | solution.py:63
  81.9 0.9 collective-permute-done.17.refs_1_
  82.9 2.4 %collective-permute-done.18.refs_2_ = bf16[128,320]{1,0:T(8,128)(2,1)S(1)} collective-permute-done((bf16[128,320]{1,0:T(8,128)(2,1)S(1)}, bf16[128,320]{1,0:T(8,128)(2,1)S(1)}, u32[]{:S(2)}, u32[]{:S(2)}) %collective-permute-start.18) | collective-permute-done | bytes 81952 | tf_op jit(solution)/shard_map/ppermute | solution.py:63
  85.2 2.8 %collective-permute-done.19.refs_3_ = bf16[128,320]{1,0:T(8,128)(2,1)S(1)} collective-permute-done((bf16[128,320]{1,0:T(8,128)(2,1)S(1)}, bf16[128,320]{1,0:T(8,128)(2,1)S(1)}, u32[]{:S(2)}, u32[]{:S(2)}) %collective-permute-start.19) | collective-permute-done | bytes 81952 | tf_op jit(solution)/shard_map/ppermute | solution.py:63
  88.0 1.3 %all-to-all-done.2 = bf16[4,320,640]{2,1,0:T(8,128)(2,1)S(1)} async-done(((bf16[4,320,640]{2,1,0:T(8,128)(2,1)}), bf16[4,320,640]{2,1,0:T(8,128)(2,1)S(1)}, u32[]{:S(2)}, u32[]{:S(2)}) %all-to-all-start.2) | async-done | bytes 1638432 | tf_op jit(solution)/shard_map/all_to_all | solution.py:59
  89.4 1.4 %collective-permute-start.24 = (bf16[8,160,640]{2,1,0:T(8,128)(2,1)S(1)}, bf16[8,160,640]{2,1,0:T(8,128)(2,1)S(1)}, u32[]{:S(2)}, u32[]{:S(2)}) collective-permute-start(bf16[8,160,640]{2,1,0:T(8,128)(2,1)S(1)} %bitcast.9), channel_id=1, source_target_pairs={{0,1},{1,0},{2,3},{3,2},{4,5},{5,4},{6,7},{7,6},{8,9},{9,8},{10,11... | collective-permute-start | bytes 4915208 | tf_op jit(solution)/shard_map/ppermute | solution.py:67
  90.7 0.0 collective-permute-start.20
  90.7 0.5 collective-permute-start.21
  91.3 0.0 collective-permute-start.22
  91.3 0.5 collective-permute-start.23
  91.8 2.2 %collective-permute-done.20.refs_4_ = bf16[128,320]{1,0:T(8,128)(2,1)S(1)} collective-permute-done((bf16[128,320]{1,0:T(8,128)(2,1)S(1)}, bf16[128,320]{1,0:T(8,128)(2,1)S(1)}, u32[]{:S(2)}, u32[]{:S(2)}) %collective-permute-start.20) | collective-permute-done | bytes 81952 | tf_op jit(solution)/shard_map/ppermute | solution.py:67
  94.0 0.1 collective-permute-done.21.refs_5_
  94.2 0.1 collective-permute-done.22.refs_6_
  94.3 0.1 collective-permute-done.23.refs_7_
  94.4 2.4 %project.1 = bf16[128,1280]{1,0:T(8,128)(2,1)} custom-call(s32[16]{0:T(128)S(1)} %concatenate.9.place, bf16[128,320]{1,0:T(8,128)(2,1)S(1)} %get-tuple-element.33.refs_0_, bf16[128,320]{1,0:T(8,128)(2,1)S(1)} %collective-permute-done.17.refs_1_, bf16[128,320]{1,0:T(8,128)(2,1)S(1)} %collective-permute-done.18.refs_2_, ...), custom_call_target="tpu_custom_call" | custom-call | tf_op jit(solution)/shard_map/project/pallas_call | solution.py:321
  (26 shorter events, 0.1 us)
Async XLA Ops:
  0.0 18.5 %copy-start = (bf16[40,1280]{1,0:T(8,128)(2,1)S(1)}, bf16[40,1280]{1,0:T(8,128)(2,1)}, u32[]{:S(2)}) copy-start(bf16[40,1280]{1,0:T(8,128)(2,1)} %param.17) | copy-start | bytes 307204
  0.0 26.8 %copy-start.2 = (f32[1280]{0:T(1024)S(1)}, f32[1280]{0:T(1024)}, u32[]{:S(2)}) copy-start(f32[1280]{0:T(1024)} %gain.1) | copy-start | bytes 15364
  0.0 26.8 %copy-start.3 = (f32[1280]{0:T(1024)S(1)}, f32[1280]{0:T(1024)}, u32[]{:S(2)}) copy-start(f32[1280]{0:T(1024)} %bias.1) | copy-start | bytes 15364
  2.0 24.9 %all-to-all-start = ((bf16[32,4,1176]{2,1,0:T(4,128)(2,1)}), bf16[32,4,1176]{2,1,0:T(4,128)(2,1)S(1)}, u32[]{:S(2)}, u32[]{:S(2)}) async-start(bf16[32,4,1176]{2,1,0:T(4,128)(2,1)} %reshape.10), calls=%async_computation | async-start | bytes 655360 | tf_op jit(solution)/shard_map/all_to_all | solution.py:240
  14.9 3.7 %collective-permute-start.7 = (bf16[40,480]{1,0:T(8,128)(2,1)S(1)}, bf16[40,480]{1,0:T(8,128)(2,1)S(1)}, u32[]{:S(2)}, u32[]{:S(2)}) collective-permute-start(bf16[40,480]{1,0:T(8,128)(2,1)S(1)} %pad_maximum_fusion.b0), channel_id=1, source_target_pairs={{64,0},{72,8},{80,16},{88,24},{96,32},{104,40},{112,48},{120,56},{... | collective-permute-start | bytes 115208 | tf_op jit(solution)/shard_map/ppermute | solution.py:71
  17.4 5.0 %collective-permute-start.8 = (bf16[40,480]{1,0:T(8,128)(2,1)S(1)}, bf16[40,480]{1,0:T(8,128)(2,1)S(1)}, u32[]{:S(2)}, u32[]{:S(2)}) collective-permute-start(bf16[40,480]{1,0:T(8,128)(2,1)S(1)} %pad_maximum_fusion.b0), channel_id=1, source_target_pairs={{128,0},{136,8},{144,16},{152,24},{160,32},{168,40},{176,48},{184,... | collective-permute-start | bytes 115208 | tf_op jit(solution)/shard_map/ppermute | solution.py:71
  18.0 5.2 %collective-permute-start.9 = (bf16[40,480]{1,0:T(8,128)(2,1)S(1)}, bf16[40,480]{1,0:T(8,128)(2,1)S(1)}, u32[]{:S(2)}, u32[]{:S(2)}) collective-permute-start(bf16[40,480]{1,0:T(8,128)(2,1)S(1)} %pad_maximum_fusion.b0), channel_id=1, source_target_pairs={{192,0},{200,8},{208,16},{216,24},{224,32},{232,40},{240,48},{248,... | collective-permute-start | bytes 115208 | tf_op jit(solution)/shard_map/ppermute | solution.py:71
  24.0 26.7 %copy-start.6 = (s32[1,3]{1,0:T(1,128)S(1)}, s32[1,3]{1,0:T(1,128)}, u32[]{:S(2)}) copy-start(s32[1,3]{1,0:T(1,128)} %param.19) | copy-start | bytes 40
  24.0 26.8 %copy-start.7 = (s32[1,3]{1,0:T(1,128)S(1)}, s32[1,3]{1,0:T(1,128)}, u32[]{:S(2)}) copy-start(s32[1,3]{1,0:T(1,128)} %param.20) | copy-start | bytes 40
  24.0 6.3 %collective-permute-start.10 = (bf16[160,480]{1,0:T(8,128)(2,1)S(1)}, bf16[160,480]{1,0:T(8,128)(2,1)S(1)}, u32[]{:S(2)}, u32[]{:S(2)}) collective-permute-start(bf16[160,480]{1,0:T(8,128)(2,1)S(1)} %get-tuple-element.27.refs_0_), channel_id=1, source_target_pairs={{8,0},{16,8},{24,16},{32,24},{40,32},{48,40},{56,48},{0,56},{72,64... | collective-permute-start | bytes 460808 | tf_op jit(solution)/shard_map/ppermute | solution.py:71
  26.8 5.4 %collective-permute-start.11 = (bf16[160,480]{1,0:T(8,128)(2,1)S(1)}, bf16[160,480]{1,0:T(8,128)(2,1)S(1)}, u32[]{:S(2)}, u32[]{:S(2)}) collective-permute-start(bf16[160,480]{1,0:T(8,128)(2,1)S(1)} %get-tuple-element.27.refs_0_), channel_id=1, source_target_pairs={{56,0},{0,8},{8,16},{16,24},{24,32},{32,40},{40,48},{48,56},{120,6... | collective-permute-start | bytes 460808 | tf_op jit(solution)/shard_map/ppermute | solution.py:71
  26.9 1.9 %copy-start.1 = (bf16[1176,1280]{1,0:T(8,128)(2,1)S(1)}, bf16[1176,1280]{1,0:T(8,128)(2,1)}, u32[]{:S(2)}) copy-start(bf16[1176,1280]{1,0:T(8,128)(2,1)} %pw.1) | copy-start | bytes 9031684
  32.2 31.1 %all-to-all-start.1 = ((bf16[8,40,640]{2,1,0:T(8,128)(2,1)}), bf16[8,40,640]{2,1,0:T(8,128)(2,1)S(1)}, u32[]{:S(2)}, u32[]{:S(2)}) async-start(bf16[8,40,640]{2,1,0:T(8,128)(2,1)} %get-tuple-element.26), calls=%async_computation.1 | async-start | bytes 819200 | tf_op jit(solution)/shard_map/all_to_all | solution.py:59
  36.1 22.2 %collective-permute-start.1 = (bf16[128,1280]{1,0:T(8,128)(2,1)}, bf16[128,1280]{1,0:T(8,128)(2,1)}, u32[]{:S(2)}, u32[]{:S(2)}) collective-permute-start(bf16[128,1280]{1,0:T(8,128)(2,1)} %get-tuple-element.22.refs_0_), channel_id=1, source_target_pairs={{2,0},{3,1},{4,2},{5,3},{6,4},{7,5},{0,6},{1,7},{10,8},{11,9},{12,... | collective-permute-start | bytes 983048 | tf_op jit(solution)/shard_map/ppermute | solution.py:63
  38.8 19.4 %collective-permute-start.3 = (bf16[128,1280]{1,0:T(8,128)(2,1)}, bf16[128,1280]{1,0:T(8,128)(2,1)}, u32[]{:S(2)}, u32[]{:S(2)}) collective-permute-start(bf16[128,1280]{1,0:T(8,128)(2,1)} %get-tuple-element.22.refs_0_), channel_id=1, source_target_pairs={{4,0},{5,1},{6,2},{7,3},{0,4},{1,5},{2,6},{3,7},{12,8},{13,9},{14,... | collective-permute-start | bytes 983048 | tf_op jit(solution)/shard_map/ppermute | solution.py:63
  39.1 19.6 %collective-permute-start.5 = (bf16[128,1280]{1,0:T(8,128)(2,1)}, bf16[128,1280]{1,0:T(8,128)(2,1)}, u32[]{:S(2)}, u32[]{:S(2)}) collective-permute-start(bf16[128,1280]{1,0:T(8,128)(2,1)} %get-tuple-element.22.refs_0_), channel_id=1, source_target_pairs={{6,0},{7,1},{0,2},{1,3},{2,4},{3,5},{4,6},{5,7},{14,8},{15,9},{8,1... | collective-permute-start | bytes 983048 | tf_op jit(solution)/shard_map/ppermute | solution.py:63
  39.8 7.2 %collective-permute-start.12 = (bf16[160,480]{1,0:T(8,128)(2,1)S(1)}, bf16[160,480]{1,0:T(8,128)(2,1)S(1)}, u32[]{:S(2)}, u32[]{:S(2)}) collective-permute-start(bf16[160,480]{1,0:T(8,128)(2,1)S(1)} %collective-permute-done.10.refs_1_), channel_id=1, source_target_pairs={{8,0},{16,8},{24,16},{32,24},{40,32},{48,40},{56,48},{0,56},{72,64... | collective-permute-start | bytes 460808 | tf_op jit(solution)/shard_map/ppermute | solution.py:71
  42.5 8.2 %collective-permute-start.15 = (bf16[160,480]{1,0:T(8,128)(2,1)S(1)}, bf16[160,480]{1,0:T(8,128)(2,1)S(1)}, u32[]{:S(2)}, u32[]{:S(2)}) collective-permute-start(bf16[160,480]{1,0:T(8,128)(2,1)S(1)} %collective-permute-done.11.refs_7_), channel_id=1, source_target_pairs={{56,0},{0,8},{8,16},{16,24},{24,32},{32,40},{40,48},{48,56},{120,6... | collective-permute-start | bytes 460808 | tf_op jit(solution)/shard_map/ppermute | solution.py:71
  47.0 6.1 %collective-permute-start.13 = (bf16[160,480]{1,0:T(8,128)(2,1)S(1)}, bf16[160,480]{1,0:T(8,128)(2,1)S(1)}, u32[]{:S(2)}, u32[]{:S(2)}) collective-permute-start(bf16[160,480]{1,0:T(8,128)(2,1)S(1)} %collective-permute-done.12.refs_2_), channel_id=1, source_target_pairs={{8,0},{16,8},{24,16},{32,24},{40,32},{48,40},{56,48},{0,56},{72,64... | collective-permute-start | bytes 460808 | tf_op jit(solution)/shard_map/ppermute | solution.py:71
  50.7 9.1 %collective-permute-start.16 = (bf16[160,480]{1,0:T(8,128)(2,1)S(1)}, bf16[160,480]{1,0:T(8,128)(2,1)S(1)}, u32[]{:S(2)}, u32[]{:S(2)}) collective-permute-start(bf16[160,480]{1,0:T(8,128)(2,1)S(1)} %collective-permute-done.15.refs_6_), channel_id=1, source_target_pairs={{56,0},{0,8},{8,16},{16,24},{24,32},{32,40},{40,48},{48,56},{120,6... | collective-permute-start | bytes 460808 | tf_op jit(solution)/shard_map/ppermute | solution.py:71
  53.1 17.6 %collective-permute-start = (bf16[128,1280]{1,0:T(8,128)(2,1)}, bf16[128,1280]{1,0:T(8,128)(2,1)}, u32[]{:S(2)}, u32[]{:S(2)}) collective-permute-start(bf16[128,1280]{1,0:T(8,128)(2,1)} %get-tuple-element.22.refs_0_), channel_id=1, source_target_pairs={{0,1},{1,0},{2,3},{3,2},{4,5},{5,4},{6,7},{7,6},{8,9},{9,8},{10,11... | collective-permute-start | bytes 983048 | tf_op jit(solution)/shard_map/ppermute | solution.py:67
  58.2 12.5 %collective-permute-start.2 = (bf16[128,1280]{1,0:T(8,128)(2,1)}, bf16[128,1280]{1,0:T(8,128)(2,1)}, u32[]{:S(2)}, u32[]{:S(2)}) collective-permute-start(bf16[128,1280]{1,0:T(8,128)(2,1)} %collective-permute-done.1.refs_2_), channel_id=1, source_target_pairs={{0,1},{1,0},{2,3},{3,2},{4,5},{5,4},{6,7},{7,6},{8,9},{9,8},{10,11... | collective-permute-start | bytes 983048 | tf_op jit(solution)/shard_map/ppermute | solution.py:67
  58.2 12.5 %collective-permute-start.4 = (bf16[128,1280]{1,0:T(8,128)(2,1)}, bf16[128,1280]{1,0:T(8,128)(2,1)}, u32[]{:S(2)}, u32[]{:S(2)}) collective-permute-start(bf16[128,1280]{1,0:T(8,128)(2,1)} %collective-permute-done.3.refs_4_), channel_id=1, source_target_pairs={{0,1},{1,0},{2,3},{3,2},{4,5},{5,4},{6,7},{7,6},{8,9},{9,8},{10,11... | collective-permute-start | bytes 983048 | tf_op jit(solution)/shard_map/ppermute | solution.py:67
  58.7 12.0 %collective-permute-start.6 = (bf16[128,1280]{1,0:T(8,128)(2,1)}, bf16[128,1280]{1,0:T(8,128)(2,1)}, u32[]{:S(2)}, u32[]{:S(2)}) collective-permute-start(bf16[128,1280]{1,0:T(8,128)(2,1)} %collective-permute-done.5.refs_6_), channel_id=1, source_target_pairs={{0,1},{1,0},{2,3},{3,2},{4,5},{5,4},{6,7},{7,6},{8,9},{9,8},{10,11... | collective-permute-start | bytes 983048 | tf_op jit(solution)/shard_map/ppermute | solution.py:67
  59.9 8.6 %collective-permute-start.14 = (bf16[160,480]{1,0:T(8,128)(2,1)S(1)}, bf16[160,480]{1,0:T(8,128)(2,1)S(1)}, u32[]{:S(2)}, u32[]{:S(2)}) collective-permute-start(bf16[160,480]{1,0:T(8,128)(2,1)S(1)} %collective-permute-done.13.refs_3_), channel_id=1, source_target_pairs={{8,0},{16,8},{24,16},{32,24},{40,32},{48,40},{56,48},{0,56},{72,64... | collective-permute-start | bytes 460808 | tf_op jit(solution)/shard_map/ppermute | solution.py:71
  64.7 3.7 %copy-start.5 = (f32[1,128]{1,0:T(1,128)S(1)}, f32[1,128]{1,0:T(1,128)}, u32[]{:S(2)}) copy-start(f32[1,128]{1,0:T(1,128)} %constant.75.clone.inverse) | copy-start | bytes 1540
  64.7 24.7 %all-to-all-start.2 = ((bf16[4,320,640]{2,1,0:T(8,128)(2,1)}), bf16[4,320,640]{2,1,0:T(8,128)(2,1)S(1)}, u32[]{:S(2)}, u32[]{:S(2)}) async-start(bf16[4,320,640]{2,1,0:T(8,128)(2,1)} %broadcast_in_dim.11), calls=%async_computation.2 | async-start | bytes 3276800 | tf_op jit(solution)/shard_map/all_to_all | solution.py:59
  70.7 23.7 %copy-start.4 = (f32[1280]{0:T(1024)S(1)}, f32[1280]{0:T(1024)}, u32[]{:S(2)}) copy-start(f32[1280]{0:T(1024)} %refs_11_.1) | copy-start | bytes 15364
  78.1 4.8 %collective-permute-start.17 = (bf16[128,320]{1,0:T(8,128)(2,1)S(1)}, bf16[128,320]{1,0:T(8,128)(2,1)S(1)}, u32[]{:S(2)}, u32[]{:S(2)}) collective-permute-start(bf16[128,320]{1,0:T(8,128)(2,1)S(1)} %get-tuple-element.34), channel_id=1, source_target_pairs={{2,0},{3,1},{4,2},{5,3},{6,4},{7,5},{0,6},{1,7},{10,8},{11,9},{12,... | collective-permute-start | bytes 245768 | tf_op jit(solution)/shard_map/ppermute | solution.py:63
  80.0 5.3 %collective-permute-start.18 = (bf16[128,320]{1,0:T(8,128)(2,1)S(1)}, bf16[128,320]{1,0:T(8,128)(2,1)S(1)}, u32[]{:S(2)}, u32[]{:S(2)}) collective-permute-start(bf16[128,320]{1,0:T(8,128)(2,1)S(1)} %get-tuple-element.35), channel_id=1, source_target_pairs={{4,0},{5,1},{6,2},{7,3},{0,4},{1,5},{2,6},{3,7},{12,8},{13,9},{14,... | collective-permute-start | bytes 245768 | tf_op jit(solution)/shard_map/ppermute | solution.py:63
  81.9 6.1 %collective-permute-start.19 = (bf16[128,320]{1,0:T(8,128)(2,1)S(1)}, bf16[128,320]{1,0:T(8,128)(2,1)S(1)}, u32[]{:S(2)}, u32[]{:S(2)}) collective-permute-start(bf16[128,320]{1,0:T(8,128)(2,1)S(1)} %get-tuple-element.36), channel_id=1, source_target_pairs={{6,0},{7,1},{0,2},{1,3},{2,4},{3,5},{4,6},{5,7},{14,8},{15,9},{8,1... | collective-permute-start | bytes 245768 | tf_op jit(solution)/shard_map/ppermute | solution.py:63
  89.4 5.1 %collective-permute-start.24 = (bf16[8,160,640]{2,1,0:T(8,128)(2,1)S(1)}, bf16[8,160,640]{2,1,0:T(8,128)(2,1)S(1)}, u32[]{:S(2)}, u32[]{:S(2)}) collective-permute-start(bf16[8,160,640]{2,1,0:T(8,128)(2,1)S(1)} %bitcast.9), channel_id=1, source_target_pairs={{0,1},{1,0},{2,3},{3,2},{4,5},{5,4},{6,7},{7,6},{8,9},{9,8},{10,11... | collective-permute-start | bytes 4915208 | tf_op jit(solution)/shard_map/ppermute | solution.py:67
  90.7 3.3 %collective-permute-start.20 = (bf16[128,320]{1,0:T(8,128)(2,1)S(1)}, bf16[128,320]{1,0:T(8,128)(2,1)S(1)}, u32[]{:S(2)}, u32[]{:S(2)}) collective-permute-start(bf16[128,320]{1,0:T(8,128)(2,1)S(1)} %get-tuple-element.33.refs_0_), channel_id=1, source_target_pairs={{0,1},{1,0},{2,3},{3,2},{4,5},{5,4},{6,7},{7,6},{8,9},{9,8},{10,11... | collective-permute-start | bytes 245768 | tf_op jit(solution)/shard_map/ppermute | solution.py:67
  90.7 3.4 %collective-permute-start.21 = (bf16[128,320]{1,0:T(8,128)(2,1)S(1)}, bf16[128,320]{1,0:T(8,128)(2,1)S(1)}, u32[]{:S(2)}, u32[]{:S(2)}) collective-permute-start(bf16[128,320]{1,0:T(8,128)(2,1)S(1)} %collective-permute-done.17.refs_1_), channel_id=1, source_target_pairs={{0,1},{1,0},{2,3},{3,2},{4,5},{5,4},{6,7},{7,6},{8,9},{9,8},{10,11... | collective-permute-start | bytes 245768 | tf_op jit(solution)/shard_map/ppermute | solution.py:67
  91.3 3.0 %collective-permute-start.22 = (bf16[128,320]{1,0:T(8,128)(2,1)S(1)}, bf16[128,320]{1,0:T(8,128)(2,1)S(1)}, u32[]{:S(2)}, u32[]{:S(2)}) collective-permute-start(bf16[128,320]{1,0:T(8,128)(2,1)S(1)} %collective-permute-done.18.refs_2_), channel_id=1, source_target_pairs={{0,1},{1,0},{2,3},{3,2},{4,5},{5,4},{6,7},{7,6},{8,9},{9,8},{10,11... | collective-permute-start | bytes 245768 | tf_op jit(solution)/shard_map/ppermute | solution.py:67
  91.3 3.2 %collective-permute-start.23 = (bf16[128,320]{1,0:T(8,128)(2,1)S(1)}, bf16[128,320]{1,0:T(8,128)(2,1)S(1)}, u32[]{:S(2)}, u32[]{:S(2)}) collective-permute-start(bf16[128,320]{1,0:T(8,128)(2,1)S(1)} %collective-permute-done.19.refs_3_), channel_id=1, source_target_pairs={{0,1},{1,0},{2,3},{3,2},{4,5},{5,4},{6,7},{7,6},{8,9},{9,8},{10,11... | collective-permute-start | bytes 245768 | tf_op jit(solution)/shard_map/ppermute | solution.py:67

commit v5 on v4

--- a/solution.py
+++ b/solution.py
@@ -316,7 +316,7 @@
     got = [parts[0]] + [from_seq(parts[(4 - d) % 4], d) for d in (1, 2, 3)]
     got_other = [swap(v) for v in got]
 
-    o_other = swap(after(o_own, *got[1:]))
+    o_other = swap(after(o_own, got[1], got[3]))
 
     return pl.pallas_call(
         out_kernel,

time: 97.4 us -> 102 us (1.047)
  waiting for transfers between devices: 23.9 us -> 28.2 us
    all_to_all x2, waiting for transfers between devices: 1.34 us -> 4.44 us  [exchange(): lax.all_to_all(value, 'dp', 0, 0, tiled=True, axis_index_groups=groups)]
    ppermute x6, waiting for transfers between devices: 6.1 us -> 8.65 us  [from_seq(): return lax.ppermute(value, 'seq', seq_shift(dy))]
    ppermute x9, waiting for transfers between devices: 2.68 us -> 1.31 us  [swap(): return lax.ppermute(value, 'seq', SWAP)]
  transfers between devices with their start and end apart: 28 -> 28, of which waited for: 14 -> 12; matrix products, arithmetic and copies ran while one was open for 4% -> 3% of each run, Pallas kernels for 12% -> 12%
where the time goes in v5:
time: 102 us; the launch traced here: 101 us
  starting transfers between devices  51.1 us (50%)
  waiting for transfers between devices  28.2 us (28%)
  Pallas kernels  14.4 us (14%)
  local copies, waits for them, and re-layouts  7.17 us (7%)
    ppermute x10, starting transfers between devices, from_dp(): return lax.ppermute(value, 'dp', dp_shift(dx, dz))  15.8 us
    ppermute x10, waiting for transfers between devices, from_dp(): return lax.ppermute(value, 'dp', dp_shift(dx, dz))  13.8 us
    all_to_all x1, starting transfers between devices, per_device(): local_pixels = lax.all_to_all(blocks, 'dp', 0, 0, tiled=True)  11.9 us
    ppermute x6, waiting for transfers between devices, from_seq(): return lax.ppermute(value, 'seq', seq_shift(dy))  8.65 us
    ppermute x9, starting transfers between devices, swap(): return lax.ppermute(value, 'seq', SWAP)  8.54 us
    all_to_all x2, starting transfers between devices, exchange(): lax.all_to_all(value, 'dp', 0, 0, tiled=True, axis_index_groups=groups)  7.54 us
    ppermute x6, starting transfers between devices, from_seq(): return lax.ppermute(value, 'seq', seq_shift(dy))  7.4 us
    pallas_call x1, Pallas kernels, per_device(): pl.pallas_call(attend_kernel, out_shape=(jax.ShapeDtypeStruct((128, 2 * O...  7.34 us
  transfers between devices with their start and end apart: 28, of which 12 were waited for; matrix products, arithmetic and copies ran while one was open for 3% of the time, Pallas kernels for 12%

profile of v5, /device:TPU:1, one launch (start us, length us, event | category | flops | bytes accessed | tf_op | source)
XLA Modules:
  0.0 101.2 jit_solution(1933800343091597229)
XLA Ops:
  0.0 1.2 %copy.13 = bf16[128,1176]{1,0:T(8,128)(2,1)S(1)} copy(bf16[128,1176]{0,1:T(8,128)(2,1)} %param.11) | data formatting | bytes 602112 | tf_op args[0]
  1.2 0.8 reshape.10
  2.0 11.9 %all-to-all-start = ((bf16[32,4,1176]{2,1,0:T(4,128)(2,1)}), bf16[32,4,1176]{2,1,0:T(4,128)(2,1)S(1)}, u32[]{:S(2)}, u32[]{:S(2)}) async-start(bf16[32,4,1176]{2,1,0:T(4,128)(2,1)} %reshape.10), calls=%async_computation | async-start | bytes 655360 | tf_op jit(solution)/shard_map/all_to_all | solution.py:240
  13.9 0.9 constant_dynamic-slice_fusion.3
  14.8 0.1 pad_maximum_fusion.b0
  14.9 2.6 %collective-permute-start.7 = (bf16[40,480]{1,0:T(8,128)(2,1)S(1)}, bf16[40,480]{1,0:T(8,128)(2,1)S(1)}, u32[]{:S(2)}, u32[]{:S(2)}) collective-permute-start(bf16[40,480]{1,0:T(8,128)(2,1)S(1)} %pad_maximum_fusion.b0), channel_id=1, source_target_pairs={{64,0},{72,8},{80,16},{88,24},{96,32},{104,40},{112,48},{120,56},{... | collective-permute-start | bytes 115208 | tf_op jit(solution)/shard_map/ppermute | solution.py:71
  17.4 0.5 collective-permute-start.8
  18.0 0.6 collective-permute-start.9
  18.6 0.0 collective-permute-done.7.b1
  18.6 3.8 %collective-permute-done.8.b2 = bf16[40,480]{1,0:T(8,128)(2,1)S(1)} collective-permute-done((bf16[40,480]{1,0:T(8,128)(2,1)S(1)}, bf16[40,480]{1,0:T(8,128)(2,1)S(1)}, u32[]{:S(2)}, u32[]{:S(2)}) %collective-permute-start.8) | collective-permute-done | bytes 38432 | tf_op jit(solution)/shard_map/ppermute | solution.py:71
  22.4 0.8 collective-permute-done.9.b3
  23.2 0.8 stack.17
  24.0 2.8 %collective-permute-start.10 = (bf16[160,480]{1,0:T(8,128)(2,1)S(1)}, bf16[160,480]{1,0:T(8,128)(2,1)S(1)}, u32[]{:S(2)}, u32[]{:S(2)}) collective-permute-start(bf16[160,480]{1,0:T(8,128)(2,1)S(1)} %get-tuple-element.27.refs_0_), channel_id=1, source_target_pairs={{8,0},{16,8},{24,16},{32,24},{40,32},{48,40},{56,48},{0,56},{72,64... | collective-permute-start | bytes 460808 | tf_op jit(solution)/shard_map/ppermute | solution.py:71
  26.8 0.0 collective-permute-start.11
  26.8 0.0 all-to-all-done.px
  26.9 0.0 copy-start.1
  26.9 1.8 %copy-done.1 = bf16[1176,1280]{1,0:T(8,128)(2,1)S(1)} copy-done((bf16[1176,1280]{1,0:T(8,128)(2,1)S(1)}, bf16[1176,1280]{1,0:T(8,128)(2,1)}, u32[]{:S(2)}) %copy-start.1) | copy-done | bytes 3010584
  28.7 1.6 %embed.1 = (bf16[128,1280]{1,0:T(8,128)(2,1)S(1)}, bf16[128,1280]{1,0:T(8,128)(2,1)}) custom-call(bf16[32,4,1176]{2,1,0:T(4,128)(2,1)S(1)} %all-to-all-done.px, bf16[1176,1280]{1,0:T(8,128)(2,1)S(1)} %copy-done.1, f32[1280]{0:T(1024)S(1)} %copy-done.2, f32[1280]{0:T(1024)S(1)} %copy-done.3), custom_call_target="tpu_custom_call" | custom-call | tf_op jit(solution)/shard_map/embed/pallas_call | solution.py:260
  30.3 1.9 %collective-permute-done.11.refs_7_ = bf16[160,480]{1,0:T(8,128)(2,1)S(1)} collective-permute-done((bf16[160,480]{1,0:T(8,128)(2,1)S(1)}, bf16[160,480]{1,0:T(8,128)(2,1)S(1)}, u32[]{:S(2)}, u32[]{:S(2)}) %collective-permute-start.11) | collective-permute-done | bytes 153632 | tf_op jit(solution)/shard_map/ppermute | solution.py:71
  32.2 3.8 %all-to-all-start.1 = ((bf16[8,40,640]{2,1,0:T(8,128)(2,1)}), bf16[8,40,640]{2,1,0:T(8,128)(2,1)S(1)}, u32[]{:S(2)}, u32[]{:S(2)}) async-start(bf16[8,40,640]{2,1,0:T(8,128)(2,1)} %get-tuple-element.26), calls=%async_computation.1 | async-start | bytes 819200 | tf_op jit(solution)/shard_map/all_to_all | solution.py:59
  36.1 2.7 %collective-permute-start.1 = (bf16[128,1280]{1,0:T(8,128)(2,1)}, bf16[128,1280]{1,0:T(8,128)(2,1)}, u32[]{:S(2)}, u32[]{:S(2)}) collective-permute-start(bf16[128,1280]{1,0:T(8,128)(2,1)} %get-tuple-element.22.refs_0_), channel_id=1, source_target_pairs={{2,0},{3,1},{4,2},{5,3},{6,4},{7,5},{0,6},{1,7},{10,8},{11,9},{12,... | collective-permute-start | bytes 983048 | tf_op jit(solution)/shard_map/ppermute | solution.py:63
  38.8 0.3 collective-permute-start.3
  39.1 0.7 collective-permute-start.5
  39.8 2.7 %collective-permute-start.12 = (bf16[160,480]{1,0:T(8,128)(2,1)S(1)}, bf16[160,480]{1,0:T(8,128)(2,1)S(1)}, u32[]{:S(2)}, u32[]{:S(2)}) collective-permute-start(bf16[160,480]{1,0:T(8,128)(2,1)S(1)} %collective-permute-done.10.refs_1_), channel_id=1, source_target_pairs={{8,0},{16,8},{24,16},{32,24},{40,32},{48,40},{56,48},{0,56},{72,64... | collective-permute-start | bytes 460808 | tf_op jit(solution)/shard_map/ppermute | solution.py:71
  42.5 0.0 collective-permute-start.15
  42.5 4.5 %collective-permute-done.12.refs_2_ = bf16[160,480]{1,0:T(8,128)(2,1)S(1)} collective-permute-done((bf16[160,480]{1,0:T(8,128)(2,1)S(1)}, bf16[160,480]{1,0:T(8,128)(2,1)S(1)}, u32[]{:S(2)}, u32[]{:S(2)}) %collective-permute-start.12) | collective-permute-done | bytes 153632 | tf_op jit(solution)/shard_map/ppermute | solution.py:71
  47.0 3.2 %collective-permute-start.13 = (bf16[160,480]{1,0:T(8,128)(2,1)S(1)}, bf16[160,480]{1,0:T(8,128)(2,1)S(1)}, u32[]{:S(2)}, u32[]{:S(2)}) collective-permute-start(bf16[160,480]{1,0:T(8,128)(2,1)S(1)} %collective-permute-done.12.refs_2_), channel_id=1, source_target_pairs={{8,0},{16,8},{24,16},{32,24},{40,32},{48,40},{56,48},{0,56},{72,64... | collective-permute-start | bytes 460808 | tf_op jit(solution)/shard_map/ppermute | solution.py:71
  50.2 0.5 collective-permute-done.15.refs_6_
  50.7 0.0 collective-permute-start.16
  50.8 0.1 concatenate.9.place
  50.8 2.3 %collective-permute-done.13.refs_3_ = bf16[160,480]{1,0:T(8,128)(2,1)S(1)} collective-permute-done((bf16[160,480]{1,0:T(8,128)(2,1)S(1)}, bf16[160,480]{1,0:T(8,128)(2,1)S(1)}, u32[]{:S(2)}, u32[]{:S(2)}) %collective-permute-start.13) | collective-permute-done | bytes 153632 | tf_op jit(solution)/shard_map/ppermute | solution.py:71
  53.1 5.1 %collective-permute-start = (bf16[128,1280]{1,0:T(8,128)(2,1)}, bf16[128,1280]{1,0:T(8,128)(2,1)}, u32[]{:S(2)}, u32[]{:S(2)}) collective-permute-start(bf16[128,1280]{1,0:T(8,128)(2,1)} %get-tuple-element.22.refs_0_), channel_id=1, source_target_pairs={{0,1},{1,0},{2,3},{3,2},{4,5},{5,4},{6,7},{7,6},{8,9},{9,8},{10,11... | collective-permute-start | bytes 983048 | tf_op jit(solution)/shard_map/ppermute | solution.py:67
  58.2 0.0 collective-permute-done.1.refs_2_
  58.2 0.0 collective-permute-start.2
  58.2 0.5 collective-permute-start.4
  58.7 0.0 collective-permute-done.5.refs_6_
  58.7 0.3 collective-permute-start.6
  59.0 0.8 fusion
  59.9 3.3 %collective-permute-start.14 = (bf16[160,480]{1,0:T(8,128)(2,1)S(1)}, bf16[160,480]{1,0:T(8,128)(2,1)S(1)}, u32[]{:S(2)}, u32[]{:S(2)}) collective-permute-start(bf16[160,480]{1,0:T(8,128)(2,1)S(1)} %collective-permute-done.13.refs_3_), channel_id=1, source_target_pairs={{8,0},{16,8},{24,16},{32,24},{40,32},{48,40},{56,48},{0,56},{72,64... | collective-permute-start | bytes 460808 | tf_op jit(solution)/shard_map/ppermute | solution.py:71
  63.2 0.1 fusion.1
  63.3 0.1 concatenate.11.refs_9_
  63.4 1.3 %broadcast_in_dim.11 = bf16[4,320,640]{2,1,0:T(8,128)(2,1)} broadcast(bf16[320,640]{1,0:T(8,128)(2,1)S(1)} %bitcast.12), dimensions={1,2} | broadcast | bytes 2048000 | tf_op jit(solution)/shard_map/broadcast_in_dim | solution.py:55
  64.7 3.7 %all-to-all-start.2 = ((bf16[4,320,640]{2,1,0:T(8,128)(2,1)}), bf16[4,320,640]{2,1,0:T(8,128)(2,1)S(1)}, u32[]{:S(2)}, u32[]{:S(2)}) async-start(bf16[4,320,640]{2,1,0:T(8,128)(2,1)} %broadcast_in_dim.11), calls=%async_computation.2 | async-start | bytes 3276800 | tf_op jit(solution)/shard_map/all_to_all | solution.py:59
  68.4 0.0 collective-permute-done.14.refs_4_
  68.4 2.3 %lay.1 = (bf16[32,40,768]{2,1,0:T(8,128)(2,1)S(1)}, f32[8,128,128]{2,1,0:T(8,128)S(1)}, f32[8,128,128]{2,1,0:T(8,128)S(1)}) custom-call(s32[16]{0:T(128)S(1)} %concatenate.9.place, f32[1,128]{1,0:T(1,128)S(1)} %copy-done.5, bf16[160,480]{1,0:T(8,128)(2,1)S(1)} %get-tuple-element.27.refs_0_, bf16[160,480]{1,0:T(8,128)(2,1)S(1)} %collective-permute-done.10.refs_1_, ...), custom_call_target="tpu_custom_call" | custom-call | tf_op jit(solution)/shard_map/lay/pallas_call | solution.py:280
  70.7 0.0 collective-permute-done.2.refs_3_
  70.7 0.0 collective-permute-done.4.refs_5_
  70.7 0.0 copy-start.4
  70.7 7.3 %attend.1 = (bf16[128,320]{1,0:T(8,128)(2,1)S(1)}, bf16[128,320]{1,0:T(8,128)(2,1)S(1)}, bf16[128,320]{1,0:T(8,128)(2,1)S(1)}, bf16[128,320]{1,0:T(8,128)(2,1)S(1)}) custom-call(s32[16]{0:T(128)S(1)} %concatenate.9.place, bf16[128,1280]{1,0:T(8,128)(2,1)} %get-tuple-element.22.refs_0_, bf16[128,1280]{1,0:T(8,128)(2,1)} %collective-permute-done.refs_1_, ...), custom_call_target="tpu_custom_call" | custom-call | flops 60000002048 | tf_op jit(solution)/shard_map/attend/pallas_call | solution.py:301
  78.1 1.9 %collective-permute-start.17 = (bf16[128,320]{1,0:T(8,128)(2,1)S(1)}, bf16[128,320]{1,0:T(8,128)(2,1)S(1)}, u32[]{:S(2)}, u32[]{:S(2)}) collective-permute-start(bf16[128,320]{1,0:T(8,128)(2,1)S(1)} %get-tuple-element.34), channel_id=1, source_target_pairs={{2,0},{3,1},{4,2},{5,3},{6,4},{7,5},{0,6},{1,7},{10,8},{11,9},{12,... | collective-permute-start | bytes 245768 | tf_op jit(solution)/shard_map/ppermute | solution.py:63
  80.0 0.3 collective-permute-start.19
  80.2 2.6 %collective-permute-done.17.refs_1_ = bf16[128,320]{1,0:T(8,128)(2,1)S(1)} collective-permute-done((bf16[128,320]{1,0:T(8,128)(2,1)S(1)}, bf16[128,320]{1,0:T(8,128)(2,1)S(1)}, u32[]{:S(2)}, u32[]{:S(2)}) %collective-permute-start.17) | collective-permute-done | bytes 81952 | tf_op jit(solution)/shard_map/ppermute | solution.py:63
  82.9 2.1 %collective-permute-done.19.refs_3_ = bf16[128,320]{1,0:T(8,128)(2,1)S(1)} collective-permute-done((bf16[128,320]{1,0:T(8,128)(2,1)S(1)}, bf16[128,320]{1,0:T(8,128)(2,1)S(1)}, u32[]{:S(2)}, u32[]{:S(2)}) %collective-permute-start.19) | collective-permute-done | bytes 81952 | tf_op jit(solution)/shard_map/ppermute | solution.py:63
  84.9 4.4 %all-to-all-done.2 = bf16[4,320,640]{2,1,0:T(8,128)(2,1)S(1)} async-done(((bf16[4,320,640]{2,1,0:T(8,128)(2,1)}), bf16[4,320,640]{2,1,0:T(8,128)(2,1)S(1)}, u32[]{:S(2)}, u32[]{:S(2)}) %all-to-all-start.2) | async-done | bytes 1638432 | tf_op jit(solution)/shard_map/all_to_all | solution.py:59
  89.4 1.4 %collective-permute-start.24 = (bf16[8,160,640]{2,1,0:T(8,128)(2,1)S(1)}, bf16[8,160,640]{2,1,0:T(8,128)(2,1)S(1)}, u32[]{:S(2)}, u32[]{:S(2)}) collective-permute-start(bf16[8,160,640]{2,1,0:T(8,128)(2,1)S(1)} %bitcast.9), channel_id=1, source_target_pairs={{0,1},{1,0},{2,3},{3,2},{4,5},{5,4},{6,7},{7,6},{8,9},{9,8},{10,11... | collective-permute-start | bytes 4915208 | tf_op jit(solution)/shard_map/ppermute | solution.py:67
  90.7 1.5 %collective-permute-start.18 = (bf16[128,320]{1,0:T(8,128)(2,1)S(1)}, bf16[128,320]{1,0:T(8,128)(2,1)S(1)}, u32[]{:S(2)}, u32[]{:S(2)}) collective-permute-start(bf16[128,320]{1,0:T(8,128)(2,1)S(1)} %get-tuple-element.35), channel_id=1, source_target_pairs={{4,0},{5,1},{6,2},{7,3},{0,4},{1,5},{2,6},{3,7},{12,8},{13,9},{14,... | collective-permute-start | bytes 245768 | tf_op jit(solution)/shard_map/ppermute | solution.py:63
  92.2 0.3 collective-permute-start.20
  92.5 0.2 collective-permute-start.21
  92.7 4.0 %collective-permute-done.18.refs_2_ = bf16[128,320]{1,0:T(8,128)(2,1)S(1)} collective-permute-done((bf16[128,320]{1,0:T(8,128)(2,1)S(1)}, bf16[128,320]{1,0:T(8,128)(2,1)S(1)}, u32[]{:S(2)}, u32[]{:S(2)}) %collective-permute-start.18) | collective-permute-done | bytes 81952 | tf_op jit(solution)/shard_map/ppermute | solution.py:63
  96.7 0.8 collective-permute-start.22
  97.5 0.0 collective-permute-start.23
  97.5 0.9 collective-permute-done.22.refs_6_
  98.4 0.4 collective-permute-done.23.refs_7_
  98.8 2.4 %project.1 = bf16[128,1280]{1,0:T(8,128)(2,1)} custom-call(s32[16]{0:T(128)S(1)} %concatenate.9.place, bf16[128,320]{1,0:T(8,128)(2,1)S(1)} %get-tuple-element.33.refs_0_, bf16[128,320]{1,0:T(8,128)(2,1)S(1)} %collective-permute-done.17.refs_1_, bf16[128,320]{1,0:T(8,128)(2,1)S(1)} %collective-permute-done.18.refs_2_, ...), custom_call_target="tpu_custom_call" | custom-call | tf_op jit(solution)/shard_map/project/pallas_call | solution.py:321
  (26 shorter events, 0.1 us)
Async XLA Ops:
  0.0 18.5 %copy-start = (bf16[40,1280]{1,0:T(8,128)(2,1)S(1)}, bf16[40,1280]{1,0:T(8,128)(2,1)}, u32[]{:S(2)}) copy-start(bf16[40,1280]{1,0:T(8,128)(2,1)} %param.17) | copy-start | bytes 307204
  0.0 26.8 %copy-start.2 = (f32[1280]{0:T(1024)S(1)}, f32[1280]{0:T(1024)}, u32[]{:S(2)}) copy-start(f32[1280]{0:T(1024)} %gain.1) | copy-start | bytes 15364
  0.0 26.8 %copy-start.3 = (f32[1280]{0:T(1024)S(1)}, f32[1280]{0:T(1024)}, u32[]{:S(2)}) copy-start(f32[1280]{0:T(1024)} %bias.1) | copy-start | bytes 15364
  2.0 24.9 %all-to-all-start = ((bf16[32,4,1176]{2,1,0:T(4,128)(2,1)}), bf16[32,4,1176]{2,1,0:T(4,128)(2,1)S(1)}, u32[]{:S(2)}, u32[]{:S(2)}) async-start(bf16[32,4,1176]{2,1,0:T(4,128)(2,1)} %reshape.10), calls=%async_computation | async-start | bytes 655360 | tf_op jit(solution)/shard_map/all_to_all | solution.py:240
  14.9 3.7 %collective-permute-start.7 = (bf16[40,480]{1,0:T(8,128)(2,1)S(1)}, bf16[40,480]{1,0:T(8,128)(2,1)S(1)}, u32[]{:S(2)}, u32[]{:S(2)}) collective-permute-start(bf16[40,480]{1,0:T(8,128)(2,1)S(1)} %pad_maximum_fusion.b0), channel_id=1, source_target_pairs={{64,0},{72,8},{80,16},{88,24},{96,32},{104,40},{112,48},{120,56},{... | collective-permute-start | bytes 115208 | tf_op jit(solution)/shard_map/ppermute | solution.py:71
  17.4 5.0 %collective-permute-start.8 = (bf16[40,480]{1,0:T(8,128)(2,1)S(1)}, bf16[40,480]{1,0:T(8,128)(2,1)S(1)}, u32[]{:S(2)}, u32[]{:S(2)}) collective-permute-start(bf16[40,480]{1,0:T(8,128)(2,1)S(1)} %pad_maximum_fusion.b0), channel_id=1, source_target_pairs={{128,0},{136,8},{144,16},{152,24},{160,32},{168,40},{176,48},{184,... | collective-permute-start | bytes 115208 | tf_op jit(solution)/shard_map/ppermute | solution.py:71
  18.0 5.2 %collective-permute-start.9 = (bf16[40,480]{1,0:T(8,128)(2,1)S(1)}, bf16[40,480]{1,0:T(8,128)(2,1)S(1)}, u32[]{:S(2)}, u32[]{:S(2)}) collective-permute-start(bf16[40,480]{1,0:T(8,128)(2,1)S(1)} %pad_maximum_fusion.b0), channel_id=1, source_target_pairs={{192,0},{200,8},{208,16},{216,24},{224,32},{232,40},{240,48},{248,... | collective-permute-start | bytes 115208 | tf_op jit(solution)/shard_map/ppermute | solution.py:71
  24.0 26.7 %copy-start.6 = (s32[1,3]{1,0:T(1,128)S(1)}, s32[1,3]{1,0:T(1,128)}, u32[]{:S(2)}) copy-start(s32[1,3]{1,0:T(1,128)} %param.19) | copy-start | bytes 40
  24.0 26.8 %copy-start.7 = (s32[1,3]{1,0:T(1,128)S(1)}, s32[1,3]{1,0:T(1,128)}, u32[]{:S(2)}) copy-start(s32[1,3]{1,0:T(1,128)} %param.20) | copy-start | bytes 40
  24.0 6.3 %collective-permute-start.10 = (bf16[160,480]{1,0:T(8,128)(2,1)S(1)}, bf16[160,480]{1,0:T(8,128)(2,1)S(1)}, u32[]{:S(2)}, u32[]{:S(2)}) collective-permute-start(bf16[160,480]{1,0:T(8,128)(2,1)S(1)} %get-tuple-element.27.refs_0_), channel_id=1, source_target_pairs={{8,0},{16,8},{24,16},{32,24},{40,32},{48,40},{56,48},{0,56},{72,64... | collective-permute-start | bytes 460808 | tf_op jit(solution)/shard_map/ppermute | solution.py:71
  26.8 5.4 %collective-permute-start.11 = (bf16[160,480]{1,0:T(8,128)(2,1)S(1)}, bf16[160,480]{1,0:T(8,128)(2,1)S(1)}, u32[]{:S(2)}, u32[]{:S(2)}) collective-permute-start(bf16[160,480]{1,0:T(8,128)(2,1)S(1)} %get-tuple-element.27.refs_0_), channel_id=1, source_target_pairs={{56,0},{0,8},{8,16},{16,24},{24,32},{32,40},{40,48},{48,56},{120,6... | collective-permute-start | bytes 460808 | tf_op jit(solution)/shard_map/ppermute | solution.py:71
  26.9 1.9 %copy-start.1 = (bf16[1176,1280]{1,0:T(8,128)(2,1)S(1)}, bf16[1176,1280]{1,0:T(8,128)(2,1)}, u32[]{:S(2)}) copy-start(bf16[1176,1280]{1,0:T(8,128)(2,1)} %pw.1) | copy-start | bytes 9031684
  32.2 31.1 %all-to-all-start.1 = ((bf16[8,40,640]{2,1,0:T(8,128)(2,1)}), bf16[8,40,640]{2,1,0:T(8,128)(2,1)S(1)}, u32[]{:S(2)}, u32[]{:S(2)}) async-start(bf16[8,40,640]{2,1,0:T(8,128)(2,1)} %get-tuple-element.26), calls=%async_computation.1 | async-start | bytes 819200 | tf_op jit(solution)/shard_map/all_to_all | solution.py:59
  36.1 22.2 %collective-permute-start.1 = (bf16[128,1280]{1,0:T(8,128)(2,1)}, bf16[128,1280]{1,0:T(8,128)(2,1)}, u32[]{:S(2)}, u32[]{:S(2)}) collective-permute-start(bf16[128,1280]{1,0:T(8,128)(2,1)} %get-tuple-element.22.refs_0_), channel_id=1, source_target_pairs={{2,0},{3,1},{4,2},{5,3},{6,4},{7,5},{0,6},{1,7},{10,8},{11,9},{12,... | collective-permute-start | bytes 983048 | tf_op jit(solution)/shard_map/ppermute | solution.py:63
  38.8 19.4 %collective-permute-start.3 = (bf16[128,1280]{1,0:T(8,128)(2,1)}, bf16[128,1280]{1,0:T(8,128)(2,1)}, u32[]{:S(2)}, u32[]{:S(2)}) collective-permute-start(bf16[128,1280]{1,0:T(8,128)(2,1)} %get-tuple-element.22.refs_0_), channel_id=1, source_target_pairs={{4,0},{5,1},{6,2},{7,3},{0,4},{1,5},{2,6},{3,7},{12,8},{13,9},{14,... | collective-permute-start | bytes 983048 | tf_op jit(solution)/shard_map/ppermute | solution.py:63
  39.1 19.6 %collective-permute-start.5 = (bf16[128,1280]{1,0:T(8,128)(2,1)}, bf16[128,1280]{1,0:T(8,128)(2,1)}, u32[]{:S(2)}, u32[]{:S(2)}) collective-permute-start(bf16[128,1280]{1,0:T(8,128)(2,1)} %get-tuple-element.22.refs_0_), channel_id=1, source_target_pairs={{6,0},{7,1},{0,2},{1,3},{2,4},{3,5},{4,6},{5,7},{14,8},{15,9},{8,1... | collective-permute-start | bytes 983048 | tf_op jit(solution)/shard_map/ppermute | solution.py:63
  39.8 7.2 %collective-permute-start.12 = (bf16[160,480]{1,0:T(8,128)(2,1)S(1)}, bf16[160,480]{1,0:T(8,128)(2,1)S(1)}, u32[]{:S(2)}, u32[]{:S(2)}) collective-permute-start(bf16[160,480]{1,0:T(8,128)(2,1)S(1)} %collective-permute-done.10.refs_1_), channel_id=1, source_target_pairs={{8,0},{16,8},{24,16},{32,24},{40,32},{48,40},{56,48},{0,56},{72,64... | collective-permute-start | bytes 460808 | tf_op jit(solution)/shard_map/ppermute | solution.py:71
  42.5 8.2 %collective-permute-start.15 = (bf16[160,480]{1,0:T(8,128)(2,1)S(1)}, bf16[160,480]{1,0:T(8,128)(2,1)S(1)}, u32[]{:S(2)}, u32[]{:S(2)}) collective-permute-start(bf16[160,480]{1,0:T(8,128)(2,1)S(1)} %collective-permute-done.11.refs_7_), channel_id=1, source_target_pairs={{56,0},{0,8},{8,16},{16,24},{24,32},{32,40},{40,48},{48,56},{120,6... | collective-permute-start | bytes 460808 | tf_op jit(solution)/shard_map/ppermute | solution.py:71
  47.0 6.1 %collective-permute-start.13 = (bf16[160,480]{1,0:T(8,128)(2,1)S(1)}, bf16[160,480]{1,0:T(8,128)(2,1)S(1)}, u32[]{:S(2)}, u32[]{:S(2)}) collective-permute-start(bf16[160,480]{1,0:T(8,128)(2,1)S(1)} %collective-permute-done.12.refs_2_), channel_id=1, source_target_pairs={{8,0},{16,8},{24,16},{32,24},{40,32},{48,40},{56,48},{0,56},{72,64... | collective-permute-start | bytes 460808 | tf_op jit(solution)/shard_map/ppermute | solution.py:71
  50.7 9.1 %collective-permute-start.16 = (bf16[160,480]{1,0:T(8,128)(2,1)S(1)}, bf16[160,480]{1,0:T(8,128)(2,1)S(1)}, u32[]{:S(2)}, u32[]{:S(2)}) collective-permute-start(bf16[160,480]{1,0:T(8,128)(2,1)S(1)} %collective-permute-done.15.refs_6_), channel_id=1, source_target_pairs={{56,0},{0,8},{8,16},{16,24},{24,32},{32,40},{40,48},{48,56},{120,6... | collective-permute-start | bytes 460808 | tf_op jit(solution)/shard_map/ppermute | solution.py:71
  53.1 17.6 %collective-permute-start = (bf16[128,1280]{1,0:T(8,128)(2,1)}, bf16[128,1280]{1,0:T(8,128)(2,1)}, u32[]{:S(2)}, u32[]{:S(2)}) collective-permute-start(bf16[128,1280]{1,0:T(8,128)(2,1)} %get-tuple-element.22.refs_0_), channel_id=1, source_target_pairs={{0,1},{1,0},{2,3},{3,2},{4,5},{5,4},{6,7},{7,6},{8,9},{9,8},{10,11... | collective-permute-start | bytes 983048 | tf_op jit(solution)/shard_map/ppermute | solution.py:67
  58.2 12.5 %collective-permute-start.2 = (bf16[128,1280]{1,0:T(8,128)(2,1)}, bf16[128,1280]{1,0:T(8,128)(2,1)}, u32[]{:S(2)}, u32[]{:S(2)}) collective-permute-start(bf16[128,1280]{1,0:T(8,128)(2,1)} %collective-permute-done.1.refs_2_), channel_id=1, source_target_pairs={{0,1},{1,0},{2,3},{3,2},{4,5},{5,4},{6,7},{7,6},{8,9},{9,8},{10,11... | collective-permute-start | bytes 983048 | tf_op jit(solution)/shard_map/ppermute | solution.py:67
  58.2 12.5 %collective-permute-start.4 = (bf16[128,1280]{1,0:T(8,128)(2,1)}, bf16[128,1280]{1,0:T(8,128)(2,1)}, u32[]{:S(2)}, u32[]{:S(2)}) collective-permute-start(bf16[128,1280]{1,0:T(8,128)(2,1)} %collective-permute-done.3.refs_4_), channel_id=1, source_target_pairs={{0,1},{1,0},{2,3},{3,2},{4,5},{5,4},{6,7},{7,6},{8,9},{9,8},{10,11... | collective-permute-start | bytes 983048 | tf_op jit(solution)/shard_map/ppermute | solution.py:67
  58.7 12.0 %collective-permute-start.6 = (bf16[128,1280]{1,0:T(8,128)(2,1)}, bf16[128,1280]{1,0:T(8,128)(2,1)}, u32[]{:S(2)}, u32[]{:S(2)}) collective-permute-start(bf16[128,1280]{1,0:T(8,128)(2,1)} %collective-permute-done.5.refs_6_), channel_id=1, source_target_pairs={{0,1},{1,0},{2,3},{3,2},{4,5},{5,4},{6,7},{7,6},{8,9},{9,8},{10,11... | collective-permute-start | bytes 983048 | tf_op jit(solution)/shard_map/ppermute | solution.py:67
  59.9 8.6 %collective-permute-start.14 = (bf16[160,480]{1,0:T(8,128)(2,1)S(1)}, bf16[160,480]{1,0:T(8,128)(2,1)S(1)}, u32[]{:S(2)}, u32[]{:S(2)}) collective-permute-start(bf16[160,480]{1,0:T(8,128)(2,1)S(1)} %collective-permute-done.13.refs_3_), channel_id=1, source_target_pairs={{8,0},{16,8},{24,16},{32,24},{40,32},{48,40},{56,48},{0,56},{72,64... | collective-permute-start | bytes 460808 | tf_op jit(solution)/shard_map/ppermute | solution.py:71
  64.7 3.7 %copy-start.5 = (f32[1,128]{1,0:T(1,128)S(1)}, f32[1,128]{1,0:T(1,128)}, u32[]{:S(2)}) copy-start(f32[1,128]{1,0:T(1,128)} %constant.75.clone.inverse) | copy-start | bytes 1540
  64.7 24.7 %all-to-all-start.2 = ((bf16[4,320,640]{2,1,0:T(8,128)(2,1)}), bf16[4,320,640]{2,1,0:T(8,128)(2,1)S(1)}, u32[]{:S(2)}, u32[]{:S(2)}) async-start(bf16[4,320,640]{2,1,0:T(8,128)(2,1)} %broadcast_in_dim.11), calls=%async_computation.2 | async-start | bytes 3276800 | tf_op jit(solution)/shard_map/all_to_all | solution.py:59
  70.7 28.0 %copy-start.4 = (f32[1280]{0:T(1024)S(1)}, f32[1280]{0:T(1024)}, u32[]{:S(2)}) copy-start(f32[1280]{0:T(1024)} %refs_11_.1) | copy-start | bytes 15364
  78.1 4.8 %collective-permute-start.17 = (bf16[128,320]{1,0:T(8,128)(2,1)S(1)}, bf16[128,320]{1,0:T(8,128)(2,1)S(1)}, u32[]{:S(2)}, u32[]{:S(2)}) collective-permute-start(bf16[128,320]{1,0:T(8,128)(2,1)S(1)} %get-tuple-element.34), channel_id=1, source_target_pairs={{2,0},{3,1},{4,2},{5,3},{6,4},{7,5},{0,6},{1,7},{10,8},{11,9},{12,... | collective-permute-start | bytes 245768 | tf_op jit(solution)/shard_map/ppermute | solution.py:63
  80.0 5.0 %collective-permute-start.19 = (bf16[128,320]{1,0:T(8,128)(2,1)S(1)}, bf16[128,320]{1,0:T(8,128)(2,1)S(1)}, u32[]{:S(2)}, u32[]{:S(2)}) collective-permute-start(bf16[128,320]{1,0:T(8,128)(2,1)S(1)} %get-tuple-element.36), channel_id=1, source_target_pairs={{6,0},{7,1},{0,2},{1,3},{2,4},{3,5},{4,6},{5,7},{14,8},{15,9},{8,1... | collective-permute-start | bytes 245768 | tf_op jit(solution)/shard_map/ppermute | solution.py:63
  89.4 9.4 %collective-permute-start.24 = (bf16[8,160,640]{2,1,0:T(8,128)(2,1)S(1)}, bf16[8,160,640]{2,1,0:T(8,128)(2,1)S(1)}, u32[]{:S(2)}, u32[]{:S(2)}) collective-permute-start(bf16[8,160,640]{2,1,0:T(8,128)(2,1)S(1)} %bitcast.9), channel_id=1, source_target_pairs={{0,1},{1,0},{2,3},{3,2},{4,5},{5,4},{6,7},{7,6},{8,9},{9,8},{10,11... | collective-permute-start | bytes 4915208 | tf_op jit(solution)/shard_map/ppermute | solution.py:67
  90.7 5.9 %collective-permute-start.18 = (bf16[128,320]{1,0:T(8,128)(2,1)S(1)}, bf16[128,320]{1,0:T(8,128)(2,1)S(1)}, u32[]{:S(2)}, u32[]{:S(2)}) collective-permute-start(bf16[128,320]{1,0:T(8,128)(2,1)S(1)} %get-tuple-element.35), channel_id=1, source_target_pairs={{4,0},{5,1},{6,2},{7,3},{0,4},{1,5},{2,6},{3,7},{12,8},{13,9},{14,... | collective-permute-start | bytes 245768 | tf_op jit(solution)/shard_map/ppermute | solution.py:63
  92.2 5.3 %collective-permute-start.20 = (bf16[128,320]{1,0:T(8,128)(2,1)S(1)}, bf16[128,320]{1,0:T(8,128)(2,1)S(1)}, u32[]{:S(2)}, u32[]{:S(2)}) collective-permute-start(bf16[128,320]{1,0:T(8,128)(2,1)S(1)} %get-tuple-element.33.refs_0_), channel_id=1, source_target_pairs={{0,1},{1,0},{2,3},{3,2},{4,5},{5,4},{6,7},{7,6},{8,9},{9,8},{10,11... | collective-permute-start | bytes 245768 | tf_op jit(solution)/shard_map/ppermute | solution.py:67
  92.5 5.0 %collective-permute-start.21 = (bf16[128,320]{1,0:T(8,128)(2,1)S(1)}, bf16[128,320]{1,0:T(8,128)(2,1)S(1)}, u32[]{:S(2)}, u32[]{:S(2)}) collective-permute-start(bf16[128,320]{1,0:T(8,128)(2,1)S(1)} %collective-permute-done.17.refs_1_), channel_id=1, source_target_pairs={{0,1},{1,0},{2,3},{3,2},{4,5},{5,4},{6,7},{7,6},{8,9},{9,8},{10,11... | collective-permute-start | bytes 245768 | tf_op jit(solution)/shard_map/ppermute | solution.py:67
  96.7 1.7 %collective-permute-start.22 = (bf16[128,320]{1,0:T(8,128)(2,1)S(1)}, bf16[128,320]{1,0:T(8,128)(2,1)S(1)}, u32[]{:S(2)}, u32[]{:S(2)}) collective-permute-start(bf16[128,320]{1,0:T(8,128)(2,1)S(1)} %collective-permute-done.18.refs_2_), channel_id=1, source_target_pairs={{0,1},{1,0},{2,3},{3,2},{4,5},{5,4},{6,7},{7,6},{8,9},{9,8},{10,11... | collective-permute-start | bytes 245768 | tf_op jit(solution)/shard_map/ppermute | solution.py:67
  97.5 1.3 %collective-permute-start.23 = (bf16[128,320]{1,0:T(8,128)(2,1)S(1)}, bf16[128,320]{1,0:T(8,128)(2,1)S(1)}, u32[]{:S(2)}, u32[]{:S(2)}) collective-permute-start(bf16[128,320]{1,0:T(8,128)(2,1)S(1)} %collective-permute-done.19.refs_3_), channel_id=1, source_target_pairs={{0,1},{1,0},{2,3},{3,2},{4,5},{5,4},{6,7},{7,6},{8,9},{9,8},{10,11... | collective-permute-start | bytes 245768 | tf_op jit(solution)/shard_map/ppermute | solution.py:67
